TPU v7x, 128 devices: a whole 4x4x4 slice. The times are simulated.
128 devices in a mesh: head: 8 (over z_hi, x), ctx: 16 (over z_lo, y, core).
Axes of the slice: x: 4, y: 4, z: 4 (z_hi: 2, z_lo: 2; z = z_hi * 2 + z_lo), core: 2. Of those that a mesh axis runs over, the one named last changes fastest.
Arguments:
- mla_queries: bfloat16 [128, 128, 576], P('head'), may hold values from -4 to 4
- latent_cache: bfloat16 [65536, 576], P('ctx'), may hold values from -4 to 4
- normalizers: float32 [128, 128], P('head'), may hold values from 9 to 15
- query_positions: int32 [128], replicated, may hold values from 0 to 131071, as said below
- key_positions: int32 [65536], P('ctx'), may hold values from 0 to 131071, as said below
- index_queries: bfloat16 [64, 128, 128], P('head'), may hold values from -24 to 24
- index_keys: bfloat16 [65536, 128], P(('ctx', 'head')), may hold values from -24 to 24
- index_weights: bfloat16 [64, 128], P('head'), may hold values from -16 to 16
Outputs:
- grad_queries: float32 [64, 128, 128], P('head')
- grad_weights: float32 [64, 128], P('head')
- grad_keys: float32 [65536, 128], P(('ctx', 'head'))
Inputs may be any that keep to these rules, and one draw needn't show every extreme that they name: `query_positions`: every query position is one the keys' positions could reach. `key_positions`: key positions rise strictly along the keys.
All inputs are finite; a program needn't handle non-finite values.
Results may differ from a plain program's by a relative error of at most 0.00115.
The roundings to bfloat16 on the way count: a program that leaves them out, or rounds other values in their place, can miss the bound.
Values may be sent and summed in bfloat16 or wider, within the bound.
No kernel may reach another device: no remote copies, remote signals or barrier semaphores. Data moves between devices by JAX's collectives and lax.ppermute only.
A program may use at most 128 MiB of HBM per device.

v0:
```python
import math

import jax
import jax.numpy as jnp
from jax import lax
from jax.sharding import PartitionSpec as P

att_scale = 192.0 ** (-0.5)
loss_scale = 1024.0
masked_floor = -1e30


def per_device(
    mla_queries,
    latent_cache,
    normalizers,
    query_positions,
    key_positions,
    index_queries,
    index_keys,
    index_weights,
):
    head_count = mla_queries.shape[0]
    query_count = mla_queries.shape[1]
    query_flat = mla_queries.reshape(head_count * query_count, mla_queries.shape[2])
    sub_keys = index_keys.shape[0]
    block_rows = math.gcd(sub_keys * lax.axis_size("head"), 512)

    def one_block(block_index):
        first_row = block_index * block_rows
        cache_rows = lax.dynamic_slice_in_dim(latent_cache, first_row, block_rows, 0)
        positions = lax.dynamic_slice_in_dim(key_positions, first_row, block_rows, 0)
        scores = jnp.dot(cache_rows, query_flat.T, preferred_element_type=jnp.float32)
        scores = scores.reshape(block_rows, head_count, query_count)
        weights = jnp.exp(scores * att_scale - normalizers[None])
        visible = positions[:, None] <= query_positions[None, :]
        return jnp.where(visible, jnp.sum(weights, axis=1), 0.0)

    pieces = lax.map(
        one_block, jnp.arange(sub_keys * lax.axis_size("head") // block_rows, dtype=jnp.int32)
    )
    summed_probs = lax.psum_scatter(
        pieces.reshape(sub_keys * lax.axis_size("head"), query_count),
        "head",
        scatter_dimension=0,
        tiled=True,
    )
    all_queries, all_weights = (
        lax.all_gather(index_queries, "head", axis=0, tiled=True),
        lax.all_gather(index_weights, "head", axis=0, tiled=True),
    )
    index_heads = all_queries.shape[0]
    index_width = all_queries.shape[2]
    offset = lax.axis_index("head") * sub_keys
    own_positions = lax.dynamic_slice_in_dim(key_positions, offset, sub_keys, 0)
    visible = own_positions[:, None] <= query_positions[None, :]
    pair_flat = all_queries.reshape(index_heads * query_count, index_width)
    relu_input = jnp.dot(index_keys, pair_flat.T, preferred_element_type=jnp.float32)
    relu_input = relu_input.reshape(sub_keys, index_heads, query_count)
    index_scale = (index_heads * index_width) ** (-0.5)
    activated = jnp.maximum(relu_input, 0.0)
    weights_float = all_weights.astype(jnp.float32)
    logits = index_scale * jnp.sum(activated * weights_float[None], axis=1)
    hidden_logits = jnp.where(visible, logits, masked_floor)
    local_max = jnp.max(hidden_logits, axis=0)
    local_target = jnp.sum(summed_probs, axis=0)
    row_max = lax.pmax(local_max, ("head", "ctx"))
    local_exp = jnp.sum(jnp.where(visible, jnp.exp(hidden_logits - row_max[None]), 0.0), axis=0)
    row_total, target_total = lax.psum((local_exp, local_target), ("head", "ctx"))
    softmax_probs = (
        jnp.where(visible, jnp.exp(hidden_logits - row_max[None]), 0.0) / row_total[None]
    )
    target = summed_probs / target_total[None]
    logit_grad = loss_scale * jnp.where(visible, softmax_probs - target, 0.0)
    gradient_gate = jnp.where(relu_input > 0.0, index_scale * weights_float[None], 0.0)
    pre_grad = (gradient_gate * logit_grad[:, None, :]).astype(jnp.bfloat16)
    pre_flat = pre_grad.reshape(sub_keys, index_heads * query_count)
    grad_weights_part = index_scale * jnp.sum(activated * logit_grad[:, None, :], axis=0)
    grad_queries_part = jnp.dot(pre_flat.T, index_keys, preferred_element_type=jnp.float32)
    grad_queries_part = grad_queries_part.reshape(index_heads, query_count, index_width)
    grad_keys = jnp.dot(pre_flat, pair_flat, preferred_element_type=jnp.float32)
    total_queries, total_weights = lax.psum((grad_queries_part, grad_weights_part), ("head", "ctx"))
    local_heads = index_heads // lax.axis_size("head")
    first_head = lax.axis_index("head") * local_heads
    grad_queries = lax.dynamic_slice_in_dim(total_queries, first_head, local_heads, 0)
    grad_weights = lax.dynamic_slice_in_dim(total_weights, first_head, local_heads, 0)
    return (grad_queries, grad_weights, grad_keys)


def solution(mesh):
    placed = (
        P("head", None, None),
        P("ctx", None),
        P("head", None),
        P(),
        P("ctx"),
        P("head", None, None),
        P(("ctx", "head"), None),
        P("head", None),
    )
    return jax.shard_map(
        per_device,
        mesh=mesh,
        in_specs=placed,
        out_specs=(P("head", None, None), P("head", None), P(("ctx", "head"), None)),
        check_vma=False,
    )
```

profile of v0, /device:TPU:1, one launch (start us, length us, event | category | flops | bytes accessed | tf_op | source)
XLA Modules:
  0.0 419.4 jit_solution(14949574977055420805)
XLA Ops:
  8.0 3.1 copy.14
  11.1 65.1 %while.10 = (s32[]{:T(128)}, f32[8,512,128]{2,1,0:T(8,128)}, s32[8]{0:T(128)S(1)}, s32[4096]{0:T(1024)}, s32[128]{0:T(128)S(1)}, /*index=5*/bf16[4096,576]{0,1:T...) while((s32[]{:T(128)}, f32[8,512,128]{2,1,0:T(8,128)}, ...), condition=%wide.region_7.8_spmd, body=%wide.region_5.7_spmd.sunk | while | flops 1211170816 | bytes 20527812 | solution.py:39
  13.1 2.9 multiply_bitcast_fusion.2
  16.1 0.9 copy.20
  17.0 1.4 fusion.24
  18.4 0.9 fusion.25
  21.3 2.9 multiply_bitcast_fusion.2
  24.2 0.9 copy.20
  25.1 1.4 fusion.24
  26.6 0.8 fusion.25
  29.4 2.9 multiply_bitcast_fusion.2
  32.3 0.9 copy.20
  33.3 1.4 fusion.24
  34.7 0.9 fusion.25
  37.5 2.9 multiply_bitcast_fusion.2
  40.5 0.9 copy.20
  41.4 1.4 fusion.24
  42.8 0.9 fusion.25
  44.9 0.8 dynamic_slice.31
  45.7 2.9 multiply_bitcast_fusion.2
  48.6 0.9 copy.20
  49.6 1.4 fusion.24
  51.0 0.9 fusion.25
  53.8 2.9 multiply_bitcast_fusion.2
  56.8 0.9 copy.20
  57.7 1.4 fusion.24
  59.1 0.8 fusion.25
  62.0 2.9 multiply_bitcast_fusion.2
  64.9 0.9 copy.20
  65.8 1.4 fusion.24
  67.2 0.8 fusion.25
  70.1 2.9 multiply_bitcast_fusion.2
  73.0 0.9 copy.20
  74.0 1.4 fusion.24
  75.4 0.8 fusion.25
  76.2 2.9 copy.15
  80.0 28.0 %all_gather.7 = bf16[64,128]{1,0:T(8,128)(2,1)S(1)} all-gather(bf16[8,128]{1,0:T(8,128)(2,1)S(1)} %copy-done.4), channel_id=1, replica_groups=mesh['head'=8,'ctx'=16] {'head'}, dimensions={0}, use_global_device_ids=true | all-gather | bytes 18432 | tf_op jit(solution)/shard_map/all_gather | solution.py:50
  108.0 8.4 %multiply_reduce_fusion.1 = (f32[512,128]{0,1:T(8,128)S(1)}, f32[512,64,128]{0,2,1:T(8,128)}) fusion(f32[64,128]{1,0:T(8,128)S(1)} %convert_element_type.6, bf16[64,128,128]{2,1,0:T(8,128)(2,1)} %all-gather.2.cloned.1.call-done, bf16[512,128]{1,0:T(8,128)(2,1)S(1)} %copy-done), kind=kOutput, calls=%fused_computation.10 | convolution fusion | flops 1086259200 | bytes 19300352 | tf_op jit(solution)/shard_map/dot_general | solution.py:58
  116.6 69.2 %pmax.7 = f32[128]{0:T(128)S(1)} all-reduce(f32[128]{0:T(128)S(1)} %fusion.8), channel_id=1, replica_groups=mesh['head'=8,'ctx'=16] {'head','ctx'}, use_global_device_ids=true, to_apply=%region_2.3 | all-reduce | flops 128 | bytes 1024 | tf_op jit(solution)/shard_map/pmax | solution.py:67
  186.0 1.1 reduce_sum.49
  187.1 63.2 %all-reduce = (f32[128]{0:T(128)S(1)}, f32[128]{0:T(128)S(1)}) all-reduce(f32[128]{0:T(128)S(1)} %reduce_sum.49, f32[128]{0:T(128)S(1)} %fusion.9), channel_id=1, replica_groups=mesh['head'=8,'ctx'=16] {'head','ctx'}, use_global_device_ids=true, to_apply=%region_10.11 | all-reduce | flops 256 | bytes 2048 | tf_op jit(solution)/shard_map/psum | solution.py:69
  250.2 1.1 fusion.7
  251.4 8.6 %fusion.5 = f32[64,128,128]{2,1,0:T(8,128)} fusion(f32[512,64,128]{0,2,1:T(8,128)} %get-tuple-element.65, f32[512,128]{0,1:T(8,128)S(1)} %fusion.7, f32[64,128]{1,0:T(8,128)S(1)} %broadcast_multiply_fusion.1, bf16[512,128]{1,0:T(8,128)(2,1)S(1)} %copy-done), kind=kOutput, calls=%fused_computation.11 | convolution fusion | flops 1090519040 | bytes 21397504 | tf_op jit(solution)/shard_map/dot_general | solution.py:79
  260.0 8.0 %multiply_reduce_fusion = f32[64,128]{1,0:T(8,128)S(1)} fusion(f32[512,64,128]{0,2,1:T(8,128)} %get-tuple-element.65, f32[512,128]{0,1:T(8,128)S(1)} %fusion.7), kind=kLoop, calls=%fused_computation.8 | loop fusion | flops 12574720 | bytes 17072128 | tf_op jit(solution)/shard_map/reduce_sum | solution.py:78
  268.0 64.3 %psum.31 = f32[64,128]{1,0:T(8,128)S(1)} all-reduce(f32[64,128]{1,0:T(8,128)S(1)} %broadcast_multiply_fusion), channel_id=1, replica_groups=mesh['head'=8,'ctx'=16] {'head','ctx'}, use_global_device_ids=true, to_apply=%region_13.14 | all-reduce | flops 8192 | bytes 65536 | tf_op jit(solution)/shard_map/psum | solution.py:82
  332.9 9.0 %convolution_bitcast_fusion = f32[512,128]{1,0:T(8,128)} fusion(bf16[64,128,128]{2,1,0:T(8,128)(2,1)S(1)} %copy-done.1, f32[512,64,128]{0,2,1:T(8,128)} %get-tuple-element.65, f32[512,128]{0,1:T(8,128)S(1)} %fusion.7, f32[64,128]{1,0:T(8,128)S(1)} %broadcast_multiply_fusion.1), kind=kOutput, calls=%fused_computation.13 | convolution fusion | flops 1090519040 | bytes 19431424 | tf_op jit(solution)/shard_map/dot_general | solution.py:81
  341.9 69.1 %all-reduce.3.cloned.1.call-done = f32[64,128,128]{2,1,0:T(8,128)} async-done(((f32[64,128,128]{2,1,0:T(8,128)}), f32[64,128,128]{2,1,0:T(8,128)}) %all-reduce.3.cloned.1.call-update) | async-done | bytes 4194320 | tf_op jit(solution)/shard_map/psum | solution.py:82
  411.0 1.9 constant_dynamic-slice_fusion.1
  (42 shorter events, 12.7 us)
Async XLA Ops:
  7.2 100.8 %copy-start = (bf16[512,128]{1,0:T(8,128)(2,1)S(1)}, bf16[512,128]{1,0:T(8,128)(2,1)}, u32[]{:S(2)}) copy-start(bf16[512,128]{1,0:T(8,128)(2,1)} %param.16) | copy-start | bytes 393220
  7.2 3.9 copy-start.3
  7.2 3.9 copy-start.2
  7.2 100.8 %all-gather.2.cloned.1.call-start = ((), (), s32[]{:S(2)}) async-start(), calls=%async_computation.1 | async-start | bytes 2359296 | tf_op jit(solution)/shard_map/all_gather | solution.py:49
  7.9 178.1 %reduce-scatter.2.cloned.1.call-start = ((), (), s32[]{:S(2)}) async-start(), calls=%async_computation.2 | async-start | bytes 2359296 | tf_op jit(solution)/shard_map/reduce_scatter | solution.py:42
  76.2 3.8 copy-start.4
  79.2 331.8 %all-reduce.3.cloned.1.call-start = ((), (), s32[]{:S(2)}) async-start(), calls=%async_computation.3 | async-start | bytes 8388608 | tf_op jit(solution)/shard_map/psum | solution.py:82
  260.0 72.9 %copy-start.1 = (bf16[64,128,128]{2,1,0:T(8,128)(2,1)S(1)}, bf16[64,128,128]{2,1,0:T(8,128)(2,1)}, u32[]{:S(2)}) copy-start(bf16[64,128,128]{2,1,0:T(8,128)(2,1)} %all-gather.2.cloned.1.call-done) | copy-start | bytes 6291460
Sparse Core Ops, SparseCore 0:
  10.4 56.8 all-gather.1
  79.3 77.4 reduce-scatter.1
  260.1 150.8 all-reduce.2
where the time goes:
time: 421 us; the launch traced here: 419 us
  blocking collectives  225 us (53%)
  waiting for transfers between devices  69.9 us (17%)
  matrix products  49.4 us (12%)
  other arithmetic  28.7 us (7%)
  local copies, waits for them, and re-layouts  27.5 us (7%)
  between operations  13.9 us (3%)
  loops' own time  5.41 us (1%)
    pmax x1, blocking collectives, per_device(): row_max = lax.pmax(local_max, ('head', 'ctx'))  69.2 us
    psum x1, waiting for transfers between devices, per_device(): lax.psum((grad_queries_part, grad_weights_part), ('head', 'ctx'))  69.1 us
    psum x1, blocking collectives, per_device(): lax.psum((grad_queries_part, grad_weights_part), ('head', 'ctx'))  64.3 us
    psum x1, blocking collectives, per_device(): lax.psum((local_exp, local_target), ('head', 'ctx'))  63.2 us
    all_gather x1, blocking collectives, per_device(): lax.all_gather(index_weights, 'head', axis=0, tiled=True)  28 us
    dot_general x8, matrix products, one_block(): jnp.dot(cache_rows, query_flat.T, preferred_element_type=jnp.float32)  23.4 us
    reduce_sum x8, other arithmetic, one_block(): return jnp.where(visible, jnp.sum(weights, axis=1), 0.0)  11.3 us
    dot_general x1, matrix products, per_device(): grad_keys = jnp.dot(pre_flat, pair_flat, preferred_element_type=jnp.float32)  8.99 us
  transfers between devices with their start and end apart: 3, of which 1 were waited for; matrix products, arithmetic and copies ran while one was open for 22% of the time, Pallas kernels for 0%

commit v1 on v0

v1 whole, which is shorter than its diff:
```python
import functools
import math

import jax
import jax.numpy as jnp
from jax import lax
from jax.experimental import pallas as pl
from jax.experimental.pallas import tpu as pltpu
from jax.sharding import Mesh
from jax.sharding import PartitionSpec as P

att_scale = 192.0 ** (-0.5)
loss_scale = 1024.0
masked_floor = -1e30
log2e = math.log2(math.e)
chunks = 2

NT = (((1,), (1,)), ((), ()))
NN = (((1,), (0,)), ((), ()))
f32 = jnp.float32
bf16 = jnp.bfloat16


def dot(a, b, dims=NN):
    return lax.dot_general(a, b, dims, preferred_element_type=f32)


def visible_mask(kp_row, qp_row):
    n = kp_row.shape[1]
    q = qp_row.shape[1]
    kp = jnp.transpose(jnp.broadcast_to(kp_row, (q, n)))
    return kp <= jnp.broadcast_to(qp_row, (n, q))


def params(mb=40):
    return pltpu.CompilerParams(vmem_limit_bytes=mb * 1024 * 1024)


def probs_kernel(cache, q, nrm, kp, qp, out, tot):
    rows = cache.shape[0]
    heads, queries = nrm.shape
    x = cache[...]
    acc = jnp.zeros((rows, queries), f32)
    for pair in range(heads // 2):
        s = dot(x, q[pl.ds(pair * 2 * queries, 2 * queries), :], NT)
        for u in range(2):
            n = nrm[pl.ds(pair * 2 + u, 1), :] * log2e
            acc += jnp.exp2(s[:, u * queries : (u + 1) * queries] * (att_scale * log2e) - n)
    acc = jnp.where(visible_mask(kp[0], qp[...]), acc, 0.0)
    out[0] = acc

    @pl.when(pl.program_id(0) == 0)
    def _():
        tot[...] = jnp.zeros(tot.shape, f32)

    tot[...] += jnp.broadcast_to(jnp.sum(acc, axis=0, keepdims=True), tot.shape)


def probs_chunk(c, cache, q, nrm, kp, qp, parts):
    keys, width = cache.shape
    rows = keys // parts // chunks
    heads, queries = nrm.shape
    return pl.pallas_call(
        probs_kernel,
        grid=(parts,),
        in_specs=[
            pl.BlockSpec((rows, width), lambda d: (d * chunks + c, 0)),
            pl.BlockSpec(q.shape, lambda d: (0, 0)),
            pl.BlockSpec(nrm.shape, lambda d: (0, 0)),
            pl.BlockSpec((1, 1, rows), lambda d: (d * chunks + c, 0, 0)),
            pl.BlockSpec(qp.shape, lambda d: (0, 0)),
        ],
        out_specs=[
            pl.BlockSpec((1, rows, queries), lambda d: (d, 0, 0)),
            pl.BlockSpec((8, queries), lambda d: (0, 0)),
        ],
        out_shape=[
            jax.ShapeDtypeStruct((parts, rows, queries), f32),
            jax.ShapeDtypeStruct((8, queries), f32),
        ],
        compiler_params=params(),
        cost_estimate=pl.CostEstimate(
            flops=2 * parts * rows * q.shape[0] * width,
            bytes_accessed=parts * rows * width * 2 + q.size * 2,
            transcendentals=parts * rows * q.shape[0],
        ),
        name="probs",
    )(cache, q, nrm, kp.reshape(parts * chunks, 1, rows), qp)


def logits_kernel(scale, half_rows, keys, qa, qb, kp, qp, e_out, stats, acc):
    queries = qp.shape[1]
    step = pl.program_id(0)

    @pl.when(step == 0)
    def _():
        acc[...] = jnp.zeros(acc.shape, f32)

    k = keys[...]
    total = acc[...]
    for q in (qa, qb):
        for pair in range(half_rows // queries // 2):
            s = dot(k, q[0, pl.ds(pair * 2 * queries, 2 * queries), :], NT)
            w = q[0, pl.ds(half_rows, 16), :].astype(f32)
            for u in range(2):
                row = pair * 2 + u
                total += jnp.maximum(s[:, u * queries : (u + 1) * queries], 0.0) * w[row : row + 1]
    acc[...] = total

    @pl.when(step == pl.num_programs(0) - 1)
    def _():
        vis = visible_mask(kp[...], qp[...])
        hidden = jnp.where(vis, total * scale, masked_floor)
        m = jnp.max(hidden, axis=0, keepdims=True)
        e = jnp.where(vis, jnp.exp(hidden - m), 0.0)
        e_out[...] = e
        z = jnp.sum(e, axis=0, keepdims=True)
        rows = lax.broadcasted_iota(jnp.int32, stats.shape, 0)
        stats[...] = jnp.where(rows == 0, m, z)


def logits_call(keys, qa, qb, kp, qp, scale, half_rows):
    n, width = keys.shape
    parts, rows, _ = qa.shape
    queries = qp.shape[1]
    qspec = pl.BlockSpec((1, rows, width), lambda d: (d, 0, 0))
    full = lambda a: pl.BlockSpec(a.shape, lambda d: (0, 0))
    return pl.pallas_call(
        functools.partial(logits_kernel, scale, half_rows),
        grid=(parts,),
        in_specs=[full(keys), qspec, qspec, full(kp), full(qp)],
        out_specs=[
            pl.BlockSpec((n, queries), lambda d: (0, 0)),
            pl.BlockSpec((8, queries), lambda d: (0, 0)),
        ],
        out_shape=[
            jax.ShapeDtypeStruct((n, queries), f32),
            jax.ShapeDtypeStruct((8, queries), f32),
        ],
        scratch_shapes=[pltpu.VMEM((n, queries), f32)],
        compiler_params=params(),
        cost_estimate=pl.CostEstimate(
            flops=4 * 2 * n * parts * half_rows * width,
            bytes_accessed=parts * rows * width * 4,
            transcendentals=0,
        ),
        name="logits",
    )(keys, qa, qb, kp, qp)


def lg_kernel(*refs):
    recs = refs[:chunks]
    e, own, stats, kp, qp, lg = refs[chunks:]
    s = jnp.concatenate([jnp.sum(r[...], axis=0) for r in recs], axis=0)
    m_all, z_all, t_all = stats[:, 0, :], stats[:, 1, :], stats[:, 2, :]
    top = jnp.max(m_all, axis=0, keepdims=True)
    z = jnp.sum(z_all * jnp.exp(m_all - top), axis=0, keepdims=True)
    t = jnp.sum(t_all, axis=0, keepdims=True)
    p = e[...] * jnp.exp(own[0:1, :] - top) / z
    target = s / t
    lg[...] = loss_scale * jnp.where(visible_mask(kp[...], qp[...]), p - target, 0.0)


def lg_call(recs, e, own, stats, kp, qp):
    return pl.pallas_call(
        lg_kernel,
        out_shape=jax.ShapeDtypeStruct(e.shape, f32),
        compiler_params=params(),
        cost_estimate=pl.CostEstimate(
            flops=sum(r.size for r in recs), bytes_accessed=4 * sum(r.size for r in recs), transcendentals=0
        ),
        name="logit_grad",
    )(*recs, e, own, stats, kp, qp)


def grads_kernel(scale, half_rows, first, *refs):
    if first:
        keys, keys_t, lg_ref, q, out, gk = refs
    else:
        keys, keys_t, lg_ref, q, gk_in, out, gk = refs
    queries = lg_ref.shape[1]
    width = keys.shape[1]
    half = width // 2

    @pl.when(pl.program_id(0) == 0)
    def _():
        gk[...] = jnp.zeros(gk.shape, f32) if first else gk_in[...]

    k = keys[...]
    lg = lg_ref[...]
    w = q[0, pl.ds(half_rows, 16), :].astype(f32) * scale
    for pair in range(half_rows // queries // 2):
        qp = q[0, pl.ds(pair * 2 * queries, 2 * queries), :]
        s = dot(k, qp, NT)
        pres = []
        for u in range(2):
            row = pair * 2 + u
            su = s[:, u * queries : (u + 1) * queries]
            pres.append(jnp.where(su > 0.0, w[row : row + 1] * lg, 0.0).astype(bf16))
            gw = scale * jnp.sum(jnp.maximum(su, 0.0) * lg, axis=0, keepdims=True)
            for v in range(2):
                out[row * 2 + v, pl.ds(half, 8), :] = jnp.broadcast_to(gw, (8, queries))
        pre = jnp.concatenate(pres, axis=1)
        gk[...] += dot(pre, qp)
        gq = dot(keys_t[...], pre)
        for u in range(2):
            for v in range(2):
                out[(pair * 2 + u) * 2 + v, pl.ds(0, half), :] = gq[
                    v * half : (v + 1) * half, u * queries : (u + 1) * queries
                ]


def grads_call(keys, keys_t, lg, q, gk_in, scale, half_rows):
    n, width = keys.shape
    parts, rows, _ = q.shape
    queries = lg.shape[1]
    per = 2 * half_rows // queries
    full = lambda a: pl.BlockSpec(a.shape, lambda d: (0, 0))
    first = gk_in is None
    args = [keys, keys_t, lg, q] + ([] if first else [gk_in])
    specs = [full(keys), full(keys_t), full(lg), pl.BlockSpec((1, rows, width), lambda d: (d, 0, 0))]
    specs += [] if first else [full(gk_in)]
    return pl.pallas_call(
        functools.partial(grads_kernel, scale, half_rows, first),
        grid=(parts,),
        in_specs=specs,
        out_specs=[
            pl.BlockSpec((per, width // 2 + 8, queries), lambda d: (d, 0, 0)),
            pl.BlockSpec((n, width), lambda d: (0, 0)),
        ],
        out_shape=[
            jax.ShapeDtypeStruct((parts * per, width // 2 + 8, queries), f32),
            jax.ShapeDtypeStruct((n, width), f32),
        ],
        compiler_params=params(),
        cost_estimate=pl.CostEstimate(
            flops=3 * 2 * n * parts * half_rows * width,
            bytes_accessed=parts * rows * width * 6,
            transcendentals=0,
        ),
        name="grads",
    )(*args)


def sum_kernel(rec, out):
    total = jnp.sum(rec[...], axis=0)
    for i in range(out.shape[0]):
        out[i] = total


def sum_call(rec, copies):
    return pl.pallas_call(
        sum_kernel,
        out_shape=jax.ShapeDtypeStruct((copies,) + rec.shape[1:], f32),
        compiler_params=params(),
        name="sum_parts",
    )(rec)


def place_kernel(rec, gq, gw):
    heads, _, width = gq.shape
    half = width // 2
    for j in range(heads):
        core, jj = j // (heads // 2), j % (heads // 2)
        lo, hi = (jj * 2) * 2 + core, (jj * 2 + 1) * 2 + core
        both = jnp.concatenate([rec[lo, pl.ds(0, half), :], rec[hi, pl.ds(0, half), :]], axis=0)
        gq[j] = jnp.transpose(both)
        gw[pl.ds(j, 1), :] = rec[lo, pl.ds(half, 1), :]


def place_call(rec, heads, width):
    queries = rec.shape[2]
    return pl.pallas_call(
        place_kernel,
        out_shape=[
            jax.ShapeDtypeStruct((heads, queries, width), f32),
            jax.ShapeDtypeStruct((heads, queries), f32),
        ],
        compiler_params=params(),
        name="place",
    )(rec)


def spread(x, axes, count):
    return lax.all_to_all(jnp.broadcast_to(x[None], (count,) + x.shape), axes, 0, 0, tiled=True)


def per_device(
    mla_queries,
    latent_cache,
    normalizers,
    query_positions,
    key_positions,
    index_queries,
    index_keys,
    index_weights,
):
    head_count, query_count, _ = mla_queries.shape
    query_flat = mla_queries.reshape(head_count * query_count, mla_queries.shape[2])
    sub_keys, index_width = index_keys.shape
    parts = lax.axis_size("head")
    zy = lax.axis_size("zy")
    local_heads = index_queries.shape[0]
    half_heads = local_heads // 2
    half_rows = half_heads * query_count
    index_scale = (local_heads * parts * index_width) ** (-0.5)
    core = lax.axis_index("core")
    swap = [(0, 1), (1, 0)]
    qp = query_positions.reshape(1, query_count)

    own_q = lax.dynamic_slice_in_dim(index_queries, core * half_heads, half_heads, 0)
    own_w = lax.dynamic_slice_in_dim(index_weights, core * half_heads, half_heads, 0)
    own = jnp.concatenate(
        [
            own_q.reshape(half_rows, index_width),
            jnp.pad(own_w, ((0, 16 - half_heads), (0, 0))),
        ],
        axis=0,
    )
    q_mine = spread(own, "head", parts)
    q_other = lax.ppermute(q_mine, "core", swap)

    pieces = [
        probs_chunk(c, latent_cache, query_flat, normalizers, key_positions, qp, parts) for c in range(chunks)
    ]
    recs = [lax.all_to_all(s, "head", 0, 0, tiled=True) for s, _ in pieces]

    offset = lax.axis_index("head") * sub_keys
    own_kp = lax.dynamic_slice_in_dim(key_positions, offset, sub_keys, 0).reshape(1, sub_keys)
    e, local = logits_call(index_keys, q_mine, q_other, own_kp, qp, index_scale, half_rows)
    target_total = sum(t for _, t in pieces)[0:1]
    stats = jnp.concatenate([local[0:2], target_total, target_total], axis=0)
    all_stats = spread(stats, ("head", "zy", "core"), parts * zy * 2)
    lg = lg_call(recs, e, local, all_stats, own_kp, qp)

    keys_t = index_keys.T
    out_other, gk = grads_call(index_keys, keys_t, lg, q_other, None, index_scale, half_rows)
    got = lax.ppermute(out_other, "core", swap)
    out_mine, gk = grads_call(index_keys, keys_t, lg, q_mine, gk, index_scale, half_rows)
    block = lax.all_to_all(out_mine + got, ("head", "zy"), 0, 0, tiled=True)
    summed = sum_call(block, zy * 2)
    final = lax.all_to_all(summed, ("zy", "core"), 0, 0, tiled=True)
    gq, gw = place_call(final, local_heads, index_width)
    return gq, gw, gk


def solution(mesh):
    heads = mesh.shape["head"]
    ctx = mesh.shape["ctx"]
    fine = Mesh(mesh.devices.reshape(heads, ctx // 2, 2), ("head", "zy", "core"))
    split = ("zy", "core")
    placed = (
        P("head", None, None),
        P(split, None),
        P("head", None),
        P(),
        P(split),
        P("head", None, None),
        P(split + ("head",), None),
        P("head", None),
    )
    return jax.shard_map(
        per_device,
        mesh=fine,
        in_specs=placed,
        out_specs=(P("head", None, None), P("head", None), P(split + ("head",), None)),
        check_vma=False,
    )
```

time: 421 us -> 169 us (0.40)
  blocking collectives: 225 us -> 52.2 us
  matrix products: 49.4 us -> 0 us
  waiting for transfers between devices: 69.9 us -> 24.5 us
  Pallas kernels: 0 us -> 40.9 us
  other arithmetic: 28.7 us -> 0.26 us
  starting transfers between devices: 0.12 us -> 27.3 us
  between operations: 13.9 us -> 0.8 us
  loops' own time: 5.41 us -> 0 us
  local copies, waits for them, and re-layouts: 27.5 us -> 22.4 us
    psum x2 -> x0, blocking collectives: 127 us -> none  [the longest x1 64.3 us: per_device(): lax.psum((grad_queries_part, grad_weights_part), ('head', 'ctx'))]
    pmax x1 -> x0, blocking collectives: 69.2 us -> none  [per_device(): row_max = lax.pmax(local_max, ('head', 'ctx'))]
    psum x1 -> x0, waiting for transfers between devices: 69.1 us -> none  [per_device(): lax.psum((grad_queries_part, grad_weights_part), ('head', 'ctx'))]
    all_to_all x0 -> x2, blocking collectives: none -> 52.2 us  [the longest x1 36.2 us: per_device(): block = lax.all_to_all(out_mine + got, ('head', 'zy'), 0, 0, tiled=True)]
    dot_general x11 -> x0, matrix products: 49.4 us -> none  [the longest x8 23.4 us: one_block(): jnp.dot(cache_rows, query_flat.T, preferred_element_type=jnp.float32)]
    pallas_call x0 -> x8, Pallas kernels: none -> 40.9 us  [the longest x2 17.8 us: probs_chunk(): pl.pallas_call(probs_kernel, grid=(parts,), in_specs=[pl.BlockSpec((rows,...]
    all_gather x1 -> x0, blocking collectives: 28 us -> none  [per_device(): lax.all_gather(index_weights, 'head', axis=0, tiled=True)]
    all_to_all x0 -> x4, starting transfers between devices: none -> 25.4 us  [the longest x2 14.1 us: spread(): lax.all_to_all(jnp.broadcast_to(x[None], (count,) + x.shape), axes, 0, 0,...]
  transfers between devices with their start and end apart: 3 -> 6, of which waited for: 1 -> 3; matrix products, arithmetic and copies ran while one was open for 22% -> 7% of each run, Pallas kernels for 0% -> 19%
where the time goes in v1:
time: 169 us; the launch traced here: 168 us
  blocking collectives  52.2 us (31%)
  Pallas kernels  40.9 us (24%)
  starting transfers between devices  27.3 us (16%)
  waiting for transfers between devices  24.5 us (14%)
  local copies, waits for them, and re-layouts  22.4 us (13%)
    all_to_all x1, blocking collectives, per_device(): block = lax.all_to_all(out_mine + got, ('head', 'zy'), 0, 0, tiled=True)  36.2 us
    unnamed x23, local copies, waits for them, and re-layouts  19.7 us
    pallas_call x2, Pallas kernels, probs_chunk(): pl.pallas_call(probs_kernel, grid=(parts,), in_specs=[pl.BlockSpec((rows,...  17.8 us
    all_to_all x1, blocking collectives, per_device(): final = lax.all_to_all(summed, ('zy', 'core'), 0, 0, tiled=True)  16 us
    pallas_call x2, Pallas kernels, grads_call(): pl.pallas_call(functools.partial(grads_kernel, scale, half_rows, first),...  15.1 us
    all_to_all x2, starting transfers between devices, spread(): lax.all_to_all(jnp.broadcast_to(x[None], (count,) + x.shape), axes, 0, 0,...  14.1 us
    all_to_all x2, waiting for transfers between devices, per_device(): recs = [lax.all_to_all(s, 'head', 0, 0, tiled=True) for s, _ in pieces]  13.1 us
    all_to_all x2, waiting for transfers between devices, spread(): lax.all_to_all(jnp.broadcast_to(x[None], (count,) + x.shape), axes, 0, 0,...  11.4 us
  transfers between devices with their start and end apart: 6, of which 3 were waited for; matrix products, arithmetic and copies ran while one was open for 7% of the time, Pallas kernels for 19%

profile of v1, /device:TPU:1, one launch (start us, length us, event | category | flops | bytes accessed | tf_op | source)
XLA Modules:
  0.0 168.4 jit_solution(9956492490541967368)
XLA Ops:
  0.6 0.0 copy-start
  0.7 0.7 constant_dynamic-slice_fusion
  1.4 0.2 copy-done
  1.6 1.1 broadcast_in_dim.4
  2.8 8.2 %all-to-all-start.2 = ((bf16[8,528,128]{2,1,0:T(8,128)(2,1)}), bf16[8,528,128]{2,1,0:T(8,128)(2,1)}, u32[]{:S(2)}, u32[]{:S(2)}) async-start(bf16[8,528,128]{2,1,0:T(8,128)(2,1)} %broadcast_in_dim.4), calls=%async_computation.2 | async-start | bytes 2162688 | tf_op jit(solution)/shard_map/all_to_all | solution.py:285
  10.9 7.7 %copy.13.cache = bf16[4096,576]{1,0:T(8,128)(2,1)} copy(bf16[4096,576]{0,1:T(8,128)(2,1)} %param.9) | data formatting | bytes 9437184 | tf_op args[1]
  18.6 0.0 copy-start.7
  18.6 0.0 copy-start.8
  18.6 0.0 copy-start.9
  18.6 3.1 %copy.12 = bf16[16,128,576]{2,1,0:T(8,128)(2,1)S(1)} copy(bf16[16,128,576]{1,2,0:T(8,128)(2,1)} %param.8) | data formatting | bytes 4718592 | tf_op args[0]
  21.7 0.0 copy-start.3
  21.7 0.0 copy-done.7
  21.7 0.0 copy-done.8
  21.7 0.0 copy-done.9
  21.7 0.0 copy-start.1
  21.8 3.4 %copy-done.1 = bf16[4096,576]{1,0:T(8,128)(2,1)S(1)} copy-done((bf16[4096,576]{1,0:T(8,128)(2,1)S(1)}, bf16[4096,576]{1,0:T(8,128)(2,1)}, u32[]{:S(2)}) %copy-start.1) | copy-done | bytes 4718616
  25.2 8.6 %probs.2 = (f32[8,256,128]{2,1,0:T(8,128)S(1)}, f32[8,128]{1,0:T(8,128)S(1)}) custom-call(bf16[4096,576]{1,0:T(8,128)(2,1)S(1)} %copy-done.1, bf16[2048,576]{1,0:T(8,128)(2,1)S(1)} %bitcast.6, f32[16,128]{1,0:T(8,128)S(1)} %copy-done.9, s32[16,1,256]{2,1,0:T(1,128)S(1)} %bitcast.16, s32[1,128]{1,0:T(1,128)S(1)} %bitcast.12), custom_call_target="tpu_custom_call" | custom-call | flops 4831838208 | bytes 4718592 | tf_op jit(solution)/shard_map/probs/pallas_call | solution.py:63
  33.8 0.0 copy-done.3
  33.8 0.0 copy-start.5
  33.8 1.0 copy-done.5
  34.8 0.0 all-to-all-done.2.qa.refs_3_
  34.8 6.7 %all-to-all-start = ((f32[8,256,128]{2,1,0:T(8,128)}), f32[8,256,128]{2,1,0:T(8,128)S(1)}, u32[]{:S(2)}, u32[]{:S(2)}) async-start(f32[8,256,128]{2,1,0:T(8,128)} %copy-done.5), calls=%async_computation | async-start | bytes 2097152 | tf_op jit(solution)/shard_map/all_to_all | solution.py:326
  41.4 1.5 collective-permute-start
  42.9 0.0 copy-start.2
  42.9 2.5 %copy-done.2 = bf16[4096,576]{1,0:T(8,128)(2,1)S(1)} copy-done((bf16[4096,576]{1,0:T(8,128)(2,1)S(1)}, bf16[4096,576]{1,0:T(8,128)(2,1)}, u32[]{:S(2)}) %copy-start.2) | copy-done | bytes 4718616
  45.4 1.7 %copy-done.4 = bf16[16,128,576]{2,1,0:T(8,128)(2,1)S(1)} copy-done((bf16[16,128,576]{2,1,0:T(8,128)(2,1)S(1)}, bf16[16,128,576]{2,1,0:T(8,128)(2,1)}, u32[]{:S(2)}) %copy-start.4) | copy-done | bytes 2359320
  47.2 9.2 %probs.3 = (f32[8,256,128]{2,1,0:T(8,128)}, f32[8,128]{1,0:T(8,128)S(1)}) custom-call(bf16[4096,576]{1,0:T(8,128)(2,1)S(1)} %copy-done.2, bf16[2048,576]{1,0:T(8,128)(2,1)S(1)} %bitcast.7, f32[16,128]{1,0:T(8,128)S(1)} %copy-done.9, s32[16,1,256]{2,1,0:T(1,128)S(1)} %bitcast.17, s32[1,128]{1,0:T(1,128)S(1)} %bitcast.13), custom_call_target="tpu_custom_call" | custom-call | flops 4831838208 | bytes 4718592 | tf_op jit(solution)/shard_map/probs/pallas_call | solution.py:63
  56.4 2.4 %all-to-all-done.refs_0_ = f32[8,256,128]{2,1,0:T(8,128)S(1)} async-done(((f32[8,256,128]{2,1,0:T(8,128)}), f32[8,256,128]{2,1,0:T(8,128)S(1)}, u32[]{:S(2)}, u32[]{:S(2)}) %all-to-all-start) | async-done | bytes 1048608 | tf_op jit(solution)/shard_map/all_to_all | solution.py:326
  58.7 4.6 %all-to-all-start.1 = ((f32[8,256,128]{2,1,0:T(8,128)}), f32[8,256,128]{2,1,0:T(8,128)S(1)}, u32[]{:S(2)}, u32[]{:S(2)}) async-start(f32[8,256,128]{2,1,0:T(8,128)} %get-tuple-element.16), calls=%async_computation.1 | async-start | bytes 2097152 | tf_op jit(solution)/shard_map/all_to_all | solution.py:326
  63.3 0.1 dynamic_slice.11
  63.4 0.0 collective-permute-done.qb.refs_3_
  63.4 0.0 copy-done.6
  63.4 6.5 %logits.1 = (f32[512,128]{1,0:T(8,128)S(1)}, f32[8,128]{1,0:T(8,128)S(1)}) custom-call(bf16[512,128]{1,0:T(8,128)(2,1)S(1)} %copy-done.6, bf16[8,528,128]{2,1,0:T(8,128)(2,1)} %all-to-all-done.2.qa.refs_3_, bf16[8,528,128]{2,1,0:T(8,128)(2,1)} %collective-permute-done.qb.refs_3_, s32[1,512]{1,0:T(1,128)S(1)} %bitcast.10, s32[1,128]{1,0:T(1,128)S(1)} %bitcast.14), custom_call_target="tpu_custom_call" | custom-call | flops 2147483648 | bytes 2162688 | tf_op jit(solution)/shard_map/logits/pallas_call | solution.py:128
  69.9 10.8 %all-to-all-done.1.refs_1_ = f32[8,256,128]{2,1,0:T(8,128)S(1)} async-done(((f32[8,256,128]{2,1,0:T(8,128)}), f32[8,256,128]{2,1,0:T(8,128)S(1)}, u32[]{:S(2)}, u32[]{:S(2)}) %all-to-all-start.1) | async-done | bytes 1048608 | tf_op jit(solution)/shard_map/all_to_all | solution.py:326
  80.7 0.7 broadcast_in_dim.5
  81.4 6.0 %all-to-all-start.3 = ((f32[128,4,128]{2,1,0:T(4,128)}), f32[128,4,128]{2,1,0:T(4,128)S(1)}, u32[]{:S(2)}, u32[]{:S(2)}) async-start(f32[128,4,128]{2,1,0:T(4,128)} %broadcast_in_dim.5), calls=%async_computation.3 | async-start | bytes 524288 | tf_op jit(solution)/shard_map/all_to_all | solution.py:285
  87.4 0.1 copy.11
  87.5 11.3 %all-to-all-done.3.refs_4_ = f32[128,4,128]{2,1,0:T(4,128)S(1)} async-done(((f32[128,4,128]{2,1,0:T(4,128)}), f32[128,4,128]{2,1,0:T(4,128)S(1)}, u32[]{:S(2)}, u32[]{:S(2)}) %all-to-all-start.3) | async-done | bytes 262176 | tf_op jit(solution)/shard_map/all_to_all | solution.py:285
  98.9 0.3 logit_grad.1.refs_2_
  99.2 7.2 %grads.2 = (f32[64,72,128]{2,1,0:T(8,128)S(1)}, f32[512,128]{1,0:T(8,128)S(1)}) custom-call(bf16[512,128]{1,0:T(8,128)(2,1)S(1)} %copy-done.6, bf16[128,512]{1,0:T(8,128)(2,1)S(1)} %bitcast.8, f32[512,128]{1,0:T(8,128)S(1)} %logit_grad.1.refs_2_, bf16[8,528,128]{2,1,0:T(8,128)(2,1)} %collective-permute-done.qb.refs_3_), custom_call_target="tpu_custom_call" | custom-call | flops 1610612736 | bytes 3244032 | tf_op jit(solution)/shard_map/grads/pallas_call | solution.py:223
  106.5 0.5 collective-permute-start.1
  106.9 7.9 %grads.3 = (f32[64,72,128]{2,1,0:T(8,128)S(1)}, f32[512,128]{1,0:T(8,128)}) custom-call(bf16[512,128]{1,0:T(8,128)(2,1)S(1)} %copy-done.6, bf16[128,512]{1,0:T(8,128)(2,1)S(1)} %bitcast.9, f32[512,128]{1,0:T(8,128)S(1)} %logit_grad.1.refs_2_, bf16[8,528,128]{2,1,0:T(8,128)(2,1)} %all-to-all-done.2.qa.refs_3_, f32[512,128]{1,0:T(8,128)S(1)} %get-tuple-element.21.refs_4_), custom_call_target="tpu_custom_call" | custom-call | flops 1610612736 | bytes 3244032 | tf_op jit(solution)/shard_map/grads/pallas_call | solution.py:223
  114.8 0.0 collective-permute-done.1
  114.8 0.2 add.18
  115.1 36.2 %all_to_all.30.rec = f32[64,72,128]{2,1,0:T(8,128)S(1)} all-to-all(f32[64,72,128]{2,1,0:T(8,128)S(1)} %add.18), channel_id=1, replica_groups=mesh['head'=8,'zy'=8,'core'=2] {'head','zy'}, dimensions={0} | all-to-all | bytes 4718592 | tf_op jit(solution)/shard_map/all_to_all | solution.py:340
  151.3 0.2 sum_parts.1
  151.4 16.0 %all_to_all.31.rec = f32[16,72,128]{2,1,0:T(8,128)S(1)} all-to-all(f32[16,72,128]{2,1,0:T(8,128)S(1)} %sum_parts.1), channel_id=1, replica_groups=mesh['head'=8,'zy'=8,'core'=2] {'zy','core'}, dimensions={0} | all-to-all | bytes 1179648 | tf_op jit(solution)/shard_map/all_to_all | solution.py:342
  167.4 1.0 place.1
  (8 shorter events, 0.0 us)
Async XLA Ops:
  0.6 1.0 copy-start
  2.8 32.0 %all-to-all-start.2 = ((bf16[8,528,128]{2,1,0:T(8,128)(2,1)}), bf16[8,528,128]{2,1,0:T(8,128)(2,1)}, u32[]{:S(2)}, u32[]{:S(2)}) async-start(bf16[8,528,128]{2,1,0:T(8,128)(2,1)} %broadcast_in_dim.4), calls=%async_computation.2 | async-start | bytes 2162688 | tf_op jit(solution)/shard_map/all_to_all | solution.py:285
  18.6 3.1 %copy-start.7 = (s32[128]{0:T(128)S(1)}, s32[128]{0:T(128)}, u32[]{:S(2)}) copy-start(s32[128]{0:T(128)} %param.11) | copy-start | bytes 1540
  18.6 3.2 %copy-start.8 = (s32[4096]{0:T(1024)S(1)}, s32[4096]{0:T(1024)}, u32[]{:S(2)}) copy-start(s32[4096]{0:T(1024)} %param.12) | copy-start | bytes 49156
  18.6 3.2 %copy-start.9 = (f32[16,128]{1,0:T(8,128)S(1)}, f32[16,128]{1,0:T(8,128)}, u32[]{:S(2)}) copy-start(f32[16,128]{1,0:T(8,128)} %nrm.3) | copy-start | bytes 24580
  21.7 12.1 %copy-start.3 = (bf16[16,128,576]{2,1,0:T(8,128)(2,1)}, bf16[16,128,576]{2,1,0:T(8,128)(2,1)S(1)}, u32[]{:S(2)}) copy-start(bf16[16,128,576]{2,1,0:T(8,128)(2,1)S(1)} %copy.12) | copy-start | bytes 7077892
  21.7 3.4 %copy-start.1 = (bf16[4096,576]{1,0:T(8,128)(2,1)S(1)}, bf16[4096,576]{1,0:T(8,128)(2,1)}, u32[]{:S(2)}) copy-start(bf16[4096,576]{1,0:T(8,128)(2,1)} %copy.13.cache) | copy-start | bytes 14155780
  33.8 1.0 copy-start.5
  34.8 24.0 %all-to-all-start = ((f32[8,256,128]{2,1,0:T(8,128)}), f32[8,256,128]{2,1,0:T(8,128)S(1)}, u32[]{:S(2)}, u32[]{:S(2)}) async-start(f32[8,256,128]{2,1,0:T(8,128)} %copy-done.5), calls=%async_computation | async-start | bytes 2097152 | tf_op jit(solution)/shard_map/all_to_all | solution.py:326
  41.4 22.0 %collective-permute-start = (bf16[8,528,128]{2,1,0:T(8,128)(2,1)}, bf16[8,528,128]{2,1,0:T(8,128)(2,1)}, u32[]{:S(2)}, u32[]{:S(2)}) collective-permute-start(bf16[8,528,128]{2,1,0:T(8,128)(2,1)} %all-to-all-done.2.qa.refs_3_), channel_id=1, source_target_pairs={{0,1},{1,0},{2,3},{3,2},{4,5},{5,4},{6,7},{7,6},{8,9},{9,8},{10,11... | collective-permute-start | bytes 3244040 | tf_op jit(solution)/shard_map/ppermute | solution.py:321
  42.9 2.5 %copy-start.2 = (bf16[4096,576]{1,0:T(8,128)(2,1)S(1)}, bf16[4096,576]{1,0:T(8,128)(2,1)}, u32[]{:S(2)}) copy-start(bf16[4096,576]{1,0:T(8,128)(2,1)} %copy.13.cache) | copy-start | bytes 14155780
  45.4 1.7 %copy-start.4 = (bf16[16,128,576]{2,1,0:T(8,128)(2,1)S(1)}, bf16[16,128,576]{2,1,0:T(8,128)(2,1)}, u32[]{:S(2)}) copy-start(bf16[16,128,576]{2,1,0:T(8,128)(2,1)} %copy-done.3) | copy-start | bytes 7077892
  47.1 16.2 %copy-start.6 = (bf16[512,128]{1,0:T(8,128)(2,1)S(1)}, bf16[512,128]{1,0:T(8,128)(2,1)}, u32[]{:S(2)}) copy-start(bf16[512,128]{1,0:T(8,128)(2,1)} %refs_0_.3) | copy-start | bytes 393220
  58.7 22.0 %all-to-all-start.1 = ((f32[8,256,128]{2,1,0:T(8,128)}), f32[8,256,128]{2,1,0:T(8,128)S(1)}, u32[]{:S(2)}, u32[]{:S(2)}) async-start(f32[8,256,128]{2,1,0:T(8,128)} %get-tuple-element.16), calls=%async_computation.1 | async-start | bytes 2097152 | tf_op jit(solution)/shard_map/all_to_all | solution.py:326
  81.4 17.4 %all-to-all-start.3 = ((f32[128,4,128]{2,1,0:T(4,128)}), f32[128,4,128]{2,1,0:T(4,128)S(1)}, u32[]{:S(2)}, u32[]{:S(2)}) async-start(f32[128,4,128]{2,1,0:T(4,128)} %broadcast_in_dim.5), calls=%async_computation.3 | async-start | bytes 524288 | tf_op jit(solution)/shard_map/all_to_all | solution.py:285
  106.5 8.4 %collective-permute-start.1 = (f32[64,72,128]{2,1,0:T(8,128)S(1)}, f32[64,72,128]{2,1,0:T(8,128)S(1)}, u32[]{:S(2)}, u32[]{:S(2)}) collective-permute-start(f32[64,72,128]{2,1,0:T(8,128)S(1)} %get-tuple-element.23), channel_id=1, source_target_pairs={{0,1},{1,0},{2,3},{3,2},{4,5},{5,4},{6,7},{7,6},{8,9},{9,8},{10,11... | collective-permute-start | bytes 7077896 | tf_op jit(solution)/shard_map/ppermute | solution.py:338

commit v2 on v1

--- a/solution.py
+++ b/solution.py
@@ -13,7 +13,6 @@
 loss_scale = 1024.0
 masked_floor = -1e30
 log2e = math.log2(math.e)
-chunks = 2
 
 NT = (((1,), (1,)), ((), ()))
 NN = (((1,), (0,)), ((), ()))
@@ -36,56 +35,100 @@
     return pltpu.CompilerParams(vmem_limit_bytes=mb * 1024 * 1024)
 
 
-def probs_kernel(cache, q, nrm, kp, qp, out, tot):
-    rows = cache.shape[0]
+def exponent(top):
+    return jnp.clip(jnp.ceil(jnp.log2(jnp.maximum(top, 1e-37))), -122.0, 128.0)
+
+
+def shrink(x, e):
+    r = jnp.exp2(e * -0.5)
+    return (x * r) * r
+
+
+def grow(x, e):
+    r = jnp.exp2(e * 0.5)
+    return (x * r) * r
+
+
+def to_code(x):
+    return jnp.clip(jnp.floor(x + 0.5), -32768.0, 32767.0).astype(jnp.int32).astype(jnp.int16)
+
+
+def from_code(c):
+    return c.astype(jnp.int32).astype(f32)
+
+
+def root_code(x, e):
+    return to_code(jnp.sqrt(jnp.sqrt(shrink(x, e))) * 65535.0 - 32768.0)
+
+
+def root_decode(c, e):
+    r = (from_code(c) + 32768.0) * (1.0 / 65535.0) * jnp.exp2(e * 0.25)
+    r = r * r
+    return r * r
+
+
+def probs_kernel(cache, q, nrm, kp, qp, out, tot, qt, nb):
+    keys = cache.shape[1]
     heads, queries = nrm.shape
-    x = cache[...]
-    acc = jnp.zeros((rows, queries), f32)
-    for pair in range(heads // 2):
-        s = dot(x, q[pl.ds(pair * 2 * queries, 2 * queries), :], NT)
-        for u in range(2):
-            n = nrm[pl.ds(pair * 2 + u, 1), :] * log2e
-            acc += jnp.exp2(s[:, u * queries : (u + 1) * queries] * (att_scale * log2e) - n)
-    acc = jnp.where(visible_mask(kp[0], qp[...]), acc, 0.0)
-    out[0] = acc
 
     @pl.when(pl.program_id(0) == 0)
     def _():
         tot[...] = jnp.zeros(tot.shape, f32)
-
-    tot[...] += jnp.broadcast_to(jnp.sum(acc, axis=0, keepdims=True), tot.shape)
-
-
-def probs_chunk(c, cache, q, nrm, kp, qp, parts):
-    keys, width = cache.shape
-    rows = keys // parts // chunks
+        for h in range(heads):
+            qt[pl.ds(h * queries, queries), :] = jnp.transpose(q[h])
+            nb[h] = jnp.transpose(jnp.broadcast_to(nrm[pl.ds(h, 1), :] * log2e, (queries, queries)))
+
+    x = cache[...]
+    acc = [jnp.zeros((queries, queries), f32) for _ in range(keys // queries)]
+    for pair in range(heads // 2):
+        s = dot(qt[pl.ds(pair * 2 * queries, 2 * queries), :], x)
+        for u in range(2):
+            n = nb[pair * 2 + u]
+            for i in range(len(acc)):
+                block = s[u * queries : (u + 1) * queries, i * queries : (i + 1) * queries]
+                acc[i] += jnp.exp2(block * (att_scale * log2e) - n)
+    summed = jnp.concatenate([jnp.transpose(a) for a in acc], axis=0)
+    summed = jnp.where(visible_mask(kp[0], qp[...]), summed, 0.0)
+    e = exponent(jnp.max(summed, axis=0, keepdims=True))
+    out[0, pl.ds(0, keys), :] = root_code(summed, e)
+    out[0, pl.ds(keys, 16), :] = to_code(jnp.broadcast_to(e, (16, queries)))
+    tot[...] += jnp.broadcast_to(jnp.sum(summed, axis=0, keepdims=True), tot.shape)
+
+
+def probs_call(cache_t, q_t, nrm, kp, qp, parts):
+    width, keys = cache_t.shape
+    rows = keys // parts
     heads, queries = nrm.shape
     return pl.pallas_call(
         probs_kernel,
         grid=(parts,),
         in_specs=[
-            pl.BlockSpec((rows, width), lambda d: (d * chunks + c, 0)),
-            pl.BlockSpec(q.shape, lambda d: (0, 0)),
+            pl.BlockSpec((width, rows), lambda d: (0, d)),
+            pl.BlockSpec(q_t.shape, lambda d: (0, 0, 0)),
             pl.BlockSpec(nrm.shape, lambda d: (0, 0)),
-            pl.BlockSpec((1, 1, rows), lambda d: (d * chunks + c, 0, 0)),
+            pl.BlockSpec((1, 1, rows), lambda d: (d, 0, 0)),
             pl.BlockSpec(qp.shape, lambda d: (0, 0)),
         ],
         out_specs=[
-            pl.BlockSpec((1, rows, queries), lambda d: (d, 0, 0)),
+            pl.BlockSpec((1, rows + 16, queries), lambda d: (d, 0, 0)),
             pl.BlockSpec((8, queries), lambda d: (0, 0)),
         ],
         out_shape=[
-            jax.ShapeDtypeStruct((parts, rows, queries), f32),
+            jax.ShapeDtypeStruct((parts, rows + 16, queries), jnp.int16),
             jax.ShapeDtypeStruct((8, queries), f32),
         ],
-        compiler_params=params(),
+        scratch_shapes=[
+            pltpu.VMEM((heads * queries, width), bf16),
+            pltpu.VMEM((heads, queries, queries), f32),
+        ],
+        compiler_params=params(56),
         cost_estimate=pl.CostEstimate(
-            flops=2 * parts * rows * q.shape[0] * width,
-            bytes_accessed=parts * rows * width * 2 + q.size * 2,
-            transcendentals=parts * rows * q.shape[0],
+            flops=2 * keys * q_t.size,
+            bytes_accessed=cache_t.size * 2 + q_t.size * 2,
+            transcendentals=keys * heads * queries,
         ),
         name="probs",
-    )(cache, q, nrm, kp.reshape(parts * chunks, 1, rows), qp)
+    )(cache_t, q_t, nrm, kp.reshape(parts, 1, rows), qp)
 
 
 def logits_kernel(scale, half_rows, keys, qa, qb, kp, qp, e_out, stats, acc):
@@ -148,10 +191,12 @@
     )(keys, qa, qb, kp, qp)
 
 
-def lg_kernel(*refs):
-    recs = refs[:chunks]
-    e, own, stats, kp, qp, lg = refs[chunks:]
-    s = jnp.concatenate([jnp.sum(r[...], axis=0) for r in recs], axis=0)
+def lg_kernel(rec, e, own, stats, kp, qp, lg):
+    n = e.shape[0]
+    s = jnp.zeros(e.shape, f32)
+    for i in range(rec.shape[0]):
+        ex = from_code(rec[i, pl.ds(n, 16), :])[0:1]
+        s += root_decode(rec[i, pl.ds(0, n), :], ex)
     m_all, z_all, t_all = stats[:, 0, :], stats[:, 1, :], stats[:, 2, :]
     top = jnp.max(m_all, axis=0, keepdims=True)
     z = jnp.sum(z_all * jnp.exp(m_all - top), axis=0, keepdims=True)
@@ -161,16 +206,14 @@
     lg[...] = loss_scale * jnp.where(visible_mask(kp[...], qp[...]), p - target, 0.0)
 
 
-def lg_call(recs, e, own, stats, kp, qp):
+def lg_call(rec, e, own, stats, kp, qp):
     return pl.pallas_call(
         lg_kernel,
         out_shape=jax.ShapeDtypeStruct(e.shape, f32),
         compiler_params=params(),
-        cost_estimate=pl.CostEstimate(
-            flops=sum(r.size for r in recs), bytes_accessed=4 * sum(r.size for r in recs), transcendentals=0
-        ),
+        cost_estimate=pl.CostEstimate(flops=8 * rec.size, bytes_accessed=2 * rec.size, transcendentals=0),
         name="logit_grad",
-    )(*recs, e, own, stats, kp, qp)
+    )(rec, e, own, stats, kp, qp)
 
 
 def grads_kernel(scale, half_rows, first, *refs):
@@ -242,16 +285,62 @@
     )(*args)
 
 
+def code_kernel(a, b, out):
+    x = a[...] + b[...]
+    half = x.shape[1] - 8
+    queries = x.shape[2]
+    for i in range(x.shape[0]):
+        g = x[i, 0:half]
+        e = exponent(jnp.max(jnp.abs(g), axis=0, keepdims=True))
+        out[i, pl.ds(0, half), :] = to_code(shrink(g, e) * 32767.0)
+        w = x[i, half : half + 8]
+        ew = exponent(jnp.abs(w))
+        fine = shrink(w, ew) * 32767.0
+        hi = jnp.floor(fine + 0.5)
+        lo = (fine - hi) * 65534.0
+        e16 = jnp.broadcast_to(e, (16, queries))
+        spare = jnp.concatenate([ew, ew], axis=0)
+        row = lax.broadcasted_iota(jnp.int32, (16, queries), 0)
+        spare = jnp.where(row == 0, e16, spare)
+        spare = jnp.where(row == 2, jnp.concatenate([hi, hi], axis=0), spare)
+        spare = jnp.where(row == 3, jnp.concatenate([lo, lo], axis=0), spare)
+        out[i, pl.ds(half, 16), :] = to_code(spare)
+
+
+def code_call(a, b, parts):
+    n, rows, queries = a.shape
+    per = n // parts
+    spec = pl.BlockSpec((per, rows, queries), lambda d: (d, 0, 0))
+    return pl.pallas_call(
+        code_kernel,
+        grid=(parts,),
+        in_specs=[spec, spec],
+        out_specs=pl.BlockSpec((per, rows + 8, queries), lambda d: (d, 0, 0)),
+        out_shape=jax.ShapeDtypeStruct((n, rows + 8, queries), jnp.int16),
+        compiler_params=params(),
+        name="code_parts",
+    )(a, b)
+
+
 def sum_kernel(rec, out):
-    total = jnp.sum(rec[...], axis=0)
+    half = rec.shape[1] - 16
+    queries = rec.shape[2]
+    g = jnp.zeros((half, queries), f32)
+    w = jnp.zeros((1, queries), f32)
+    for i in range(rec.shape[0]):
+        spare = from_code(rec[i, pl.ds(half, 16), :])
+        g += grow(from_code(rec[i, pl.ds(0, half), :]) * (1.0 / 32767.0), spare[0:1])
+        w += grow((spare[2:3] + spare[3:4] * (1.0 / 65534.0)) * (1.0 / 32767.0), spare[1:2])
     for i in range(out.shape[0]):
-        out[i] = total
+        out[i, pl.ds(0, half), :] = g
+        out[i, pl.ds(half, 8), :] = jnp.broadcast_to(w, (8, queries))
 
 
 def sum_call(rec, copies):
+    n, rows, queries = rec.shape
     return pl.pallas_call(
         sum_kernel,
-        out_shape=jax.ShapeDtypeStruct((copies,) + rec.shape[1:], f32),
+        out_shape=jax.ShapeDtypeStruct((copies, rows - 8, queries), f32),
         compiler_params=params(),
         name="sum_parts",
     )(rec)
@@ -295,8 +384,7 @@
     index_keys,
     index_weights,
 ):
-    head_count, query_count, _ = mla_queries.shape
-    query_flat = mla_queries.reshape(head_count * query_count, mla_queries.shape[2])
+    query_count = mla_queries.shape[1]
     sub_keys, index_width = index_keys.shape
     parts = lax.axis_size("head")
     zy = lax.axis_size("zy")
@@ -318,26 +406,25 @@
         axis=0,
     )
     q_mine = spread(own, "head", parts)
+    coded, totals = probs_call(
+        latent_cache.T, mla_queries.transpose(0, 2, 1), normalizers, key_positions, qp, parts
+    )
+    q_mine, coded = lax.optimization_barrier((q_mine, coded))
     q_other = lax.ppermute(q_mine, "core", swap)
-
-    pieces = [
-        probs_chunk(c, latent_cache, query_flat, normalizers, key_positions, qp, parts) for c in range(chunks)
-    ]
-    recs = [lax.all_to_all(s, "head", 0, 0, tiled=True) for s, _ in pieces]
+    rec = lax.all_to_all(coded, "head", 0, 0, tiled=True)
 
     offset = lax.axis_index("head") * sub_keys
     own_kp = lax.dynamic_slice_in_dim(key_positions, offset, sub_keys, 0).reshape(1, sub_keys)
     e, local = logits_call(index_keys, q_mine, q_other, own_kp, qp, index_scale, half_rows)
-    target_total = sum(t for _, t in pieces)[0:1]
-    stats = jnp.concatenate([local[0:2], target_total, target_total], axis=0)
+    stats = jnp.concatenate([local[0:2], totals[0:2]], axis=0)
     all_stats = spread(stats, ("head", "zy", "core"), parts * zy * 2)
-    lg = lg_call(recs, e, local, all_stats, own_kp, qp)
+    lg = lg_call(rec, e, local, all_stats, own_kp, qp)
 
     keys_t = index_keys.T
     out_other, gk = grads_call(index_keys, keys_t, lg, q_other, None, index_scale, half_rows)
     got = lax.ppermute(out_other, "core", swap)
     out_mine, gk = grads_call(index_keys, keys_t, lg, q_mine, gk, index_scale, half_rows)
-    block = lax.all_to_all(out_mine + got, ("head", "zy"), 0, 0, tiled=True)
+    block = lax.all_to_all(code_call(out_mine, got, parts), ("head", "zy"), 0, 0, tiled=True)
     summed = sum_call(block, zy * 2)
     final = lax.all_to_all(summed, ("zy", "core"), 0, 0, tiled=True)
     gq, gw = place_call(final, local_heads, index_width)

time: 169 us -> 136 us (0.80)
  local copies, waits for them, and re-layouts: 22.4 us -> 4.42 us
  blocking collectives: 52.2 us -> 40.6 us
  starting transfers between devices: 27.3 us -> 22.6 us
  Pallas kernels: 40.9 us -> 45.2 us
  waiting for transfers between devices: 24.5 us -> 21.4 us
    unnamed x23 -> x7, local copies, waits for them, and re-layouts: 19.7 us -> 0.35 us
    all_to_all x1, blocking collectives: 36.2 us -> 24.3 us  [per_device(): lax.all_to_all(code_call(out_mine, got, parts), ('head', 'zy'), 0, 0, til...]
    pallas_call x3, Pallas kernels: 18 us -> 23.6 us  [the longest x1 21.7 us: probs_call(): pl.pallas_call(probs_kernel, grid=(parts,), in_specs=[pl.BlockSpec((width...]
    all_to_all x2 -> x1, starting transfers between devices: 11.2 us -> 6.93 us  [per_device(): rec = lax.all_to_all(coded, 'head', 0, 0, tiled=True)]
    all_to_all x2 -> x1, waiting for transfers between devices: 13.1 us -> 10.1 us  [per_device(): rec = lax.all_to_all(coded, 'head', 0, 0, tiled=True)]
  transfers between devices with their start and end apart: 6 -> 5, of which waited for: 3 -> 2; matrix products, arithmetic and copies ran while one was open for 7% -> 1% of each run, Pallas kernels for 19% -> 25%
where the time goes in v2:
time: 136 us; the launch traced here: 135 us
  Pallas kernels  45.2 us (33%)
  blocking collectives  40.6 us (30%)
  starting transfers between devices  22.6 us (17%)
  waiting for transfers between devices  21.4 us (16%)
  local copies, waits for them, and re-layouts  4.42 us (3%)
    all_to_all x1, blocking collectives, per_device(): lax.all_to_all(code_call(out_mine, got, parts), ('head', 'zy'), 0, 0, til...  24.3 us
    pallas_call x1, Pallas kernels, probs_call(): pl.pallas_call(probs_kernel, grid=(parts,), in_specs=[pl.BlockSpec((width...  21.7 us
    all_to_all x1, blocking collectives, per_device(): final = lax.all_to_all(summed, ('zy', 'core'), 0, 0, tiled=True)  16.3 us
    all_to_all x2, starting transfers between devices, spread(): lax.all_to_all(jnp.broadcast_to(x[None], (count,) + x.shape), axes, 0, 0,...  14.2 us
    pallas_call x2, Pallas kernels, grads_call(): pl.pallas_call(functools.partial(grads_kernel, scale, half_rows, first),...  13.6 us
    all_to_all x2, waiting for transfers between devices, spread(): lax.all_to_all(jnp.broadcast_to(x[None], (count,) + x.shape), axes, 0, 0,...  11.4 us
    all_to_all x1, waiting for transfers between devices, per_device(): rec = lax.all_to_all(coded, 'head', 0, 0, tiled=True)  10.1 us
    all_to_all x1, starting transfers between devices, per_device(): rec = lax.all_to_all(coded, 'head', 0, 0, tiled=True)  6.93 us
  transfers between devices with their start and end apart: 5, of which 2 were waited for; matrix products, arithmetic and copies ran while one was open for 1% of the time, Pallas kernels for 25%

profile of v2, /device:TPU:1, one launch (start us, length us, event | category | flops | bytes accessed | tf_op | source)
XLA Modules:
  0.0 135.0 jit_solution(15542129716835791289)
XLA Ops:
  0.6 0.0 copy-start
  0.7 0.7 constant_dynamic-slice_fusion
  1.4 0.2 copy-done
  1.6 1.1 broadcast_in_dim.4
  2.8 8.2 %all-to-all-start = ((bf16[8,528,128]{2,1,0:T(8,128)(2,1)}), bf16[8,528,128]{2,1,0:T(8,128)(2,1)S(1)}, u32[]{:S(2)}, u32[]{:S(2)}) async-start(bf16[8,528,128]{2,1,0:T(8,128)(2,1)} %broadcast_in_dim.4), calls=%async_computation | async-start | bytes 2162688 | tf_op jit(solution)/shard_map/all_to_all | solution.py:374
  10.9 21.7 %probs.1 = (s16[8,528,128]{2,1,0:T(8,128)(2,1)}, f32[8,128]{1,0:T(8,128)}) custom-call(bf16[576,4096]{1,0:T(8,128)(2,1)} %bitcast.16, bf16[16,576,128]{2,1,0:T(8,128)(2,1)} %bitcast.17, f32[16,128]{1,0:T(8,128)} %nrm.1, s32[8,1,512]{2,1,0:T(1,128)} %bitcast.15, s32[1,128]{1,0:T(1,128)} %bitcast.11), custom_call_target="tpu_custom_call" | custom-call | flops 9663676416 | bytes 7077888 | tf_op jit(solution)/shard_map/probs/pallas_call | solution.py:102
  32.6 0.0 copy-start.1
  32.7 0.0 copy-start.2
  32.7 0.0 all-to-all-done.qa.refs_3_
  32.7 1.0 collective-permute-start
  33.7 6.9 %all-to-all-start.1 = ((s16[8,528,128]{2,1,0:T(8,128)(2,1)}), s16[8,528,128]{2,1,0:T(8,128)(2,1)S(1)}, u32[]{:S(2)}, u32[]{:S(2)}) async-start(s16[8,528,128]{2,1,0:T(8,128)(2,1)} %get-tuple-element.16), calls=%async_computation.1 | async-start | bytes 2162688 | tf_op jit(solution)/shard_map/all_to_all | solution.py:414
  40.6 0.8 dynamic_slice.11
  41.4 0.7 slice.7
  42.1 0.0 collective-permute-done.qb.refs_3_
  42.1 0.0 copy-done.1
  42.1 0.0 copy-done.2
  42.1 6.2 %logits.1 = (f32[512,128]{1,0:T(8,128)S(1)}, f32[8,128]{1,0:T(8,128)S(1)}) custom-call(bf16[512,128]{1,0:T(8,128)(2,1)S(1)} %copy-done.1, bf16[8,528,128]{2,1,0:T(8,128)(2,1)S(1)} %all-to-all-done.qa.refs_3_, bf16[8,528,128]{2,1,0:T(8,128)(2,1)} %collective-permute-done.qb.refs_3_, s32[1,512]{1,0:T(1,128)S(1)} %bitcast.9, s32[1,128]{1,0:T(1,128)S(1)} %bitcast.12), custom_call_target="tpu_custom_call" | custom-call | flops 2147483648 | bytes 2162688 | tf_op jit(solution)/shard_map/logits/pallas_call | solution.py:171
  48.3 10.1 %all-to-all-done.1.rec = s16[8,528,128]{2,1,0:T(8,128)(2,1)S(1)} async-done(((s16[8,528,128]{2,1,0:T(8,128)(2,1)}), s16[8,528,128]{2,1,0:T(8,128)(2,1)S(1)}, u32[]{:S(2)}, u32[]{:S(2)}) %all-to-all-start.1) | async-done | bytes 1081376 | tf_op jit(solution)/shard_map/all_to_all | solution.py:414
  58.4 0.7 broadcast_in_dim.5
  59.1 6.0 %all-to-all-start.2 = ((f32[128,4,128]{2,1,0:T(4,128)}), f32[128,4,128]{2,1,0:T(4,128)S(1)}, u32[]{:S(2)}, u32[]{:S(2)}) async-start(f32[128,4,128]{2,1,0:T(4,128)} %broadcast_in_dim.5), calls=%async_computation.2 | async-start | bytes 524288 | tf_op jit(solution)/shard_map/all_to_all | solution.py:374
  65.1 0.1 copy.11
  65.2 11.3 %all-to-all-done.2.stats = f32[128,4,128]{2,1,0:T(4,128)S(1)} async-done(((f32[128,4,128]{2,1,0:T(4,128)}), f32[128,4,128]{2,1,0:T(4,128)S(1)}, u32[]{:S(2)}, u32[]{:S(2)}) %all-to-all-start.2) | async-done | bytes 262176 | tf_op jit(solution)/shard_map/all_to_all | solution.py:374
  76.6 0.8 logit_grad.1.refs_2_
  77.4 7.2 %grads.2 = (f32[64,72,128]{2,1,0:T(8,128)S(1)}, f32[512,128]{1,0:T(8,128)S(1)}) custom-call(bf16[512,128]{1,0:T(8,128)(2,1)S(1)} %copy-done.1, bf16[128,512]{1,0:T(8,128)(2,1)S(1)} %bitcast.7, f32[512,128]{1,0:T(8,128)S(1)} %logit_grad.1.refs_2_, bf16[8,528,128]{2,1,0:T(8,128)(2,1)} %collective-permute-done.qb.refs_3_), custom_call_target="tpu_custom_call" | custom-call | flops 1610612736 | bytes 3244032 | tf_op jit(solution)/shard_map/grads/pallas_call | solution.py:266
  84.6 0.5 collective-permute-start.1
  85.1 6.3 %grads.3 = (f32[64,72,128]{2,1,0:T(8,128)S(1)}, f32[512,128]{1,0:T(8,128)}) custom-call(bf16[512,128]{1,0:T(8,128)(2,1)S(1)} %copy-done.1, bf16[128,512]{1,0:T(8,128)(2,1)S(1)} %bitcast.8, f32[512,128]{1,0:T(8,128)S(1)} %logit_grad.1.refs_2_, bf16[8,528,128]{2,1,0:T(8,128)(2,1)S(1)} %all-to-all-done.qa.refs_3_, f32[512,128]{1,0:T(8,128)S(1)} %get-tuple-element.21.refs_4_), custom_call_target="tpu_custom_call" | custom-call | flops 1610612736 | bytes 3244032 | tf_op jit(solution)/shard_map/grads/pallas_call | solution.py:266
  91.5 0.0 collective-permute-done.1.b
  91.5 1.4 %code_parts.1 = s16[64,80,128]{2,1,0:T(8,128)(2,1)S(1)} custom-call(f32[64,72,128]{2,1,0:T(8,128)S(1)} %get-tuple-element.22.a, f32[64,72,128]{2,1,0:T(8,128)S(1)} %collective-permute-done.1.b), custom_call_target="tpu_custom_call" | custom-call | tf_op jit(solution)/shard_map/code_parts/pallas_call | solution.py:314
  92.9 24.3 %all_to_all.25.rec = s16[64,80,128]{2,1,0:T(8,128)(2,1)S(1)} all-to-all(s16[64,80,128]{2,1,0:T(8,128)(2,1)S(1)} %code_parts.1), channel_id=1, replica_groups=mesh['head'=8,'zy'=8,'core'=2] {'head','zy'}, dimensions={0} | all-to-all | bytes 2621440 | tf_op jit(solution)/shard_map/all_to_all | solution.py:427
  117.2 0.5 sum_parts.1
  117.7 16.3 %all_to_all.26.rec = f32[16,72,128]{2,1,0:T(8,128)S(1)} all-to-all(f32[16,72,128]{2,1,0:T(8,128)S(1)} %sum_parts.1), channel_id=1, replica_groups=mesh['head'=8,'zy'=8,'core'=2] {'zy','core'}, dimensions={0} | all-to-all | bytes 1179648 | tf_op jit(solution)/shard_map/all_to_all | solution.py:429
  134.0 1.0 place.1
  (4 shorter events, 0.0 us)
Async XLA Ops:
  0.6 1.0 copy-start
  2.8 29.9 %all-to-all-start = ((bf16[8,528,128]{2,1,0:T(8,128)(2,1)}), bf16[8,528,128]{2,1,0:T(8,128)(2,1)S(1)}, u32[]{:S(2)}, u32[]{:S(2)}) async-start(bf16[8,528,128]{2,1,0:T(8,128)(2,1)} %broadcast_in_dim.4), calls=%async_computation | async-start | bytes 2162688 | tf_op jit(solution)/shard_map/all_to_all | solution.py:374
  32.6 9.4 %copy-start.1 = (bf16[512,128]{1,0:T(8,128)(2,1)S(1)}, bf16[512,128]{1,0:T(8,128)(2,1)}, u32[]{:S(2)}) copy-start(bf16[512,128]{1,0:T(8,128)(2,1)} %refs_0_.3) | copy-start | bytes 393220
  32.7 9.4 %copy-start.2 = (s32[128]{0:T(128)S(1)}, s32[128]{0:T(128)}, u32[]{:S(2)}) copy-start(s32[128]{0:T(128)} %param.11) | copy-start | bytes 1540
  32.7 9.4 %collective-permute-start = (bf16[8,528,128]{2,1,0:T(8,128)(2,1)S(1)}, bf16[8,528,128]{2,1,0:T(8,128)(2,1)}, u32[]{:S(2)}, u32[]{:S(2)}) collective-permute-start(bf16[8,528,128]{2,1,0:T(8,128)(2,1)S(1)} %all-to-all-done.qa.refs_3_), channel_id=1, source_target_pairs={{0,1},{1,0},{2,3},{3,2},{4,5},{5,4},{6,7},{7,6},{8,9},{9,8},{10,11... | collective-permute-start | bytes 3244040 | tf_op jit(solution)/shard_map/ppermute | solution.py:413
  33.7 24.7 %all-to-all-start.1 = ((s16[8,528,128]{2,1,0:T(8,128)(2,1)}), s16[8,528,128]{2,1,0:T(8,128)(2,1)S(1)}, u32[]{:S(2)}, u32[]{:S(2)}) async-start(s16[8,528,128]{2,1,0:T(8,128)(2,1)} %get-tuple-element.16), calls=%async_computation.1 | async-start | bytes 2162688 | tf_op jit(solution)/shard_map/all_to_all | solution.py:414
  59.1 17.5 %all-to-all-start.2 = ((f32[128,4,128]{2,1,0:T(4,128)}), f32[128,4,128]{2,1,0:T(4,128)S(1)}, u32[]{:S(2)}, u32[]{:S(2)}) async-start(f32[128,4,128]{2,1,0:T(4,128)} %broadcast_in_dim.5), calls=%async_computation.2 | async-start | bytes 524288 | tf_op jit(solution)/shard_map/all_to_all | solution.py:374
  84.6 6.8 %collective-permute-start.1 = (f32[64,72,128]{2,1,0:T(8,128)S(1)}, f32[64,72,128]{2,1,0:T(8,128)S(1)}, u32[]{:S(2)}, u32[]{:S(2)}) collective-permute-start(f32[64,72,128]{2,1,0:T(8,128)S(1)} %get-tuple-element.23), channel_id=1, source_target_pairs={{0,1},{1,0},{2,3},{3,2},{4,5},{5,4},{6,7},{7,6},{8,9},{9,8},{10,11... | collective-permute-start | bytes 7077896 | tf_op jit(solution)/shard_map/ppermute | solution.py:425

commit v3 on v2

--- a/solution.py
+++ b/solution.py
@@ -67,27 +67,31 @@
     return r * r
 
 
-def probs_kernel(cache, q, nrm, kp, qp, out, tot, qt, nb):
+def probs_kernel(first, *refs):
+    if first:
+        cache, q, nrm, kp, qp, out, tot = refs
+    else:
+        cache, q, nrm, kp, qp, _, out, tot = refs
     keys = cache.shape[1]
     heads, queries = nrm.shape
 
     @pl.when(pl.program_id(0) == 0)
     def _():
         tot[...] = jnp.zeros(tot.shape, f32)
-        for h in range(heads):
-            qt[pl.ds(h * queries, queries), :] = jnp.transpose(q[h])
-            nb[h] = jnp.transpose(jnp.broadcast_to(nrm[pl.ds(h, 1), :] * log2e, (queries, queries)))
-
-    x = cache[...]
-    acc = [jnp.zeros((queries, queries), f32) for _ in range(keys // queries)]
-    for pair in range(heads // 2):
-        s = dot(qt[pl.ds(pair * 2 * queries, 2 * queries), :], x)
-        for u in range(2):
-            n = nb[pair * 2 + u]
-            for i in range(len(acc)):
-                block = s[u * queries : (u + 1) * queries, i * queries : (i + 1) * queries]
-                acc[i] += jnp.exp2(block * (att_scale * log2e) - n)
-    summed = jnp.concatenate([jnp.transpose(a) for a in acc], axis=0)
+
+    rows = keys // 2
+    sums = []
+    xt = jnp.transpose(cache[...])
+    for block in range(2):
+        x = xt[block * rows : (block + 1) * rows]
+        acc = jnp.zeros((rows, queries), f32)
+        for pair in range(heads // 2):
+            s = dot(x, jnp.concatenate([q[pair * 2], q[pair * 2 + 1]], axis=1))
+            for u in range(2):
+                n = nrm[pl.ds(pair * 2 + u, 1), :] * log2e
+                acc += jnp.exp2(s[:, u * queries : (u + 1) * queries] * (att_scale * log2e) - n)
+        sums.append(acc)
+    summed = jnp.concatenate(sums, axis=0)
     summed = jnp.where(visible_mask(kp[0], qp[...]), summed, 0.0)
     e = exponent(jnp.max(summed, axis=0, keepdims=True))
     out[0, pl.ds(0, keys), :] = root_code(summed, e)
@@ -95,65 +99,70 @@
     tot[...] += jnp.broadcast_to(jnp.sum(summed, axis=0, keepdims=True), tot.shape)
 
 
-def probs_call(cache_t, q_t, nrm, kp, qp, parts):
+def probs_call(cache_t, q_t, nrm, kp, qp, parts, start, count, before):
     width, keys = cache_t.shape
     rows = keys // parts
     heads, queries = nrm.shape
-    return pl.pallas_call(
-        probs_kernel,
-        grid=(parts,),
-        in_specs=[
-            pl.BlockSpec((width, rows), lambda d: (0, d)),
-            pl.BlockSpec(q_t.shape, lambda d: (0, 0, 0)),
-            pl.BlockSpec(nrm.shape, lambda d: (0, 0)),
-            pl.BlockSpec((1, 1, rows), lambda d: (d, 0, 0)),
-            pl.BlockSpec(qp.shape, lambda d: (0, 0)),
-        ],
+    first = before is None
+    args = [cache_t, q_t, nrm, kp.reshape(parts, 1, rows), qp] + ([] if first else [before])
+    specs = [
+        pl.BlockSpec((width, rows), lambda d: (0, d + start)),
+        pl.BlockSpec(q_t.shape, lambda d: (0, 0, 0)),
+        pl.BlockSpec(nrm.shape, lambda d: (0, 0)),
+        pl.BlockSpec((1, 1, rows), lambda d: (d + start, 0, 0)),
+        pl.BlockSpec(qp.shape, lambda d: (0, 0)),
+    ] + ([] if first else [pl.BlockSpec(memory_space=pl.ANY)])
+    return pl.pallas_call(
+        functools.partial(probs_kernel, first),
+        grid=(count,),
+        in_specs=specs,
         out_specs=[
-            pl.BlockSpec((1, rows + 16, queries), lambda d: (d, 0, 0)),
+            pl.BlockSpec((1, rows + 16, queries), lambda d: (d + start, 0, 0)),
             pl.BlockSpec((8, queries), lambda d: (0, 0)),
         ],
         out_shape=[
             jax.ShapeDtypeStruct((parts, rows + 16, queries), jnp.int16),
             jax.ShapeDtypeStruct((8, queries), f32),
         ],
-        scratch_shapes=[
-            pltpu.VMEM((heads * queries, width), bf16),
-            pltpu.VMEM((heads, queries, queries), f32),
-        ],
+        input_output_aliases={} if first else {5: 0},
         compiler_params=params(56),
         cost_estimate=pl.CostEstimate(
-            flops=2 * keys * q_t.size,
-            bytes_accessed=cache_t.size * 2 + q_t.size * 2,
-            transcendentals=keys * heads * queries,
+            flops=2 * rows * count * q_t.size,
+            bytes_accessed=cache_t.size * 2 * count // parts + q_t.size * 2,
+            transcendentals=rows * count * heads * queries,
         ),
         name="probs",
-    )(cache_t, q_t, nrm, kp.reshape(parts, 1, rows), qp)
-
-
-def logits_kernel(scale, half_rows, keys, qa, qb, kp, qp, e_out, stats, acc):
-    queries = qp.shape[1]
+    )(*args)
+
+
+def logits_kernel(scale, half_rows, first, *refs):
+    if first:
+        keys, q, acc = refs
+    else:
+        keys, q, before, kp, qp, e_out, stats, acc = refs
+    queries = acc.shape[1]
     step = pl.program_id(0)
 
     @pl.when(step == 0)
     def _():
-        acc[...] = jnp.zeros(acc.shape, f32)
+        acc[...] = jnp.zeros(acc.shape, f32) if first else before[...]
 
     k = keys[...]
     total = acc[...]
-    for q in (qa, qb):
-        for pair in range(half_rows // queries // 2):
-            s = dot(k, q[0, pl.ds(pair * 2 * queries, 2 * queries), :], NT)
-            w = q[0, pl.ds(half_rows, 16), :].astype(f32)
-            for u in range(2):
-                row = pair * 2 + u
-                total += jnp.maximum(s[:, u * queries : (u + 1) * queries], 0.0) * w[row : row + 1]
+    w = q[0, pl.ds(half_rows, 16), :].astype(f32)
+    for pair in range(half_rows // queries // 2):
+        s = dot(k, q[0, pl.ds(pair * 2 * queries, 2 * queries), :], NT)
+        for u in range(2):
+            row = pair * 2 + u
+            total += jnp.maximum(s[:, u * queries : (u + 1) * queries], 0.0) * w[row : row + 1]
     acc[...] = total
+    if first:
+        return
 
     @pl.when(step == pl.num_programs(0) - 1)
     def _():
         vis = visible_mask(kp[...], qp[...])
-        hidden = jnp.where(vis, total * scale, masked_floor)
+        hidden = jnp.where(vis, acc[...] * scale, masked_floor)
         m = jnp.max(hidden, axis=0, keepdims=True)
         e = jnp.where(vis, jnp.exp(hidden - m), 0.0)
         e_out[...] = e
@@ -162,33 +171,32 @@
         stats[...] = jnp.where(rows == 0, m, z)
 
 
-def logits_call(keys, qa, qb, kp, qp, scale, half_rows):
+def logits_call(keys, q, before, kp, qp, scale, half_rows):
     n, width = keys.shape
-    parts, rows, _ = qa.shape
+    parts, rows, _ = q.shape
     queries = qp.shape[1]
-    qspec = pl.BlockSpec((1, rows, width), lambda d: (d, 0, 0))
     full = lambda a: pl.BlockSpec(a.shape, lambda d: (0, 0))
-    return pl.pallas_call(
-        functools.partial(logits_kernel, scale, half_rows),
+    first = before is None
+    whole = pl.BlockSpec((n, queries), lambda d: (0, 0))
+    args = [keys, q] + ([] if first else [before, kp, qp])
+    specs = [full(keys), pl.BlockSpec((1, rows, width), lambda d: (d, 0, 0))]
+    specs += [] if first else [full(before), full(kp), full(qp)]
+    table = jax.ShapeDtypeStruct((n, queries), f32)
+    return pl.pallas_call(
+        functools.partial(logits_kernel, scale, half_rows, first),
         grid=(parts,),
-        in_specs=[full(keys), qspec, qspec, full(kp), full(qp)],
-        out_specs=[
-            pl.BlockSpec((n, queries), lambda d: (0, 0)),
-            pl.BlockSpec((8, queries), lambda d: (0, 0)),
-        ],
-        out_shape=[
-            jax.ShapeDtypeStruct((n, queries), f32),
-            jax.ShapeDtypeStruct((8, queries), f32),
-        ],
-        scratch_shapes=[pltpu.VMEM((n, queries), f32)],
+        in_specs=specs,
+        out_specs=whole if first else [whole, pl.BlockSpec((8, queries), lambda d: (0, 0))],
+        out_shape=table if first else [table, jax.ShapeDtypeStruct((8, queries), f32)],
+        scratch_shapes=[] if first else [pltpu.VMEM((n, queries), f32)],
         compiler_params=params(),
         cost_estimate=pl.CostEstimate(
-            flops=4 * 2 * n * parts * half_rows * width,
-            bytes_accessed=parts * rows * width * 4,
+            flops=2 * 2 * n * parts * half_rows * width,
+            bytes_accessed=parts * rows * width * 2,
             transcendentals=0,
         ),
         name="logits",
-    )(keys, qa, qb, kp, qp)
+    )(*args)
 
 
 def lg_kernel(rec, e, own, stats, kp, qp, lg):
@@ -197,10 +205,7 @@
     for i in range(rec.shape[0]):
         ex = from_code(rec[i, pl.ds(n, 16), :])[0:1]
         s += root_decode(rec[i, pl.ds(0, n), :], ex)
-    m_all, z_all, t_all = stats[:, 0, :], stats[:, 1, :], stats[:, 2, :]
-    top = jnp.max(m_all, axis=0, keepdims=True)
-    z = jnp.sum(z_all * jnp.exp(m_all - top), axis=0, keepdims=True)
-    t = jnp.sum(t_all, axis=0, keepdims=True)
+    top, z, t = stats[0:1, :], stats[1:2, :], stats[2:3, :]
     p = e[...] * jnp.exp(own[0:1, :] - top) / z
     target = s / t
     lg[...] = loss_scale * jnp.where(visible_mask(kp[...], qp[...]), p - target, 0.0)
@@ -346,32 +351,53 @@
     )(rec)
 
 
-def place_kernel(rec, gq, gw):
+def place_kernel(core, mine, other, gq, gw):
     heads, _, width = gq.shape
     half = width // 2
     for j in range(heads):
-        core, jj = j // (heads // 2), j % (heads // 2)
-        lo, hi = (jj * 2) * 2 + core, (jj * 2 + 1) * 2 + core
-        both = jnp.concatenate([rec[lo, pl.ds(0, half), :], rec[hi, pl.ds(0, half), :]], axis=0)
-        gq[j] = jnp.transpose(both)
-        gw[pl.ds(j, 1), :] = rec[lo, pl.ds(half, 1), :]
-
-
-def place_call(rec, heads, width):
-    queries = rec.shape[2]
+        side, jj = j // (heads // 2), j % (heads // 2)
+        own = core[0] == side
+        pick = lambda i: jnp.where(own, mine[i], other[i])
+        lo, hi = pick(2 * jj), pick(2 * jj + 1)
+        gq[j] = jnp.transpose(jnp.concatenate([lo[0:half], hi[0:half]], axis=0))
+        gw[pl.ds(j, 1), :] = lo[half : half + 1]
+
+
+def place_call(core, mine, other, heads, width):
+    queries = mine.shape[2]
+    vmem = pl.BlockSpec(memory_space=pltpu.VMEM)
     return pl.pallas_call(
         place_kernel,
+        in_specs=[pl.BlockSpec(memory_space=pltpu.SMEM), vmem, vmem],
+        out_specs=[vmem, vmem],
         out_shape=[
             jax.ShapeDtypeStruct((heads, queries, width), f32),
             jax.ShapeDtypeStruct((heads, queries), f32),
         ],
         compiler_params=params(),
         name="place",
-    )(rec)
+    )(core.reshape(1), mine, other)
+
+
+def merge(parts):
+    top = functools.reduce(jnp.maximum, [p[0:1] for p in parts])
+    z = sum(p[1:2] * jnp.exp(p[0:1] - top) for p in parts)
+    t = sum(p[2:3] for p in parts)
+    return jnp.concatenate([top, z, t, t], axis=0)
+
+
+def ring_merge(s, axes):
+    n = lax.axis_size(axes)
+    moved = [lax.ppermute(s, axes, [(i, (i + k) % n) for i in range(n)]) for k in range(1, n)]
+    return merge([s] + moved)
 
 
 def spread(x, axes, count):
     return lax.all_to_all(jnp.broadcast_to(x[None], (count,) + x.shape), axes, 0, 0, tiled=True)
+
+
+HEAD = ("zh", "x")
+ZY = ("zl", "y")
 
 
 def per_device(
@@ -386,8 +412,8 @@
 ):
     query_count = mla_queries.shape[1]
     sub_keys, index_width = index_keys.shape
-    parts = lax.axis_size("head")
-    zy = lax.axis_size("zy")
+    parts = lax.axis_size(HEAD)
+    zy = lax.axis_size(ZY)
     local_heads = index_queries.shape[0]
     half_heads = local_heads // 2
     half_rows = half_heads * query_count
@@ -405,51 +431,57 @@
         ],
         axis=0,
     )
-    q_mine = spread(own, "head", parts)
-    coded, totals = probs_call(
-        latent_cache.T, mla_queries.transpose(0, 2, 1), normalizers, key_positions, qp, parts
-    )
+    q_mine = spread(own, HEAD, parts)
+    cache_t = latent_cache.T
+    mla_t = mla_queries.transpose(0, 2, 1)
+    probs = functools.partial(probs_call, cache_t, mla_t, normalizers, key_positions, qp, parts)
+    coded, total_a = probs(0, parts // 2, None)
     q_mine, coded = lax.optimization_barrier((q_mine, coded))
     q_other = lax.ppermute(q_mine, "core", swap)
-    rec = lax.all_to_all(coded, "head", 0, 0, tiled=True)
-
-    offset = lax.axis_index("head") * sub_keys
+
+    offset = lax.axis_index(HEAD) * sub_keys
     own_kp = lax.dynamic_slice_in_dim(key_positions, offset, sub_keys, 0).reshape(1, sub_keys)
-    e, local = logits_call(index_keys, q_mine, q_other, own_kp, qp, index_scale, half_rows)
-    stats = jnp.concatenate([local[0:2], totals[0:2]], axis=0)
-    all_stats = spread(stats, ("head", "zy", "core"), parts * zy * 2)
-    lg = lg_call(rec, e, local, all_stats, own_kp, qp)
+    acc = logits_call(index_keys, q_mine, None, own_kp, qp, index_scale, half_rows)
+    e, local = logits_call(index_keys, q_other, acc, own_kp, qp, index_scale, half_rows)
+    coded, e = lax.optimization_barrier((coded, e))
+    coded, total_b = probs(parts // 2, parts // 2, coded)
+
+    stats = jnp.concatenate([local[0:2], (total_a + total_b)[0:2]], axis=0)
+    stats = ring_merge(stats, "core")
+    stats, coded = lax.optimization_barrier((stats, coded))
+    rec = lax.all_to_all(coded, HEAD, 0, 0, tiled=True)
+    for axes in ("y", ("zh", "zl"), "x"):
+        stats = ring_merge(stats, axes)
+    lg = lg_call(rec, e, local, stats, own_kp, qp)
 
     keys_t = index_keys.T
     out_other, gk = grads_call(index_keys, keys_t, lg, q_other, None, index_scale, half_rows)
     got = lax.ppermute(out_other, "core", swap)
     out_mine, gk = grads_call(index_keys, keys_t, lg, q_mine, gk, index_scale, half_rows)
-    block = lax.all_to_all(code_call(out_mine, got, parts), ("head", "zy"), 0, 0, tiled=True)
-    summed = sum_call(block, zy * 2)
-    final = lax.all_to_all(summed, ("zy", "core"), 0, 0, tiled=True)
-    gq, gw = place_call(final, local_heads, index_width)
+    block = lax.all_to_all(code_call(out_mine, got, parts), HEAD + ZY, 0, 0, tiled=True)
+    mine = lax.all_to_all(sum_call(block, zy), ZY, 0, 0, tiled=True)
+    other = lax.ppermute(mine, "core", swap)
+    gq, gw = place_call(core, mine, other, local_heads, index_width)
     return gq, gw, gk
 
 
 def solution(mesh):
-    heads = mesh.shape["head"]
-    ctx = mesh.shape["ctx"]
-    fine = Mesh(mesh.devices.reshape(heads, ctx // 2, 2), ("head", "zy", "core"))
-    split = ("zy", "core")
+    fine = Mesh(mesh.devices.reshape(2, 4, 2, 4, 2), HEAD + ZY + ("core",))
+    ctx = ZY + ("core",)
     placed = (
-        P("head", None, None),
-        P(split, None),
-        P("head", None),
+        P(HEAD, None, None),
+        P(ctx, None),
+        P(HEAD, None),
         P(),
-        P(split),
-        P("head", None, None),
-        P(split + ("head",), None),
-        P("head", None),
+        P(ctx),
+        P(HEAD, None, None),
+        P(ctx + HEAD, None),
+        P(HEAD, None),
     )
     return jax.shard_map(
         per_device,
         mesh=fine,
         in_specs=placed,
-        out_specs=(P("head", None, None), P("head", None), P(split + ("head",), None)),
+        out_specs=(P(HEAD, None, None), P(HEAD, None), P(ctx + HEAD, None)),
         check_vma=False,
     )

time: 136 us -> 138 us (1.015)
  starting transfers between devices: 22.6 us -> 36.9 us
  waiting for transfers between devices: 21.4 us -> 15.3 us
  blocking collectives: 40.6 us -> 36.4 us
  Pallas kernels: 45.2 us -> 43.3 us
    ppermute x0 -> x11, starting transfers between devices: none -> 22.3 us  [the longest x10 19.6 us: ring_merge(): lax.ppermute(s, axes, [(i, (i + k) % n) for i in range(n)])]
    all_to_all x1, waiting for transfers between devices: 10.1 us -> 0.01 us  [per_device(): rec = lax.all_to_all(coded, HEAD, 0, 0, tiled=True)]
    ppermute x0 -> x11, waiting for transfers between devices: none -> 8.83 us  [the longest x10 7.62 us: ring_merge(): lax.ppermute(s, axes, [(i, (i + k) % n) for i in range(n)])]
    all_to_all x2 -> x1, starting transfers between devices: 14.2 us -> 8.16 us  [spread(): lax.all_to_all(jnp.broadcast_to(x[None], (count,) + x.shape), axes, 0, 0,...]
    all_to_all x2 -> x1, waiting for transfers between devices: 11.4 us -> 6.44 us  [spread(): lax.all_to_all(jnp.broadcast_to(x[None], (count,) + x.shape), axes, 0, 0,...]
    all_to_all x2, blocking collectives: 40.6 us -> 36.4 us  [the longest x1 26.4 us: per_device(): lax.all_to_all(code_call(out_mine, got, parts), HEAD + ZY, 0, 0, tiled=True)]
    all_to_all x1, starting transfers between devices: 6.93 us -> 3.56 us  [per_device(): rec = lax.all_to_all(coded, HEAD, 0, 0, tiled=True)]
    ppermute x1, starting transfers between devices: 0.48 us -> 2.05 us  [per_device(): got = lax.ppermute(out_other, 'core', swap)]
  transfers between devices with their start and end apart: 5 -> 15, of which waited for: 2 -> 6; matrix products, arithmetic and copies ran while one was open for 1% -> 1% of each run, Pallas kernels for 25% -> 15%
where the time goes in v3:
time: 138 us; the launch traced here: 137 us
  Pallas kernels  43.3 us (31%)
  starting transfers between devices  36.9 us (27%)
  blocking collectives  36.4 us (26%)
  waiting for transfers between devices  15.3 us (11%)
  local copies, waits for them, and re-layouts  3.61 us (3%)
    all_to_all x1, blocking collectives, per_device(): lax.all_to_all(code_call(out_mine, got, parts), HEAD + ZY, 0, 0, tiled=True)  26.4 us
    pallas_call x2, Pallas kernels, probs_call(): pl.pallas_call(functools.partial(probs_kernel, first), grid=(count,), in_...  22.4 us
    ppermute x10, starting transfers between devices, ring_merge(): lax.ppermute(s, axes, [(i, (i + k) % n) for i in range(n)])  19.6 us
    pallas_call x2, Pallas kernels, grads_call(): pl.pallas_call(functools.partial(grads_kernel, scale, half_rows, first),...  12 us
    all_to_all x1, blocking collectives, per_device(): mine = lax.all_to_all(sum_call(block, zy), ZY, 0, 0, tiled=True)  9.98 us
    all_to_all x1, starting transfers between devices, spread(): lax.all_to_all(jnp.broadcast_to(x[None], (count,) + x.shape), axes, 0, 0,...  8.16 us
    ppermute x10, waiting for transfers between devices, ring_merge(): lax.ppermute(s, axes, [(i, (i + k) % n) for i in range(n)])  7.62 us
    all_to_all x1, waiting for transfers between devices, spread(): lax.all_to_all(jnp.broadcast_to(x[None], (count,) + x.shape), axes, 0, 0,...  6.44 us
  transfers between devices with their start and end apart: 15, of which 6 were waited for; matrix products, arithmetic and copies ran while one was open for 1% of the time, Pallas kernels for 15%

profile of v3, /device:TPU:1, one launch (start us, length us, event | category | flops | bytes accessed | tf_op | source)
XLA Modules:
  0.0 137.1 jit_solution(431068882796736412)
XLA Ops:
  0.6 0.0 copy-start
  0.7 0.7 constant_dynamic-slice_fusion
  1.4 0.2 copy-done
  1.6 1.1 broadcast_in_dim.2
  2.8 8.2 %all-to-all-start = ((bf16[8,528,128]{2,1,0:T(8,128)(2,1)}), bf16[8,528,128]{2,1,0:T(8,128)(2,1)S(1)}, u32[]{:S(2)}, u32[]{:S(2)}) async-start(bf16[8,528,128]{2,1,0:T(8,128)(2,1)} %broadcast_in_dim.2), calls=%async_computation | async-start | bytes 2162688 | tf_op jit(solution)/shard_map/all_to_all | solution.py:396
  10.9 11.2 %probs.2 = (s16[8,528,128]{2,1,0:T(8,128)(2,1)}, f32[8,128]{1,0:T(8,128)}) custom-call(bf16[576,4096]{1,0:T(8,128)(2,1)} %bitcast.19, bf16[16,576,128]{2,1,0:T(8,128)(2,1)} %bitcast.21, f32[16,128]{1,0:T(8,128)} %refs_2_.3, s32[8,1,512]{2,1,0:T(1,128)} %bitcast.17, s32[1,128]{1,0:T(1,128)} %bitcast.12), custom_call_target="tpu_custom_call" | custom-call | flops 4831838208 | bytes 4718592 | tf_op jit(solution)/shard_map/probs/pallas_call | solution.py:115
  22.2 6.4 %all-to-all-done.refs_1_.refs_3_ = bf16[8,528,128]{2,1,0:T(8,128)(2,1)S(1)} async-done(((bf16[8,528,128]{2,1,0:T(8,128)(2,1)}), bf16[8,528,128]{2,1,0:T(8,128)(2,1)S(1)}, u32[]{:S(2)}, u32[]{:S(2)}) %all-to-all-start) | async-done | bytes 1081376 | tf_op jit(solution)/shard_map/all_to_all | solution.py:396
  28.6 0.8 collective-permute-start
  29.4 0.8 dynamic_slice.11
  30.2 2.5 %logits.2.refs_2_ = f32[512,128]{1,0:T(8,128)S(1)} custom-call(bf16[512,128]{1,0:T(8,128)(2,1)S(1)} %copy-done.1, bf16[8,528,128]{2,1,0:T(8,128)(2,1)S(1)} %all-to-all-done.refs_1_.refs_3_), custom_call_target="tpu_custom_call" | custom-call | flops 1073741824 | bytes 1081344 | tf_op jit(solution)/shard_map/logits/pallas_call | solution.py:185
  32.7 0.0 collective-permute-done.refs_1_.refs_3_
  32.8 2.8 %logits.3 = (f32[512,128]{1,0:T(8,128)S(1)}, f32[8,128]{1,0:T(8,128)S(1)}) custom-call(bf16[512,128]{1,0:T(8,128)(2,1)S(1)} %copy-done.1, bf16[8,528,128]{2,1,0:T(8,128)(2,1)S(1)} %collective-permute-done.refs_1_.refs_3_, f32[512,128]{1,0:T(8,128)S(1)} %logits.2.refs_2_, s32[1,512]{1,0:T(1,128)S(1)} %bitcast.10, s32[1,128]{1,0:T(1,128)S(1)} %bitcast.14), custom_call_target="tpu_custom_call" | custom-call | flops 1073741824 | bytes 1081344 | tf_op jit(solution)/shard_map/logits/pallas_call | solution.py:185
  35.6 0.0 copy-start.6
  35.6 11.2 %probs.3 = (s16[8,528,128]{2,1,0:T(8,128)(2,1)}, f32[8,128]{1,0:T(8,128)}) custom-call(bf16[576,4096]{1,0:T(8,128)(2,1)} %bitcast.20, bf16[16,576,128]{2,1,0:T(8,128)(2,1)} %bitcast.22, f32[16,128]{1,0:T(8,128)} %refs_2_.3, s32[8,1,512]{2,1,0:T(1,128)} %bitcast.18, s32[1,128]{1,0:T(1,128)} %bitcast.13, ...), custom_call_target="tpu_custom_call", output_to_operand_aliasing={{0}: (5, {})} | custom-call | flops 4831838208 | bytes 4718592 | tf_op jit(solution)/shard_map/probs/pallas_call | solution.py:115
  46.8 0.7 add.78
  47.5 0.1 collective-permute-start.1
  47.6 1.1 collective-permute-done.1
  48.7 2.8 %collective-permute-start.4 = (f32[4,128]{1,0:T(4,128)S(1)}, f32[4,128]{1,0:T(4,128)S(1)}, u32[]{:S(2)}, u32[]{:S(2)}) collective-permute-start(f32[4,128]{1,0:T(4,128)S(1)} %pad_maximum_fusion.1), channel_id=1, source_target_pairs={{0,6},{2,0},{4,2},{6,4},{1,7},{3,1},{5,3},{7,5},{8,14},{10,8},{12,... | collective-permute-start | bytes 6152 | tf_op jit(solution)/shard_map/ppermute | solution.py:391
  51.5 0.3 collective-permute-start.3
  51.9 0.7 collective-permute-start.2
  52.6 3.6 %all-to-all-start.1 = ((s16[8,528,128]{2,1,0:T(8,128)(2,1)}), s16[8,528,128]{2,1,0:T(8,128)(2,1)S(1)}, u32[]{:S(2)}, u32[]{:S(2)}) async-start(s16[8,528,128]{2,1,0:T(8,128)(2,1)} %get-tuple-element.30), calls=%async_computation.1 | async-start | bytes 2162688 | tf_op jit(solution)/shard_map/all_to_all | solution.py:452
  56.2 0.0 collective-permute-done.4
  56.2 0.0 collective-permute-done.3
  56.2 0.0 collective-permute-done.2
  56.2 3.1 %collective-permute-start.7 = (f32[4,128]{1,0:T(4,128)S(1)}, f32[4,128]{1,0:T(4,128)S(1)}, u32[]{:S(2)}, u32[]{:S(2)}) collective-permute-start(f32[4,128]{1,0:T(4,128)S(1)} %pad_maximum_fusion.2), channel_id=1, source_target_pairs={{0,72},{8,0},{64,8},{72,64},{1,73},{9,1},{65,9},{73,65},{2,74},{10... | collective-permute-start | bytes 6152 | tf_op jit(solution)/shard_map/ppermute | solution.py:391
  59.3 0.7 collective-permute-start.5
  60.0 0.0 collective-permute-done.7
  60.1 3.7 %collective-permute-done.6 = f32[4,128]{1,0:T(4,128)S(1)} collective-permute-done((f32[4,128]{1,0:T(4,128)S(1)}, f32[4,128]{1,0:T(4,128)S(1)}, u32[]{:S(2)}, u32[]{:S(2)}) %collective-permute-start.6) | collective-permute-done | bytes 2080 | tf_op jit(solution)/shard_map/ppermute | solution.py:391
  63.8 10.7 %collective-permute-start.10 = (f32[4,128]{1,0:T(4,128)S(1)}, f32[4,128]{1,0:T(4,128)S(1)}, u32[]{:S(2)}, u32[]{:S(2)}) collective-permute-start(f32[4,128]{1,0:T(4,128)S(1)} %pad_maximum_fusion.3), channel_id=1, source_target_pairs={{0,48},{16,0},{32,16},{48,32},{1,49},{17,1},{33,17},{49,33},{2,50}... | collective-permute-start | bytes 6152 | tf_op jit(solution)/shard_map/ppermute | solution.py:391
  74.5 0.4 collective-permute-start.9
  74.9 0.8 collective-permute-start.8
  75.7 0.1 copy.12
  75.8 2.7 %collective-permute-done.9 = f32[4,128]{1,0:T(4,128)S(1)} collective-permute-done((f32[4,128]{1,0:T(4,128)S(1)}, f32[4,128]{1,0:T(4,128)S(1)}, u32[]{:S(2)}, u32[]{:S(2)}) %collective-permute-start.9) | collective-permute-done | bytes 2080 | tf_op jit(solution)/shard_map/ppermute | solution.py:391
  78.5 0.1 collective-permute-done.8
  78.6 0.0 all-to-all-done.1.rec
  78.6 0.6 logit_grad.1.refs_2_
  79.2 0.6 copy-done.5
  79.9 5.7 %grads.2 = (f32[64,72,128]{2,1,0:T(8,128)S(1)}, f32[512,128]{1,0:T(8,128)S(1)}) custom-call(bf16[512,128]{1,0:T(8,128)(2,1)S(1)} %copy-done.1, bf16[128,512]{1,0:T(8,128)(2,1)S(1)} %bitcast.8, f32[512,128]{1,0:T(8,128)S(1)} %logit_grad.1.refs_2_, bf16[8,528,128]{2,1,0:T(8,128)(2,1)S(1)} %copy-done.5), custom_call_target="tpu_custom_call" | custom-call | flops 1610612736 | bytes 3244032 | tf_op jit(solution)/shard_map/grads/pallas_call | solution.py:271
  85.5 2.0 %collective-permute-start.11 = (f32[64,72,128]{2,1,0:T(8,128)S(1)}, f32[64,72,128]{2,1,0:T(8,128)S(1)}, u32[]{:S(2)}, u32[]{:S(2)}) collective-permute-start(f32[64,72,128]{2,1,0:T(8,128)S(1)} %get-tuple-element.35), channel_id=1, source_target_pairs={{0,1},{1,0},{2,3},{3,2},{4,5},{5,4},{6,7},{7,6},{8,9},{9,8},{10,11... | collective-permute-start | bytes 7077896 | tf_op jit(solution)/shard_map/ppermute | solution.py:459
  87.6 6.3 %grads.3 = (f32[64,72,128]{2,1,0:T(8,128)S(1)}, f32[512,128]{1,0:T(8,128)}) custom-call(bf16[512,128]{1,0:T(8,128)(2,1)S(1)} %copy-done.1, bf16[128,512]{1,0:T(8,128)(2,1)S(1)} %bitcast.9, f32[512,128]{1,0:T(8,128)S(1)} %logit_grad.1.refs_2_, bf16[8,528,128]{2,1,0:T(8,128)(2,1)S(1)} %all-to-all-done.refs_1_.refs_3_, f32[512,128]{1,0:T(8,128)S(1)} %get-tuple-element.33.refs_4_), custom_call_target="tpu_custom_call" | custom-call | flops 1610612736 | bytes 3244032 | tf_op jit(solution)/shard_map/grads/pallas_call | solution.py:271
  93.9 0.0 collective-permute-done.11.b
  93.9 1.4 %code_parts.1 = s16[64,80,128]{2,1,0:T(8,128)(2,1)S(1)} custom-call(f32[64,72,128]{2,1,0:T(8,128)S(1)} %get-tuple-element.34.a, f32[64,72,128]{2,1,0:T(8,128)S(1)} %collective-permute-done.11.b), custom_call_target="tpu_custom_call" | custom-call | tf_op jit(solution)/shard_map/code_parts/pallas_call | solution.py:319
  95.3 26.4 %all_to_all.20.rec = s16[64,80,128]{2,1,0:T(8,128)(2,1)S(1)} all-to-all(s16[64,80,128]{2,1,0:T(8,128)(2,1)S(1)} %code_parts.1), channel_id=1, replica_groups=mesh['zh'=2,'x'=4,'zl'=2,'y'=4,'core'=2] {'zh','x','zl','y'}, dimensions={0} | all-to-all | bytes 2621440 | tf_op jit(solution)/shard_map/all_to_all | solution.py:461
  121.7 0.5 sum_parts.1
  122.2 10.0 %all_to_all.21.mine = f32[8,72,128]{2,1,0:T(8,128)S(1)} all-to-all(f32[8,72,128]{2,1,0:T(8,128)S(1)} %sum_parts.1), channel_id=1, replica_groups=mesh['zh'=2,'x'=4,'zl'=2,'y'=4,'core'=2] {'zl','y'}, dimensions={0} | all-to-all | bytes 589824 | tf_op jit(solution)/shard_map/all_to_all | solution.py:462
  132.2 2.7 %collective-permute-start.12 = (f32[8,72,128]{2,1,0:T(8,128)S(1)}, f32[8,72,128]{2,1,0:T(8,128)S(1)}, u32[]{:S(2)}, u32[]{:S(2)}) collective-permute-start(f32[8,72,128]{2,1,0:T(8,128)S(1)} %all_to_all.21.mine), channel_id=1, source_target_pairs={{0,1},{1,0},{2,3},{3,2},{4,5},{5,4},{6,7},{7,6},{8,9},{9,8},{10,11... | collective-permute-start | bytes 884744 | tf_op jit(solution)/shard_map/ppermute | solution.py:463
  134.9 1.2 collective-permute-done.12.other
  136.1 1.0 place.1
  (26 shorter events, 0.2 us)
Async XLA Ops:
  0.6 1.0 copy-start
  2.8 25.8 %all-to-all-start = ((bf16[8,528,128]{2,1,0:T(8,128)(2,1)}), bf16[8,528,128]{2,1,0:T(8,128)(2,1)S(1)}, u32[]{:S(2)}, u32[]{:S(2)}) async-start(bf16[8,528,128]{2,1,0:T(8,128)(2,1)} %broadcast_in_dim.2), calls=%async_computation | async-start | bytes 2162688 | tf_op jit(solution)/shard_map/all_to_all | solution.py:396
  10.9 19.3 %copy-start.1 = (bf16[512,128]{1,0:T(8,128)(2,1)S(1)}, bf16[512,128]{1,0:T(8,128)(2,1)}, u32[]{:S(2)}) copy-start(bf16[512,128]{1,0:T(8,128)(2,1)} %refs_0_.7) | copy-start | bytes 393220
  28.6 4.1 %collective-permute-start = (bf16[8,528,128]{2,1,0:T(8,128)(2,1)S(1)}, bf16[8,528,128]{2,1,0:T(8,128)(2,1)S(1)}, u32[]{:S(2)}, u32[]{:S(2)}) collective-permute-start(bf16[8,528,128]{2,1,0:T(8,128)(2,1)S(1)} %all-to-all-done.refs_1_.refs_3_), channel_id=1, source_target_pairs={{0,1},{1,0},{2,3},{3,2},{4,5},{5,4},{6,7},{7,6},{8,9},{9,8},{10,11... | collective-permute-start | bytes 3244040 | tf_op jit(solution)/shard_map/ppermute | solution.py:440
  30.2 2.5 %copy-start.2 = (s32[128]{0:T(128)S(1)}, s32[128]{0:T(128)}, u32[]{:S(2)}) copy-start(s32[128]{0:T(128)} %param.11) | copy-start | bytes 1540
  32.7 2.8 %copy-start.4 = (bf16[8,528,128]{2,1,0:T(8,128)(2,1)}, bf16[8,528,128]{2,1,0:T(8,128)(2,1)S(1)}, u32[]{:S(2)}) copy-start(bf16[8,528,128]{2,1,0:T(8,128)(2,1)S(1)} %collective-permute-done.refs_1_.refs_3_) | copy-start | bytes 3244036
  35.6 11.2 %copy-start.6 = (f32[8,128]{1,0:T(8,128)S(1)}, f32[8,128]{1,0:T(8,128)}, u32[]{:S(2)}) copy-start(f32[8,128]{1,0:T(8,128)} %get-tuple-element.24) | copy-start | bytes 12292
  46.8 31.8 %copy-start.3 = (s32[128]{0:T(128)S(1)}, s32[128]{0:T(128)}, u32[]{:S(2)}) copy-start(s32[128]{0:T(128)} %param.11) | copy-start | bytes 1540
  47.5 1.2 collective-permute-start.1
  48.7 7.4 %collective-permute-start.4 = (f32[4,128]{1,0:T(4,128)S(1)}, f32[4,128]{1,0:T(4,128)S(1)}, u32[]{:S(2)}, u32[]{:S(2)}) collective-permute-start(f32[4,128]{1,0:T(4,128)S(1)} %pad_maximum_fusion.1), channel_id=1, source_target_pairs={{0,6},{2,0},{4,2},{6,4},{1,7},{3,1},{5,3},{7,5},{8,14},{10,8},{12,... | collective-permute-start | bytes 6152 | tf_op jit(solution)/shard_map/ppermute | solution.py:391
  51.5 4.6 %collective-permute-start.3 = (f32[4,128]{1,0:T(4,128)S(1)}, f32[4,128]{1,0:T(4,128)S(1)}, u32[]{:S(2)}, u32[]{:S(2)}) collective-permute-start(f32[4,128]{1,0:T(4,128)S(1)} %pad_maximum_fusion.1), channel_id=1, source_target_pairs={{0,4},{2,6},{4,0},{6,2},{1,5},{3,7},{5,1},{7,3},{8,12},{10,14},{12... | collective-permute-start | bytes 6152 | tf_op jit(solution)/shard_map/ppermute | solution.py:391
  51.9 4.3 %collective-permute-start.2 = (f32[4,128]{1,0:T(4,128)S(1)}, f32[4,128]{1,0:T(4,128)S(1)}, u32[]{:S(2)}, u32[]{:S(2)}) collective-permute-start(f32[4,128]{1,0:T(4,128)S(1)} %pad_maximum_fusion.1), channel_id=1, source_target_pairs={{0,2},{2,4},{4,6},{6,0},{1,3},{3,5},{5,7},{7,1},{8,10},{10,12},{12... | collective-permute-start | bytes 6152 | tf_op jit(solution)/shard_map/ppermute | solution.py:391
  52.6 26.0 %all-to-all-start.1 = ((s16[8,528,128]{2,1,0:T(8,128)(2,1)}), s16[8,528,128]{2,1,0:T(8,128)(2,1)S(1)}, u32[]{:S(2)}, u32[]{:S(2)}) async-start(s16[8,528,128]{2,1,0:T(8,128)(2,1)} %get-tuple-element.30), calls=%async_computation.1 | async-start | bytes 2162688 | tf_op jit(solution)/shard_map/all_to_all | solution.py:452
  56.2 3.8 %collective-permute-start.7 = (f32[4,128]{1,0:T(4,128)S(1)}, f32[4,128]{1,0:T(4,128)S(1)}, u32[]{:S(2)}, u32[]{:S(2)}) collective-permute-start(f32[4,128]{1,0:T(4,128)S(1)} %pad_maximum_fusion.2), channel_id=1, source_target_pairs={{0,72},{8,0},{64,8},{72,64},{1,73},{9,1},{65,9},{73,65},{2,74},{10... | collective-permute-start | bytes 6152 | tf_op jit(solution)/shard_map/ppermute | solution.py:391
  59.3 4.4 %collective-permute-start.6 = (f32[4,128]{1,0:T(4,128)S(1)}, f32[4,128]{1,0:T(4,128)S(1)}, u32[]{:S(2)}, u32[]{:S(2)}) collective-permute-start(f32[4,128]{1,0:T(4,128)S(1)} %pad_maximum_fusion.2), channel_id=1, source_target_pairs={{0,64},{8,72},{64,0},{72,8},{1,65},{9,73},{65,1},{73,9},{2,66},{10... | collective-permute-start | bytes 6152 | tf_op jit(solution)/shard_map/ppermute | solution.py:391
  59.3 4.4 %collective-permute-start.5 = (f32[4,128]{1,0:T(4,128)S(1)}, f32[4,128]{1,0:T(4,128)S(1)}, u32[]{:S(2)}, u32[]{:S(2)}) collective-permute-start(f32[4,128]{1,0:T(4,128)S(1)} %pad_maximum_fusion.2), channel_id=1, source_target_pairs={{0,8},{8,64},{64,72},{72,0},{1,9},{9,65},{65,73},{73,1},{2,10},{10... | collective-permute-start | bytes 6152 | tf_op jit(solution)/shard_map/ppermute | solution.py:391
  63.8 12.0 %collective-permute-start.10 = (f32[4,128]{1,0:T(4,128)S(1)}, f32[4,128]{1,0:T(4,128)S(1)}, u32[]{:S(2)}, u32[]{:S(2)}) collective-permute-start(f32[4,128]{1,0:T(4,128)S(1)} %pad_maximum_fusion.3), channel_id=1, source_target_pairs={{0,48},{16,0},{32,16},{48,32},{1,49},{17,1},{33,17},{49,33},{2,50}... | collective-permute-start | bytes 6152 | tf_op jit(solution)/shard_map/ppermute | solution.py:391
  74.5 3.9 %collective-permute-start.9 = (f32[4,128]{1,0:T(4,128)S(1)}, f32[4,128]{1,0:T(4,128)S(1)}, u32[]{:S(2)}, u32[]{:S(2)}) collective-permute-start(f32[4,128]{1,0:T(4,128)S(1)} %pad_maximum_fusion.3), channel_id=1, source_target_pairs={{0,32},{16,48},{32,0},{48,16},{1,33},{17,49},{33,1},{49,17},{2,34}... | collective-permute-start | bytes 6152 | tf_op jit(solution)/shard_map/ppermute | solution.py:391
  74.9 3.6 %collective-permute-start.8 = (f32[4,128]{1,0:T(4,128)S(1)}, f32[4,128]{1,0:T(4,128)S(1)}, u32[]{:S(2)}, u32[]{:S(2)}) collective-permute-start(f32[4,128]{1,0:T(4,128)S(1)} %pad_maximum_fusion.3), channel_id=1, source_target_pairs={{0,16},{16,32},{32,48},{48,0},{1,17},{17,33},{33,49},{49,1},{2,18}... | collective-permute-start | bytes 6152 | tf_op jit(solution)/shard_map/ppermute | solution.py:391
  78.6 1.2 copy-start.5
  85.5 8.4 %collective-permute-start.11 = (f32[64,72,128]{2,1,0:T(8,128)S(1)}, f32[64,72,128]{2,1,0:T(8,128)S(1)}, u32[]{:S(2)}, u32[]{:S(2)}) collective-permute-start(f32[64,72,128]{2,1,0:T(8,128)S(1)} %get-tuple-element.35), channel_id=1, source_target_pairs={{0,1},{1,0},{2,3},{3,2},{4,5},{5,4},{6,7},{7,6},{8,9},{9,8},{10,11... | collective-permute-start | bytes 7077896 | tf_op jit(solution)/shard_map/ppermute | solution.py:459
  132.2 3.9 %collective-permute-start.12 = (f32[8,72,128]{2,1,0:T(8,128)S(1)}, f32[8,72,128]{2,1,0:T(8,128)S(1)}, u32[]{:S(2)}, u32[]{:S(2)}) collective-permute-start(f32[8,72,128]{2,1,0:T(8,128)S(1)} %all_to_all.21.mine), channel_id=1, source_target_pairs={{0,1},{1,0},{2,3},{3,2},{4,5},{5,4},{6,7},{7,6},{8,9},{9,8},{10,11... | collective-permute-start | bytes 884744 | tf_op jit(solution)/shard_map/ppermute | solution.py:463

commit v4 on v3

--- a/solution.py
+++ b/solution.py
@@ -13,6 +13,7 @@
 loss_scale = 1024.0
 masked_floor = -1e30
 log2e = math.log2(math.e)
+per_step = 4
 
 NT = (((1,), (1,)), ((), ()))
 NN = (((1,), (0,)), ((), ()))
@@ -67,11 +68,7 @@
     return r * r
 
 
-def probs_kernel(first, *refs):
-    if first:
-        cache, q, nrm, kp, qp, out, tot = refs
-    else:
-        cache, q, nrm, kp, qp, _, out, tot = refs
+def probs_kernel(cache, q, nrm, kp, qp, out, tot):
     keys = cache.shape[1]
     heads, queries = nrm.shape
 
@@ -99,47 +96,43 @@
     tot[...] += jnp.broadcast_to(jnp.sum(summed, axis=0, keepdims=True), tot.shape)
 
 
-def probs_call(cache_t, q_t, nrm, kp, qp, parts, start, count, before):
+def probs_call(cache_t, q_t, nrm, kp, qp, parts):
     width, keys = cache_t.shape
     rows = keys // parts
     heads, queries = nrm.shape
-    first = before is None
-    args = [cache_t, q_t, nrm, kp.reshape(parts, 1, rows), qp] + ([] if first else [before])
-    specs = [
-        pl.BlockSpec((width, rows), lambda d: (0, d + start)),
-        pl.BlockSpec(q_t.shape, lambda d: (0, 0, 0)),
-        pl.BlockSpec(nrm.shape, lambda d: (0, 0)),
-        pl.BlockSpec((1, 1, rows), lambda d: (d + start, 0, 0)),
-        pl.BlockSpec(qp.shape, lambda d: (0, 0)),
-    ] + ([] if first else [pl.BlockSpec(memory_space=pl.ANY)])
-    return pl.pallas_call(
-        functools.partial(probs_kernel, first),
-        grid=(count,),
-        in_specs=specs,
+    return pl.pallas_call(
+        probs_kernel,
+        grid=(parts,),
+        in_specs=[
+            pl.BlockSpec((width, rows), lambda d: (0, d)),
+            pl.BlockSpec(q_t.shape, lambda d: (0, 0, 0)),
+            pl.BlockSpec(nrm.shape, lambda d: (0, 0)),
+            pl.BlockSpec((1, 1, rows), lambda d: (d, 0, 0)),
+            pl.BlockSpec(qp.shape, lambda d: (0, 0)),
+        ],
         out_specs=[
-            pl.BlockSpec((1, rows + 16, queries), lambda d: (d + start, 0, 0)),
+            pl.BlockSpec((1, rows + 16, queries), lambda d: (d, 0, 0)),
             pl.BlockSpec((8, queries), lambda d: (0, 0)),
         ],
         out_shape=[
             jax.ShapeDtypeStruct((parts, rows + 16, queries), jnp.int16),
             jax.ShapeDtypeStruct((8, queries), f32),
         ],
-        input_output_aliases={} if first else {5: 0},
         compiler_params=params(56),
         cost_estimate=pl.CostEstimate(
-            flops=2 * rows * count * q_t.size,
-            bytes_accessed=cache_t.size * 2 * count // parts + q_t.size * 2,
-            transcendentals=rows * count * heads * queries,
+            flops=2 * keys * q_t.size,
+            bytes_accessed=cache_t.size * 2 + q_t.size * 2,
+            transcendentals=keys * heads * queries,
         ),
         name="probs",
-    )(*args)
+    )(cache_t, q_t, nrm, kp.reshape(parts, 1, rows), qp)
 
 
 def logits_kernel(scale, half_rows, first, *refs):
     if first:
         keys, q, acc = refs
     else:
-        keys, q, before, kp, qp, e_out, stats, acc = refs
+        keys, q, before, kp, qp, e_out, stats, keys_t, acc = refs
     queries = acc.shape[1]
     step = pl.program_id(0)
 
@@ -149,12 +142,13 @@
 
     k = keys[...]
     total = acc[...]
-    w = q[0, pl.ds(half_rows, 16), :].astype(f32)
-    for pair in range(half_rows // queries // 2):
-        s = dot(k, q[0, pl.ds(pair * 2 * queries, 2 * queries), :], NT)
-        for u in range(2):
-            row = pair * 2 + u
-            total += jnp.maximum(s[:, u * queries : (u + 1) * queries], 0.0) * w[row : row + 1]
+    for part in range(q.shape[0]):
+        w = q[part, pl.ds(half_rows, 16), :].astype(f32)
+        for pair in range(half_rows // queries // 2):
+            s = dot(k, q[part, pl.ds(pair * 2 * queries, 2 * queries), :], NT)
+            for u in range(2):
+                row = pair * 2 + u
+                total += jnp.maximum(s[:, u * queries : (u + 1) * queries], 0.0) * w[row : row + 1]
     acc[...] = total
     if first:
         return
@@ -166,6 +160,7 @@
         m = jnp.max(hidden, axis=0, keepdims=True)
         e = jnp.where(vis, jnp.exp(hidden - m), 0.0)
         e_out[...] = e
+        keys_t[...] = jnp.transpose(k)
         z = jnp.sum(e, axis=0, keepdims=True)
         rows = lax.broadcasted_iota(jnp.int32, stats.shape, 0)
         stats[...] = jnp.where(rows == 0, m, z)
@@ -179,15 +174,15 @@
     first = before is None
     whole = pl.BlockSpec((n, queries), lambda d: (0, 0))
     args = [keys, q] + ([] if first else [before, kp, qp])
-    specs = [full(keys), pl.BlockSpec((1, rows, width), lambda d: (d, 0, 0))]
+    specs = [full(keys), pl.BlockSpec((per_step, rows, width), lambda d: (d, 0, 0))]
     specs += [] if first else [full(before), full(kp), full(qp)]
     table = jax.ShapeDtypeStruct((n, queries), f32)
     return pl.pallas_call(
         functools.partial(logits_kernel, scale, half_rows, first),
-        grid=(parts,),
+        grid=(parts // per_step,),
         in_specs=specs,
-        out_specs=whole if first else [whole, pl.BlockSpec((8, queries), lambda d: (0, 0))],
-        out_shape=table if first else [table, jax.ShapeDtypeStruct((8, queries), f32)],
+        out_specs=whole if first else [whole, pl.BlockSpec((8, queries), lambda d: (0, 0)), pl.BlockSpec((width, n), lambda d: (0, 0))],
+        out_shape=table if first else [table, jax.ShapeDtypeStruct((8, queries), f32), jax.ShapeDtypeStruct((width, n), bf16)],
         scratch_shapes=[] if first else [pltpu.VMEM((n, queries), f32)],
         compiler_params=params(),
         cost_estimate=pl.CostEstimate(
@@ -205,7 +200,10 @@
     for i in range(rec.shape[0]):
         ex = from_code(rec[i, pl.ds(n, 16), :])[0:1]
         s += root_decode(rec[i, pl.ds(0, n), :], ex)
-    top, z, t = stats[0:1, :], stats[1:2, :], stats[2:3, :]
+    m_all, z_all, t_all = stats[:, 0, :], stats[:, 1, :], stats[:, 2, :]
+    top = jnp.max(m_all, axis=0, keepdims=True)
+    z = jnp.sum(z_all * jnp.exp(m_all - top), axis=0, keepdims=True)
+    t = jnp.sum(t_all, axis=0, keepdims=True)
     p = e[...] * jnp.exp(own[0:1, :] - top) / z
     target = s / t
     lg[...] = loss_scale * jnp.where(visible_mask(kp[...], qp[...]), p - target, 0.0)
@@ -236,24 +234,24 @@
 
     k = keys[...]
     lg = lg_ref[...]
-    w = q[0, pl.ds(half_rows, 16), :].astype(f32) * scale
-    for pair in range(half_rows // queries // 2):
-        qp = q[0, pl.ds(pair * 2 * queries, 2 * queries), :]
+    heads = half_rows // queries
+    for part in range(q.shape[0]):
+        w = q[part, pl.ds(half_rows, 16), :].astype(f32) * scale
+        qp = q[part, pl.ds(0, half_rows), :]
         s = dot(k, qp, NT)
         pres = []
-        for u in range(2):
-            row = pair * 2 + u
+        for u in range(heads):
             su = s[:, u * queries : (u + 1) * queries]
-            pres.append(jnp.where(su > 0.0, w[row : row + 1] * lg, 0.0).astype(bf16))
+            pres.append(jnp.where(su > 0.0, w[u : u + 1] * lg, 0.0).astype(bf16))
             gw = scale * jnp.sum(jnp.maximum(su, 0.0) * lg, axis=0, keepdims=True)
             for v in range(2):
-                out[row * 2 + v, pl.ds(half, 8), :] = jnp.broadcast_to(gw, (8, queries))
+                out[(part * heads + u) * 2 + v, pl.ds(half, 8), :] = jnp.broadcast_to(gw, (8, queries))
         pre = jnp.concatenate(pres, axis=1)
         gk[...] += dot(pre, qp)
         gq = dot(keys_t[...], pre)
-        for u in range(2):
+        for u in range(heads):
             for v in range(2):
-                out[(pair * 2 + u) * 2 + v, pl.ds(0, half), :] = gq[
+                out[(part * heads + u) * 2 + v, pl.ds(0, half), :] = gq[
                     v * half : (v + 1) * half, u * queries : (u + 1) * queries
                 ]
 
@@ -266,14 +264,14 @@
     full = lambda a: pl.BlockSpec(a.shape, lambda d: (0, 0))
     first = gk_in is None
     args = [keys, keys_t, lg, q] + ([] if first else [gk_in])
-    specs = [full(keys), full(keys_t), full(lg), pl.BlockSpec((1, rows, width), lambda d: (d, 0, 0))]
+    specs = [full(keys), full(keys_t), full(lg), pl.BlockSpec((per_step, rows, width), lambda d: (d, 0, 0))]
     specs += [] if first else [full(gk_in)]
     return pl.pallas_call(
         functools.partial(grads_kernel, scale, half_rows, first),
-        grid=(parts,),
+        grid=(parts // per_step,),
         in_specs=specs,
         out_specs=[
-            pl.BlockSpec((per, width // 2 + 8, queries), lambda d: (d, 0, 0)),
+            pl.BlockSpec((per * per_step, width // 2 + 8, queries), lambda d: (d, 0, 0)),
             pl.BlockSpec((n, width), lambda d: (0, 0)),
         ],
         out_shape=[
@@ -379,25 +377,13 @@
     )(core.reshape(1), mine, other)
 
 
-def merge(parts):
-    top = functools.reduce(jnp.maximum, [p[0:1] for p in parts])
-    z = sum(p[1:2] * jnp.exp(p[0:1] - top) for p in parts)
-    t = sum(p[2:3] for p in parts)
-    return jnp.concatenate([top, z, t, t], axis=0)
-
-
-def ring_merge(s, axes):
-    n = lax.axis_size(axes)
-    moved = [lax.ppermute(s, axes, [(i, (i + k) % n) for i in range(n)]) for k in range(1, n)]
-    return merge([s] + moved)
-
-
 def spread(x, axes, count):
     return lax.all_to_all(jnp.broadcast_to(x[None], (count,) + x.shape), axes, 0, 0, tiled=True)
 
 
 HEAD = ("zh", "x")
 ZY = ("zl", "y")
+CORE = ("core",)
 
 
 def per_device(
@@ -432,29 +418,22 @@
         axis=0,
     )
     q_mine = spread(own, HEAD, parts)
-    cache_t = latent_cache.T
-    mla_t = mla_queries.transpose(0, 2, 1)
-    probs = functools.partial(probs_call, cache_t, mla_t, normalizers, key_positions, qp, parts)
-    coded, total_a = probs(0, parts // 2, None)
+    coded, total = probs_call(
+        latent_cache.T, mla_queries.transpose(0, 2, 1), normalizers, key_positions, qp, parts
+    )
     q_mine, coded = lax.optimization_barrier((q_mine, coded))
     q_other = lax.ppermute(q_mine, "core", swap)
+    rec = lax.all_to_all(coded, HEAD, 0, 0, tiled=True)
 
     offset = lax.axis_index(HEAD) * sub_keys
     own_kp = lax.dynamic_slice_in_dim(key_positions, offset, sub_keys, 0).reshape(1, sub_keys)
     acc = logits_call(index_keys, q_mine, None, own_kp, qp, index_scale, half_rows)
-    e, local = logits_call(index_keys, q_other, acc, own_kp, qp, index_scale, half_rows)
-    coded, e = lax.optimization_barrier((coded, e))
-    coded, total_b = probs(parts // 2, parts // 2, coded)
-
-    stats = jnp.concatenate([local[0:2], (total_a + total_b)[0:2]], axis=0)
-    stats = ring_merge(stats, "core")
-    stats, coded = lax.optimization_barrier((stats, coded))
-    rec = lax.all_to_all(coded, HEAD, 0, 0, tiled=True)
-    for axes in ("y", ("zh", "zl"), "x"):
-        stats = ring_merge(stats, axes)
+    e, local, keys_t = logits_call(index_keys, q_other, acc, own_kp, qp, index_scale, half_rows)
+    stats = jnp.concatenate([local[0:2], total[0:2]], axis=0)
+    stats, rec = lax.optimization_barrier((stats, rec))
+    stats = spread(stats, HEAD + ZY + CORE, parts * zy * 2)
     lg = lg_call(rec, e, local, stats, own_kp, qp)
 
-    keys_t = index_keys.T
     out_other, gk = grads_call(index_keys, keys_t, lg, q_other, None, index_scale, half_rows)
     got = lax.ppermute(out_other, "core", swap)
     out_mine, gk = grads_call(index_keys, keys_t, lg, q_mine, gk, index_scale, half_rows)

time: 138 us -> 126 us (0.913)
  starting transfers between devices: 36.9 us -> 19.5 us
  blocking collectives: 36.4 us -> 51.4 us
  Pallas kernels: 43.3 us -> 36.8 us
  waiting for transfers between devices: 15.3 us -> 13.2 us
    ppermute x10 -> x0, starting transfers between devices: 19.6 us -> none  [ring_merge(): lax.ppermute(s, axes, [(i, (i + k) % n) for i in range(n)])]
    all_to_all x0 -> x1, blocking collectives: none -> 17.3 us  [spread(): lax.all_to_all(jnp.broadcast_to(x[None], (count,) + x.shape), axes, 0, 0,...]
    all_to_all x1, waiting for transfers between devices: 0.01 us -> 12 us  [per_device(): rec = lax.all_to_all(coded, HEAD, 0, 0, tiled=True)]
    ppermute x10 -> x0, waiting for transfers between devices: 7.62 us -> none  [ring_merge(): lax.ppermute(s, axes, [(i, (i + k) % n) for i in range(n)])]
    all_to_all x1, waiting for transfers between devices: 6.44 us -> 0.01 us  [spread(): lax.all_to_all(jnp.broadcast_to(x[None], (count,) + x.shape), axes, 0, 0,...]
    all_to_all x1, starting transfers between devices: 3.56 us -> 6.93 us  [per_device(): rec = lax.all_to_all(coded, HEAD, 0, 0, tiled=True)]
    pallas_call x2, Pallas kernels: 12 us -> 9.02 us  [grads_call(): pl.pallas_call(functools.partial(grads_kernel, scale, half_rows, first),...]
    pallas_call x2 -> x1, Pallas kernels: 22.4 us -> 19.8 us  [probs_call(): pl.pallas_call(probs_kernel, grid=(parts,), in_specs=[pl.BlockSpec((width...]
  transfers between devices with their start and end apart: 15 -> 5, of which waited for: 6 -> 2; matrix products, arithmetic and copies ran while one was open for 1% -> 1% of each run, Pallas kernels for 15% -> 23%
where the time goes in v4:
time: 126 us; the launch traced here: 125 us
  blocking collectives  51.4 us (41%)
  Pallas kernels  36.8 us (29%)
  starting transfers between devices  19.5 us (15%)
  waiting for transfers between devices  13.2 us (10%)
  local copies, waits for them, and re-layouts  3.6 us (3%)
    all_to_all x1, blocking collectives, per_device(): lax.all_to_all(code_call(out_mine, got, parts), HEAD + ZY, 0, 0, tiled=True)  24.3 us
    pallas_call x1, Pallas kernels, probs_call(): pl.pallas_call(probs_kernel, grid=(parts,), in_specs=[pl.BlockSpec((width...  19.8 us
    all_to_all x1, blocking collectives, spread(): lax.all_to_all(jnp.broadcast_to(x[None], (count,) + x.shape), axes, 0, 0,...  17.3 us
    all_to_all x1, waiting for transfers between devices, per_device(): rec = lax.all_to_all(coded, HEAD, 0, 0, tiled=True)  12 us
    all_to_all x1, blocking collectives, per_device(): mine = lax.all_to_all(sum_call(block, zy), ZY, 0, 0, tiled=True)  9.75 us
    pallas_call x2, Pallas kernels, grads_call(): pl.pallas_call(functools.partial(grads_kernel, scale, half_rows, first),...  9.02 us
    all_to_all x1, starting transfers between devices, spread(): lax.all_to_all(jnp.broadcast_to(x[None], (count,) + x.shape), axes, 0, 0,...  8.16 us
    all_to_all x1, starting transfers between devices, per_device(): rec = lax.all_to_all(coded, HEAD, 0, 0, tiled=True)  6.93 us
  transfers between devices with their start and end apart: 5, of which 2 were waited for; matrix products, arithmetic and copies ran while one was open for 1% of the time, Pallas kernels for 23%

profile of v4, /device:TPU:1, one launch (start us, length us, event | category | flops | bytes accessed | tf_op | source)
XLA Modules:
  0.0 125.2 jit_solution(17086294639339767103)
XLA Ops:
  0.6 0.0 copy-start
  0.7 0.7 constant_dynamic-slice_fusion
  1.4 0.2 copy-done
  1.6 1.1 broadcast_in_dim.4
  2.8 8.2 %all-to-all-start = ((bf16[8,528,128]{2,1,0:T(8,128)(2,1)}), bf16[8,528,128]{2,1,0:T(8,128)(2,1)S(1)}, u32[]{:S(2)}, u32[]{:S(2)}) async-start(bf16[8,528,128]{2,1,0:T(8,128)(2,1)} %broadcast_in_dim.4), calls=%async_computation | async-start | bytes 2162688 | tf_op jit(solution)/shard_map/all_to_all | solution.py:381
  10.9 19.8 %probs.1 = (s16[8,528,128]{2,1,0:T(8,128)(2,1)}, f32[8,128]{1,0:T(8,128)}) custom-call(bf16[576,4096]{1,0:T(8,128)(2,1)} %bitcast.14, bf16[16,576,128]{2,1,0:T(8,128)(2,1)} %bitcast.15, f32[16,128]{1,0:T(8,128)} %nrm.1, s32[8,1,512]{2,1,0:T(1,128)} %bitcast.13, s32[1,128]{1,0:T(1,128)} %bitcast.9), custom_call_target="tpu_custom_call" | custom-call | flops 9663676416 | bytes 7077888 | tf_op jit(solution)/shard_map/probs/pallas_call | solution.py:103
  30.8 0.0 copy-start.2
  30.8 0.0 all-to-all-done.refs_1_.refs_3_
  30.8 1.0 collective-permute-start
  31.8 6.9 %all-to-all-start.1 = ((s16[8,528,128]{2,1,0:T(8,128)(2,1)}), s16[8,528,128]{2,1,0:T(8,128)(2,1)S(1)}, u32[]{:S(2)}, u32[]{:S(2)}) async-start(s16[8,528,128]{2,1,0:T(8,128)(2,1)} %get-tuple-element.23), calls=%async_computation.1 | async-start | bytes 2162688 | tf_op jit(solution)/shard_map/all_to_all | solution.py:426
  38.7 0.8 dynamic_slice.11
  39.5 0.7 slice.7
  40.2 0.0 copy-done.2
  40.2 0.0 copy-start.1
  40.2 1.5 %logits.2.refs_2_ = f32[512,128]{1,0:T(8,128)S(1)} custom-call(bf16[512,128]{1,0:T(8,128)(2,1)S(1)} %copy-done.2, bf16[8,528,128]{2,1,0:T(8,128)(2,1)S(1)} %all-to-all-done.refs_1_.refs_3_), custom_call_target="tpu_custom_call" | custom-call | flops 1073741824 | bytes 1081344 | tf_op jit(solution)/shard_map/logits/pallas_call | solution.py:180
  41.7 0.0 collective-permute-done.refs_1_.refs_3_
  41.7 0.0 copy-done.1
  41.7 2.8 %logits.3 = (f32[512,128]{1,0:T(8,128)S(1)}, f32[8,128]{1,0:T(8,128)S(1)}, bf16[128,512]{1,0:T(8,128)(2,1)S(1)}) custom-call(bf16[512,128]{1,0:T(8,128)(2,1)S(1)} %copy-done.2, bf16[8,528,128]{2,1,0:T(8,128)(2,1)} %collective-permute-done.refs_1_.refs_3_, f32[512,128]{1,0:T(8,128)S(1)} %logits.2.refs_2_, s32[1,512]{1,0:T(1,128)S(1)} %bitcast.7, ...), custom_call_target="tpu_custom_call" | custom-call | flops 1073741824 | bytes 1081344 | tf_op jit(solution)/shard_map/logits/pallas_call | solution.py:180
  44.5 12.0 %all-to-all-done.1.rec = s16[8,528,128]{2,1,0:T(8,128)(2,1)S(1)} async-done(((s16[8,528,128]{2,1,0:T(8,128)(2,1)}), s16[8,528,128]{2,1,0:T(8,128)(2,1)S(1)}, u32[]{:S(2)}, u32[]{:S(2)}) %all-to-all-start.1) | async-done | bytes 1081376 | tf_op jit(solution)/shard_map/all_to_all | solution.py:426
  56.5 17.3 %all_to_all.25.stats = f32[128,4,128]{2,1,0:T(4,128)S(1)} all-to-all(f32[128,4,128]{2,1,0:T(4,128)S(1)} %broadcast_in_dim.5), channel_id=1, replica_groups=mesh['zh'=2,'x'=4,'zl'=2,'y'=4,'core'=2] {'zh','x','zl','y','core'}, dimensions={0} | all-to-all | bytes 524288 | tf_op jit(solution)/shard_map/all_to_all | solution.py:381
  73.8 0.8 logit_grad.1.refs_2_
  74.6 4.7 %grads.2 = (f32[64,72,128]{2,1,0:T(8,128)S(1)}, f32[512,128]{1,0:T(8,128)S(1)}) custom-call(bf16[512,128]{1,0:T(8,128)(2,1)S(1)} %copy-done.2, bf16[128,512]{1,0:T(8,128)(2,1)S(1)} %get-tuple-element.20.refs_1_, f32[512,128]{1,0:T(8,128)S(1)} %logit_grad.1.refs_2_, bf16[8,528,128]{2,1,0:T(8,128)(2,1)} %collective-permute-done.refs_1_.refs_3_), custom_call_target="tpu_custom_call" | custom-call | flops 1610612736 | bytes 3244032 | tf_op jit(solution)/shard_map/grads/pallas_call | solution.py:269
  79.3 0.5 collective-permute-start.1
  79.8 4.3 %grads.3 = (f32[64,72,128]{2,1,0:T(8,128)S(1)}, f32[512,128]{1,0:T(8,128)}) custom-call(bf16[512,128]{1,0:T(8,128)(2,1)S(1)} %copy-done.2, bf16[128,512]{1,0:T(8,128)(2,1)S(1)} %get-tuple-element.20.refs_1_, f32[512,128]{1,0:T(8,128)S(1)} %logit_grad.1.refs_2_, bf16[8,528,128]{2,1,0:T(8,128)(2,1)S(1)} %all-to-all-done.refs_1_.refs_3_, ...), custom_call_target="tpu_custom_call" | custom-call | flops 1610612736 | bytes 3244032 | tf_op jit(solution)/shard_map/grads/pallas_call | solution.py:269
  84.1 0.0 collective-permute-done.1.b
  84.1 1.4 %code_parts.1 = s16[64,80,128]{2,1,0:T(8,128)(2,1)S(1)} custom-call(f32[64,72,128]{2,1,0:T(8,128)S(1)} %get-tuple-element.28.a, f32[64,72,128]{2,1,0:T(8,128)S(1)} %collective-permute-done.1.b), custom_call_target="tpu_custom_call" | custom-call | tf_op jit(solution)/shard_map/code_parts/pallas_call | solution.py:317
  85.5 24.3 %all_to_all.26.rec = s16[64,80,128]{2,1,0:T(8,128)(2,1)S(1)} all-to-all(s16[64,80,128]{2,1,0:T(8,128)(2,1)S(1)} %code_parts.1), channel_id=1, replica_groups=mesh['zh'=2,'x'=4,'zl'=2,'y'=4,'core'=2] {'zh','x','zl','y'}, dimensions={0} | all-to-all | bytes 2621440 | tf_op jit(solution)/shard_map/all_to_all | solution.py:440
  109.9 0.5 sum_parts.1
  110.4 9.7 %all_to_all.27.mine = f32[8,72,128]{2,1,0:T(8,128)S(1)} all-to-all(f32[8,72,128]{2,1,0:T(8,128)S(1)} %sum_parts.1), channel_id=1, replica_groups=mesh['zh'=2,'x'=4,'zl'=2,'y'=4,'core'=2] {'zl','y'}, dimensions={0} | all-to-all | bytes 589824 | tf_op jit(solution)/shard_map/all_to_all | solution.py:441
  120.1 2.9 %collective-permute-start.2 = (f32[8,72,128]{2,1,0:T(8,128)S(1)}, f32[8,72,128]{2,1,0:T(8,128)S(1)}, u32[]{:S(2)}, u32[]{:S(2)}) collective-permute-start(f32[8,72,128]{2,1,0:T(8,128)S(1)} %all_to_all.27.mine), channel_id=1, source_target_pairs={{0,1},{1,0},{2,3},{3,2},{4,5},{5,4},{6,7},{7,6},{8,9},{9,8},{10,11... | collective-permute-start | bytes 884744 | tf_op jit(solution)/shard_map/ppermute | solution.py:442
  123.0 1.2 collective-permute-done.2.other
  124.2 1.0 place.1
  (5 shorter events, 0.1 us)
Async XLA Ops:
  0.6 1.0 copy-start
  2.8 28.0 %all-to-all-start = ((bf16[8,528,128]{2,1,0:T(8,128)(2,1)}), bf16[8,528,128]{2,1,0:T(8,128)(2,1)S(1)}, u32[]{:S(2)}, u32[]{:S(2)}) async-start(bf16[8,528,128]{2,1,0:T(8,128)(2,1)} %broadcast_in_dim.4), calls=%async_computation | async-start | bytes 2162688 | tf_op jit(solution)/shard_map/all_to_all | solution.py:381
  30.8 9.4 %copy-start.2 = (bf16[512,128]{1,0:T(8,128)(2,1)S(1)}, bf16[512,128]{1,0:T(8,128)(2,1)}, u32[]{:S(2)}) copy-start(bf16[512,128]{1,0:T(8,128)(2,1)} %refs_0_.7) | copy-start | bytes 393220
  30.8 10.9 %collective-permute-start = (bf16[8,528,128]{2,1,0:T(8,128)(2,1)S(1)}, bf16[8,528,128]{2,1,0:T(8,128)(2,1)}, u32[]{:S(2)}, u32[]{:S(2)}) collective-permute-start(bf16[8,528,128]{2,1,0:T(8,128)(2,1)S(1)} %all-to-all-done.refs_1_.refs_3_), channel_id=1, source_target_pairs={{0,1},{1,0},{2,3},{3,2},{4,5},{5,4},{6,7},{7,6},{8,9},{9,8},{10,11... | collective-permute-start | bytes 3244040 | tf_op jit(solution)/shard_map/ppermute | solution.py:425
  31.8 24.7 %all-to-all-start.1 = ((s16[8,528,128]{2,1,0:T(8,128)(2,1)}), s16[8,528,128]{2,1,0:T(8,128)(2,1)S(1)}, u32[]{:S(2)}, u32[]{:S(2)}) async-start(s16[8,528,128]{2,1,0:T(8,128)(2,1)} %get-tuple-element.23), calls=%async_computation.1 | async-start | bytes 2162688 | tf_op jit(solution)/shard_map/all_to_all | solution.py:426
  40.2 1.5 %copy-start.1 = (s32[128]{0:T(128)S(1)}, s32[128]{0:T(128)}, u32[]{:S(2)}) copy-start(s32[128]{0:T(128)} %param.11) | copy-start | bytes 1540
  79.3 4.8 %collective-permute-start.1 = (f32[64,72,128]{2,1,0:T(8,128)S(1)}, f32[64,72,128]{2,1,0:T(8,128)S(1)}, u32[]{:S(2)}, u32[]{:S(2)}) collective-permute-start(f32[64,72,128]{2,1,0:T(8,128)S(1)} %get-tuple-element.29), channel_id=1, source_target_pairs={{0,1},{1,0},{2,3},{3,2},{4,5},{5,4},{6,7},{7,6},{8,9},{9,8},{10,11... | collective-permute-start | bytes 7077896 | tf_op jit(solution)/shard_map/ppermute | solution.py:438
  120.1 4.1 %collective-permute-start.2 = (f32[8,72,128]{2,1,0:T(8,128)S(1)}, f32[8,72,128]{2,1,0:T(8,128)S(1)}, u32[]{:S(2)}, u32[]{:S(2)}) collective-permute-start(f32[8,72,128]{2,1,0:T(8,128)S(1)} %all_to_all.27.mine), channel_id=1, source_target_pairs={{0,1},{1,0},{2,3},{3,2},{4,5},{5,4},{6,7},{7,6},{8,9},{9,8},{10,11... | collective-permute-start | bytes 884744 | tf_op jit(solution)/shard_map/ppermute | solution.py:442

commit v5 on v4

--- a/solution.py
+++ b/solution.py
@@ -14,6 +14,7 @@
 masked_floor = -1e30
 log2e = math.log2(math.e)
 per_step = 4
+grads_step = 4
 
 NT = (((1,), (1,)), ((), ()))
 NN = (((1,), (0,)), ((), ()))
@@ -32,7 +33,7 @@
     return kp <= jnp.broadcast_to(qp_row, (n, q))
 
 
-def params(mb=40):
+def params(mb=20):
     return pltpu.CompilerParams(vmem_limit_bytes=mb * 1024 * 1024)
 
 
@@ -59,7 +60,8 @@
 
 
 def root_code(x, e):
-    return to_code(jnp.sqrt(jnp.sqrt(shrink(x, e))) * 65535.0 - 32768.0)
+    root = jnp.where(x > 0.0, lax.rsqrt(lax.rsqrt(x)), 0.0)
+    return ((root * (65535.0 * jnp.exp2(e * -0.25)) + 0.5).astype(jnp.int32) - 32768).astype(jnp.int16)
 
 
 def root_decode(c, e):
@@ -132,7 +134,7 @@
     if first:
         keys, q, acc = refs
     else:
-        keys, q, before, kp, qp, e_out, stats, keys_t, acc = refs
+        keys, q, before, kp, qp, e_out, stats, acc = refs
     queries = acc.shape[1]
     step = pl.program_id(0)
 
@@ -160,7 +162,6 @@
         m = jnp.max(hidden, axis=0, keepdims=True)
         e = jnp.where(vis, jnp.exp(hidden - m), 0.0)
         e_out[...] = e
-        keys_t[...] = jnp.transpose(k)
         z = jnp.sum(e, axis=0, keepdims=True)
         rows = lax.broadcasted_iota(jnp.int32, stats.shape, 0)
         stats[...] = jnp.where(rows == 0, m, z)
@@ -181,8 +182,8 @@
         functools.partial(logits_kernel, scale, half_rows, first),
         grid=(parts // per_step,),
         in_specs=specs,
-        out_specs=whole if first else [whole, pl.BlockSpec((8, queries), lambda d: (0, 0)), pl.BlockSpec((width, n), lambda d: (0, 0))],
-        out_shape=table if first else [table, jax.ShapeDtypeStruct((8, queries), f32), jax.ShapeDtypeStruct((width, n), bf16)],
+        out_specs=whole if first else [whole, pl.BlockSpec((8, queries), lambda d: (0, 0))],
+        out_shape=table if first else [table, jax.ShapeDtypeStruct((8, queries), f32)],
         scratch_shapes=[] if first else [pltpu.VMEM((n, queries), f32)],
         compiler_params=params(),
         cost_estimate=pl.CostEstimate(
@@ -200,7 +201,8 @@
     for i in range(rec.shape[0]):
         ex = from_code(rec[i, pl.ds(n, 16), :])[0:1]
         s += root_decode(rec[i, pl.ds(0, n), :], ex)
-    m_all, z_all, t_all = stats[:, 0, :], stats[:, 1, :], stats[:, 2, :]
+    every, queries = stats[:, 0, :], e.shape[1]
+    m_all, z_all, t_all = (every[:, i * queries : (i + 1) * queries] for i in range(3))
     top = jnp.max(m_all, axis=0, keepdims=True)
     z = jnp.sum(z_all * jnp.exp(m_all - top), axis=0, keepdims=True)
     t = jnp.sum(t_all, axis=0, keepdims=True)
@@ -219,73 +221,92 @@
     )(rec, e, own, stats, kp, qp)
 
 
-def grads_kernel(scale, half_rows, first, *refs):
-    if first:
-        keys, keys_t, lg_ref, q, out, gk = refs
-    else:
-        keys, keys_t, lg_ref, q, gk_in, out, gk = refs
+def grads_kernel(scale, half_rows, sides, sums, more, gk_out, gk_more, which, keys, lg_ref, *refs):
+    refs = list(refs)
+    take = lambda count: [refs.pop(0) for _ in range(count)]
+    qs = take(sides)
+    befores = take(sides if more else 0)
+    gk_in = take(1)[0] if gk_more else None
+    outs = take(sides if sums else 0)
+    gk = take(1)[0] if gk_out else None
+    keys_t = take(1)[0]
     queries = lg_ref.shape[1]
     width = keys.shape[1]
     half = width // 2
 
     @pl.when(pl.program_id(0) == 0)
     def _():
-        gk[...] = jnp.zeros(gk.shape, f32) if first else gk_in[...]
+        if gk_out:
+            gk[...] = gk_in[...] if gk_more else jnp.zeros(gk.shape, f32)
+        keys_t[...] = jnp.transpose(keys[...])
 
     k = keys[...]
     lg = lg_ref[...]
     heads = half_rows // queries
-    for part in range(q.shape[0]):
-        w = q[part, pl.ds(half_rows, 16), :].astype(f32) * scale
-        qp = q[part, pl.ds(0, half_rows), :]
-        s = dot(k, qp, NT)
-        pres = []
-        for u in range(heads):
-            su = s[:, u * queries : (u + 1) * queries]
-            pres.append(jnp.where(su > 0.0, w[u : u + 1] * lg, 0.0).astype(bf16))
-            gw = scale * jnp.sum(jnp.maximum(su, 0.0) * lg, axis=0, keepdims=True)
-            for v in range(2):
-                out[(part * heads + u) * 2 + v, pl.ds(half, 8), :] = jnp.broadcast_to(gw, (8, queries))
-        pre = jnp.concatenate(pres, axis=1)
-        gk[...] += dot(pre, qp)
-        gq = dot(keys_t[...], pre)
-        for u in range(heads):
-            for v in range(2):
-                out[(part * heads + u) * 2 + v, pl.ds(0, half), :] = gq[
-                    v * half : (v + 1) * half, u * queries : (u + 1) * queries
-                ]
-
-
-def grads_call(keys, keys_t, lg, q, gk_in, scale, half_rows):
+    for side in range(sides):
+        q = qs[side]
+        for part in range(q.shape[1]):
+            w = q[0, part, pl.ds(half_rows, 16), :].astype(f32) * scale
+            qp = q[0, part, pl.ds(0, half_rows), :]
+            s = dot(k, qp, NT)
+            cut = lambda x, u: x[:, u * queries : (u + 1) * queries]
+            pres = [
+                jnp.where(cut(s, u) > 0.0, w[u : u + 1] * lg, 0.0).astype(bf16) for u in range(heads)
+            ]
+            pre = jnp.concatenate(pres, axis=1)
+            if gk_out:
+                gk[...] += dot(pre, qp)
+            if not sums:
+                continue
+            gq = dot(keys_t[...], pre)
+            for u in range(heads):
+                gw = scale * jnp.sum(jnp.maximum(cut(s, u), 0.0) * lg, axis=0, keepdims=True)
+                for v in range(2):
+                    at = (part * heads + u) * 2 + v
+                    block = cut(gq, u)[v * half : (v + 1) * half]
+                    row = jnp.broadcast_to(gw, (8, queries))
+                    if more:
+                        block += befores[side][at, pl.ds(0, half), :]
+                        row += befores[side][at, pl.ds(half, 8), :]
+                    outs[side][at, pl.ds(0, half), :] = block
+                    outs[side][at, pl.ds(half, 8), :] = row
+
+
+def grads_call(which, keys, lg, qs, befores, gk_out, gk_in, scale, half_rows, sums=True):
     n, width = keys.shape
-    parts, rows, _ = q.shape
+    parts, rows, _ = qs[0].shape
     queries = lg.shape[1]
-    per = 2 * half_rows // queries
-    full = lambda a: pl.BlockSpec(a.shape, lambda d: (0, 0))
-    first = gk_in is None
-    args = [keys, keys_t, lg, q] + ([] if first else [gk_in])
-    specs = [full(keys), full(keys_t), full(lg), pl.BlockSpec((per_step, rows, width), lambda d: (d, 0, 0))]
-    specs += [] if first else [full(gk_in)]
-    return pl.pallas_call(
-        functools.partial(grads_kernel, scale, half_rows, first),
-        grid=(parts // per_step,),
-        in_specs=specs,
-        out_specs=[
-            pl.BlockSpec((per * per_step, width // 2 + 8, queries), lambda d: (d, 0, 0)),
-            pl.BlockSpec((n, width), lambda d: (0, 0)),
-        ],
-        out_shape=[
-            jax.ShapeDtypeStruct((parts * per, width // 2 + 8, queries), f32),
-            jax.ShapeDtypeStruct((n, width), f32),
-        ],
+    blocks = 2 * half_rows // queries * grads_step
+    steps = parts // 2 // grads_step
+    full = lambda a: pl.BlockSpec(a.shape, lambda d, z: (0, 0))
+    part = pl.BlockSpec((1, grads_step, rows, width), lambda d, z: (z[0], d, 0, 0))
+    out = pl.BlockSpec((blocks, width // 2 + 8, queries), lambda d, z: (d, 0, 0))
+    more, gk_more = befores is not None, gk_in is not None
+    args = [keys, lg] + [q.reshape(2, parts // 2, rows, width) for q in qs]
+    args += (befores if more else []) + ([gk_in] if gk_more else [])
+    specs = [full(keys), full(lg)] + [part] * len(qs)
+    specs += [out] * len(qs) if more else []
+    specs += [full(gk_in)] if gk_more else []
+    table = jax.ShapeDtypeStruct((steps * blocks, width // 2 + 8, queries), f32)
+    given = len(qs) if sums else 0
+    return pl.pallas_call(
+        functools.partial(grads_kernel, scale, half_rows, len(qs), sums, more, gk_out, gk_more),
+        grid_spec=pltpu.PrefetchScalarGridSpec(
+            num_scalar_prefetch=1,
+            grid=(steps,),
+            in_specs=specs,
+            out_specs=[out] * given + [pl.BlockSpec((n, width), lambda d, z: (0, 0))] * gk_out,
+            scratch_shapes=[pltpu.VMEM((width, n), bf16)],
+        ),
+        out_shape=[table] * given + [jax.ShapeDtypeStruct((n, width), f32)] * gk_out,
         compiler_params=params(),
         cost_estimate=pl.CostEstimate(
-            flops=3 * 2 * n * parts * half_rows * width,
-            bytes_accessed=parts * rows * width * 6,
+            flops=3 * n * parts * len(qs) * half_rows * width,
+            bytes_accessed=parts * len(qs) * rows * width * 3,
             transcendentals=0,
         ),
         name="grads",
-    )(*args)
+    )(which, *args)
 
 
 def code_kernel(a, b, out):
@@ -421,23 +442,30 @@
     coded, total = probs_call(
         latent_cache.T, mla_queries.transpose(0, 2, 1), normalizers, key_positions, qp, parts
     )
-    q_mine, coded = lax.optimization_barrier((q_mine, coded))
+    pair_keys = lax.ppermute(index_keys, "zh", swap)
+    q_mine, coded, pair_keys = lax.optimization_barrier((q_mine, coded, pair_keys))
     q_other = lax.ppermute(q_mine, "core", swap)
     rec = lax.all_to_all(coded, HEAD, 0, 0, tiled=True)
 
     offset = lax.axis_index(HEAD) * sub_keys
     own_kp = lax.dynamic_slice_in_dim(key_positions, offset, sub_keys, 0).reshape(1, sub_keys)
     acc = logits_call(index_keys, q_mine, None, own_kp, qp, index_scale, half_rows)
-    e, local, keys_t = logits_call(index_keys, q_other, acc, own_kp, qp, index_scale, half_rows)
-    stats = jnp.concatenate([local[0:2], total[0:2]], axis=0)
-    stats, rec = lax.optimization_barrier((stats, rec))
+    e, local = logits_call(index_keys, q_other, acc, own_kp, qp, index_scale, half_rows)
+    stats = jnp.concatenate([local[0:1], local[1:2], total[0:1]], axis=1)
+    side = lax.axis_index("zh").reshape(1)
+    stats, rec, side, far = lax.optimization_barrier((stats, rec, side, 1 - side))
     stats = spread(stats, HEAD + ZY + CORE, parts * zy * 2)
     lg = lg_call(rec, e, local, stats, own_kp, qp)
 
-    out_other, gk = grads_call(index_keys, keys_t, lg, q_other, None, index_scale, half_rows)
+    pair_lg = lax.ppermute(lg, "zh", swap)
+    grads = functools.partial(grads_call, scale=index_scale, half_rows=half_rows)
+    own_other, own_mine, gk = grads(side, index_keys, lg, [q_other, q_mine], None, True, None)
+    (gk,) = grads(far, index_keys, lg, [q_other, q_mine], None, True, gk, sums=False)
+    (own_other, own_mine, gk, pair_lg) = lax.optimization_barrier((own_other, own_mine, gk, pair_lg))
+    (out_other,) = grads(side, pair_keys, pair_lg, [q_other], [own_other], False, None)
     got = lax.ppermute(out_other, "core", swap)
-    out_mine, gk = grads_call(index_keys, keys_t, lg, q_mine, gk, index_scale, half_rows)
-    block = lax.all_to_all(code_call(out_mine, got, parts), HEAD + ZY, 0, 0, tiled=True)
+    (out_mine,) = grads(side, pair_keys, pair_lg, [q_mine], [own_mine], False, None)
+    block = lax.all_to_all(code_call(out_mine, got, parts // 2), ("x",) + ZY, 0, 0, tiled=True)
     mine = lax.all_to_all(sum_call(block, zy), ZY, 0, 0, tiled=True)
     other = lax.ppermute(mine, "core", swap)
     gq, gw = place_call(core, mine, other, local_heads, index_width)

time: 126 us -> 120 us (0.952)
  blocking collectives: 51.4 us -> 40.9 us
  local copies, waits for them, and re-layouts: 3.6 us -> 6.86 us
  Pallas kernels: 36.8 us -> 34.1 us
  starting transfers between devices: 19.5 us -> 22 us
  waiting for transfers between devices: 13.2 us -> 15.3 us
    all_to_all x1, blocking collectives: 24.3 us -> 14.1 us  [per_device(): lax.all_to_all(code_call(out_mine, got, parts // 2), ('x',) + ZY, 0, 0, t...]
    ppermute x0 -> x2, starting transfers between devices: none -> 3.85 us  [the longest x1 2.96 us: per_device(): pair_keys = lax.ppermute(index_keys, 'zh', swap)]
    unnamed x6 -> x18, local copies, waits for them, and re-layouts: 0.23 us -> 3.44 us
    all_to_all x1, starting transfers between devices: 6.93 us -> 3.96 us  [per_device(): rec = lax.all_to_all(coded, HEAD, 0, 0, tiled=True)]
    ppermute x0 -> x2, waiting for transfers between devices: none -> 1.75 us  [the longest x1 1.75 us: per_device(): pair_lg = lax.ppermute(lg, 'zh', swap)]
    pallas_call x1, Pallas kernels: 19.8 us -> 18.4 us  [probs_call(): pl.pallas_call(probs_kernel, grid=(parts,), in_specs=[pl.BlockSpec((width...]
    pallas_call x2 -> x4, Pallas kernels: 9.02 us -> 9.84 us  [grads_call(): pl.pallas_call(functools.partial(grads_kernel, scale, half_rows, len(qs),...]
  transfers between devices with their start and end apart: 5 -> 7, of which waited for: 2 -> 4; matrix products, arithmetic and copies ran while one was open for 1% -> 1% of each run, Pallas kernels for 23% -> 25%
where the time goes in v5:
time: 120 us
  blocking collectives  40.9 us (34%)
  Pallas kernels  34.1 us (28%)
  starting transfers between devices  22 us (18%)
  waiting for transfers between devices  15.3 us (13%)
  local copies, waits for them, and re-layouts  6.86 us (6%)
    pallas_call x1, Pallas kernels, probs_call(): pl.pallas_call(probs_kernel, grid=(parts,), in_specs=[pl.BlockSpec((width...  18.4 us
    all_to_all x1, blocking collectives, spread(): lax.all_to_all(jnp.broadcast_to(x[None], (count,) + x.shape), axes, 0, 0,...  16.7 us
    all_to_all x1, blocking collectives, per_device(): lax.all_to_all(code_call(out_mine, got, parts // 2), ('x',) + ZY, 0, 0, t...  14.1 us
    all_to_all x1, waiting for transfers between devices, per_device(): rec = lax.all_to_all(coded, HEAD, 0, 0, tiled=True)  11.5 us
    all_to_all x1, blocking collectives, per_device(): mine = lax.all_to_all(sum_call(block, zy), ZY, 0, 0, tiled=True)  10.2 us
    pallas_call x4, Pallas kernels, grads_call(): pl.pallas_call(functools.partial(grads_kernel, scale, half_rows, len(qs),...  9.84 us
    all_to_all x1, starting transfers between devices, spread(): lax.all_to_all(jnp.broadcast_to(x[None], (count,) + x.shape), axes, 0, 0,...  8.29 us
    all_to_all x1, starting transfers between devices, per_device(): rec = lax.all_to_all(coded, HEAD, 0, 0, tiled=True)  3.96 us
  transfers between devices with their start and end apart: 7, of which 4 were waited for; matrix products, arithmetic and copies ran while one was open for 1% of the time, Pallas kernels for 25%

profile of v5, /device:TPU:1, one launch (start us, length us, event | category | flops | bytes accessed | tf_op | source)
XLA Modules:
  0.0 120.0 jit_solution(14779902034756639374)
XLA Ops:
  0.6 0.0 copy-start
  0.7 0.7 constant_dynamic-slice_fusion
  1.4 0.2 copy-done
  1.6 1.1 broadcast_in_dim.6
  2.8 0.0 copy-start.6
  2.8 8.3 %all-to-all-start = ((bf16[8,528,128]{2,1,0:T(8,128)(2,1)}), bf16[8,528,128]{2,1,0:T(8,128)(2,1)S(1)}, u32[]{:S(2)}, u32[]{:S(2)}) async-start(bf16[8,528,128]{2,1,0:T(8,128)(2,1)} %broadcast_in_dim.6), calls=%async_computation | async-start | bytes 2162688 | tf_op jit(solution)/shard_map/all_to_all | solution.py:402
  11.1 0.0 copy-done.6
  11.1 3.0 %collective-permute-start = (bf16[512,128]{1,0:T(8,128)(2,1)S(1)}, bf16[512,128]{1,0:T(8,128)(2,1)S(1)}, u32[]{:S(2)}, u32[]{:S(2)}) collective-permute-start(bf16[512,128]{1,0:T(8,128)(2,1)S(1)} %copy-done.6), channel_id=1, source_target_pairs={{0,64},{64,0},{1,65},{65,1},{2,66},{66,2},{3,67},{67,3},{4,68},{68... | collective-permute-start | bytes 393224 | tf_op jit(solution)/shard_map/ppermute | solution.py:445
  14.0 18.4 %probs.1 = (s16[8,528,128]{2,1,0:T(8,128)(2,1)}, f32[8,128]{1,0:T(8,128)}) custom-call(bf16[576,4096]{1,0:T(8,128)(2,1)} %bitcast.23, bf16[16,576,128]{2,1,0:T(8,128)(2,1)} %bitcast.24, f32[16,128]{1,0:T(8,128)} %nrm.1, s32[8,1,512]{2,1,0:T(1,128)} %bitcast.22, s32[1,128]{1,0:T(1,128)} %bitcast.18), custom_call_target="tpu_custom_call" | custom-call | flops 9663676416 | bytes 7077888 | tf_op jit(solution)/shard_map/probs/pallas_call | solution.py:105
  32.5 0.0 collective-permute-done.keys
  32.5 0.0 copy-start.1
  32.5 0.6 copy-done.1
  33.1 0.0 all-to-all-done.refs_1_
  33.1 1.5 %collective-permute-start.1 = (bf16[8,528,128]{2,1,0:T(8,128)(2,1)S(1)}, bf16[8,528,128]{2,1,0:T(8,128)(2,1)S(1)}, u32[]{:S(2)}, u32[]{:S(2)}) collective-permute-start(bf16[8,528,128]{2,1,0:T(8,128)(2,1)S(1)} %all-to-all-done.refs_1_), channel_id=1, source_target_pairs={{0,1},{1,0},{2,3},{3,2},{4,5},{5,4},{6,7},{7,6},{8,9},{9,8},{10,11... | collective-permute-start | bytes 3244040 | tf_op jit(solution)/shard_map/ppermute | solution.py:447
  34.6 4.0 %all-to-all-start.1 = ((s16[8,528,128]{2,1,0:T(8,128)(2,1)}), s16[8,528,128]{2,1,0:T(8,128)(2,1)S(1)}, u32[]{:S(2)}, u32[]{:S(2)}) async-start(s16[8,528,128]{2,1,0:T(8,128)(2,1)} %get-tuple-element.27), calls=%async_computation.1 | async-start | bytes 2162688 | tf_op jit(solution)/shard_map/all_to_all | solution.py:448
  38.6 0.8 dynamic_slice.11
  39.4 0.7 slice.11
  40.0 0.0 copy-start.7
  40.0 0.9 copy-done.7
  41.0 1.5 %logits.2.refs_2_ = f32[512,128]{1,0:T(8,128)S(1)} custom-call(bf16[512,128]{1,0:T(8,128)(2,1)S(1)} %copy-done.7, bf16[8,528,128]{2,1,0:T(8,128)(2,1)S(1)} %all-to-all-done.refs_1_), custom_call_target="tpu_custom_call" | custom-call | flops 1073741824 | bytes 1081344 | tf_op jit(solution)/shard_map/logits/pallas_call | solution.py:181
  42.4 0.0 collective-permute-done.1.refs_1_
  42.4 0.0 copy-done.5
  42.4 1.7 %logits.3 = (f32[512,128]{1,0:T(8,128)S(1)}, f32[8,128]{1,0:T(8,128)S(1)}) custom-call(bf16[512,128]{1,0:T(8,128)(2,1)S(1)} %copy-done.7, bf16[8,528,128]{2,1,0:T(8,128)(2,1)S(1)} %collective-permute-done.1.refs_1_, f32[512,128]{1,0:T(8,128)S(1)} %logits.2.refs_2_, s32[1,512]{1,0:T(1,128)S(1)} %bitcast.16, s32[1,128]{1,0:T(1,128)S(1)} %bitcast.19), custom_call_target="tpu_custom_call" | custom-call | flops 1073741824 | bytes 1081344 | tf_op jit(solution)/shard_map/logits/pallas_call | solution.py:181
  44.2 0.0 copy-start.3
  44.2 0.7 copy-done.3
  44.9 11.5 %all-to-all-done.1.rec = s16[8,528,128]{2,1,0:T(8,128)(2,1)S(1)} async-done(((s16[8,528,128]{2,1,0:T(8,128)(2,1)}), s16[8,528,128]{2,1,0:T(8,128)(2,1)S(1)}, u32[]{:S(2)}, u32[]{:S(2)}) %all-to-all-start.1) | async-done | bytes 1081376 | tf_op jit(solution)/shard_map/all_to_all | solution.py:448
  56.4 0.1 broadcast_in_dim.16
  56.5 16.7 %all_to_all.25.stats = f32[128,1,384]{2,1,0:T(1,128)S(1)} all-to-all(f32[128,1,384]{2,1,0:T(1,128)S(1)} %broadcast_in_dim.16), channel_id=1, replica_groups=mesh['zh'=2,'x'=4,'zl'=2,'y'=4,'core'=2] {'zh','x','zl','y','core'}, dimensions={0} | all-to-all | bytes 393216 | tf_op jit(solution)/shard_map/all_to_all | solution.py:402
  73.2 0.9 copy-done.4
  74.1 0.7 logit_grad.1.lg_ref
  74.9 0.9 collective-permute-start.2
  75.7 0.0 copy-done.8
  75.7 3.4 %grads.4 = (f32[32,72,128]{2,1,0:T(8,128)S(1)}, f32[32,72,128]{2,1,0:T(8,128)S(1)}, f32[512,128]{1,0:T(8,128)S(1)}) custom-call(s32[1]{0:T(128)} %bitcast.7.which, bf16[512,128]{1,0:T(8,128)(2,1)S(1)} %copy-done.8, f32[512,128]{1,0:T(8,128)S(1)} %logit_grad.1.lg_ref, bf16[2,4,528,128]{3,2,1,0:T(8,128)(2,1)S(1)} %bitcast.13, bf16[2,4,528,128]{3,2,1,0:T(8,128)(2,1)S(1)} %bitcast.10), custom_call_target="tpu_custom_call" | custom-call | flops 1610612736 | bytes 3244032 | tf_op jit(solution)/shard_map/grads/pallas_call | solution.py:292
  79.2 0.0 copy-start.2
  79.2 3.2 %grads.5 = f32[512,128]{1,0:T(8,128)} custom-call(s32[1]{0:T(128)S(6)} %sub.3.which, bf16[512,128]{1,0:T(8,128)(2,1)S(1)} %copy-done.8, f32[512,128]{1,0:T(8,128)S(1)} %logit_grad.1.lg_ref, bf16[2,4,528,128]{3,2,1,0:T(8,128)(2,1)S(1)} %bitcast.14, bf16[2,4,528,128]{3,2,1,0:T(8,128)(2,1)S(1)} %bitcast.11, f32[512,128]{1,0:T(8,128)S(1)} %get-tuple-element.36.refs_2_), custom_call_target="tpu_custom_call" | custom-call | flops 1610612736 | bytes 3244032 | tf_op jit(solution)/shard_map/grads/pallas_call | solution.py:292
  82.4 1.8 %collective-permute-done.2.lg_ref = f32[512,128]{1,0:T(8,128)S(1)} collective-permute-done((f32[512,128]{1,0:T(8,128)S(1)}, f32[512,128]{1,0:T(8,128)S(1)}, u32[]{:S(2)}, u32[]{:S(2)}) %collective-permute-start.2) | collective-permute-done | bytes 262176 | tf_op jit(solution)/shard_map/ppermute | solution.py:460
  84.1 0.0 copy-done.2
  84.1 1.6 %grads.7 = f32[32,72,128]{2,1,0:T(8,128)S(1)} custom-call(s32[1]{0:T(128)} %bitcast.7.which, bf16[512,128]{1,0:T(8,128)(2,1)S(1)} %copy-done.2, f32[512,128]{1,0:T(8,128)S(1)} %collective-permute-done.2.lg_ref, bf16[2,4,528,128]{3,2,1,0:T(8,128)(2,1)S(1)} %bitcast.15, f32[32,72,128]{2,1,0:T(8,128)S(1)} %get-tuple-element.39.refs_1_), custom_call_target="tpu_custom_call" | custom-call | flops 805306368 | bytes 1622016 | tf_op jit(solution)/shard_map/grads/pallas_call | solution.py:292
  85.7 1.3 %collective-permute-start.3 = (f32[32,72,128]{2,1,0:T(8,128)S(1)}, f32[32,72,128]{2,1,0:T(8,128)S(1)}, u32[]{:S(2)}, u32[]{:S(2)}) collective-permute-start(f32[32,72,128]{2,1,0:T(8,128)S(1)} %grads.7), channel_id=1, source_target_pairs={{0,1},{1,0},{2,3},{3,2},{4,5},{5,4},{6,7},{7,6},{8,9},{9,8},{10,11... | collective-permute-start | bytes 3538952 | tf_op jit(solution)/shard_map/ppermute | solution.py:466
  87.1 1.6 %grads.6.a = f32[32,72,128]{2,1,0:T(8,128)S(1)} custom-call(s32[1]{0:T(128)} %bitcast.7.which, bf16[512,128]{1,0:T(8,128)(2,1)S(1)} %copy-done.2, f32[512,128]{1,0:T(8,128)S(1)} %collective-permute-done.2.lg_ref, bf16[2,4,528,128]{3,2,1,0:T(8,128)(2,1)S(1)} %bitcast.12, f32[32,72,128]{2,1,0:T(8,128)S(1)} %get-tuple-element.38.refs_1_), custom_call_target="tpu_custom_call" | custom-call | flops 805306368 | bytes 1622016 | tf_op jit(solution)/shard_map/grads/pallas_call | solution.py:292
  88.7 0.8 collective-permute-done.3.b
  89.5 0.7 code_parts.1
  90.2 14.1 %all_to_all.26.rec = s16[32,80,128]{2,1,0:T(8,128)(2,1)S(1)} all-to-all(s16[32,80,128]{2,1,0:T(8,128)(2,1)S(1)} %code_parts.1), channel_id=1, replica_groups=mesh['zh'=2,'x'=4,'zl'=2,'y'=4,'core'=2] {'x','zl','y'}, dimensions={0} | all-to-all | bytes 1310720 | tf_op jit(solution)/shard_map/all_to_all | solution.py:468
  104.3 0.3 sum_parts.1
  104.6 10.2 %all_to_all.27.mine = f32[8,72,128]{2,1,0:T(8,128)S(1)} all-to-all(f32[8,72,128]{2,1,0:T(8,128)S(1)} %sum_parts.1), channel_id=1, replica_groups=mesh['zh'=2,'x'=4,'zl'=2,'y'=4,'core'=2] {'zl','y'}, dimensions={0} | all-to-all | bytes 589824 | tf_op jit(solution)/shard_map/all_to_all | solution.py:469
  114.8 3.1 %collective-permute-start.4 = (f32[8,72,128]{2,1,0:T(8,128)S(1)}, f32[8,72,128]{2,1,0:T(8,128)S(1)}, u32[]{:S(2)}, u32[]{:S(2)}) collective-permute-start(f32[8,72,128]{2,1,0:T(8,128)S(1)} %all_to_all.27.mine), channel_id=1, source_target_pairs={{0,1},{1,0},{2,3},{3,2},{4,5},{5,4},{6,7},{7,6},{8,9},{9,8},{10,11... | collective-permute-start | bytes 884744 | tf_op jit(solution)/shard_map/ppermute | solution.py:470
  117.8 1.2 %collective-permute-done.4.other = f32[8,72,128]{2,1,0:T(8,128)S(1)} collective-permute-done((f32[8,72,128]{2,1,0:T(8,128)S(1)}, f32[8,72,128]{2,1,0:T(8,128)S(1)}, u32[]{:S(2)}, u32[]{:S(2)}) %collective-permute-start.4) | collective-permute-done | bytes 294944 | tf_op jit(solution)/shard_map/ppermute | solution.py:470
  119.0 1.0 place.1
  (8 shorter events, 0.1 us)
Async XLA Ops:
  0.6 1.0 copy-start
  2.8 8.3 %copy-start.6 = (bf16[512,128]{1,0:T(8,128)(2,1)S(1)}, bf16[512,128]{1,0:T(8,128)(2,1)}, u32[]{:S(2)}) copy-start(bf16[512,128]{1,0:T(8,128)(2,1)} %keys.3) | copy-start | bytes 393220
  2.8 30.4 %all-to-all-start = ((bf16[8,528,128]{2,1,0:T(8,128)(2,1)}), bf16[8,528,128]{2,1,0:T(8,128)(2,1)S(1)}, u32[]{:S(2)}, u32[]{:S(2)}) async-start(bf16[8,528,128]{2,1,0:T(8,128)(2,1)} %broadcast_in_dim.6), calls=%async_computation | async-start | bytes 2162688 | tf_op jit(solution)/shard_map/all_to_all | solution.py:402
  11.1 21.4 %collective-permute-start = (bf16[512,128]{1,0:T(8,128)(2,1)S(1)}, bf16[512,128]{1,0:T(8,128)(2,1)S(1)}, u32[]{:S(2)}, u32[]{:S(2)}) collective-permute-start(bf16[512,128]{1,0:T(8,128)(2,1)S(1)} %copy-done.6), channel_id=1, source_target_pairs={{0,64},{64,0},{1,65},{65,1},{2,66},{66,2},{3,67},{67,3},{4,68},{68... | collective-permute-start | bytes 393224 | tf_op jit(solution)/shard_map/ppermute | solution.py:445
  32.5 0.7 copy-start.1
  33.1 9.3 %collective-permute-start.1 = (bf16[8,528,128]{2,1,0:T(8,128)(2,1)S(1)}, bf16[8,528,128]{2,1,0:T(8,128)(2,1)S(1)}, u32[]{:S(2)}, u32[]{:S(2)}) collective-permute-start(bf16[8,528,128]{2,1,0:T(8,128)(2,1)S(1)} %all-to-all-done.refs_1_), channel_id=1, source_target_pairs={{0,1},{1,0},{2,3},{3,2},{4,5},{5,4},{6,7},{7,6},{8,9},{9,8},{10,11... | collective-permute-start | bytes 3244040 | tf_op jit(solution)/shard_map/ppermute | solution.py:447
  34.6 21.7 %all-to-all-start.1 = ((s16[8,528,128]{2,1,0:T(8,128)(2,1)}), s16[8,528,128]{2,1,0:T(8,128)(2,1)S(1)}, u32[]{:S(2)}, u32[]{:S(2)}) async-start(s16[8,528,128]{2,1,0:T(8,128)(2,1)} %get-tuple-element.27), calls=%async_computation.1 | async-start | bytes 2162688 | tf_op jit(solution)/shard_map/all_to_all | solution.py:448
  40.0 0.9 copy-start.7
  41.0 1.5 %copy-start.5 = (s32[128]{0:T(128)S(1)}, s32[128]{0:T(128)}, u32[]{:S(2)}) copy-start(s32[128]{0:T(128)} %param.11) | copy-start | bytes 1540
  44.2 0.7 copy-start.3
  56.4 19.4 %copy-start.8 = (bf16[512,128]{1,0:T(8,128)(2,1)S(1)}, bf16[512,128]{1,0:T(8,128)(2,1)}, u32[]{:S(2)}) copy-start(bf16[512,128]{1,0:T(8,128)(2,1)} %keys.3) | copy-start | bytes 393220
  73.2 1.0 copy-start.4
  74.9 9.3 %collective-permute-start.2 = (f32[512,128]{1,0:T(8,128)S(1)}, f32[512,128]{1,0:T(8,128)S(1)}, u32[]{:S(2)}, u32[]{:S(2)}) collective-permute-start(f32[512,128]{1,0:T(8,128)S(1)} %logit_grad.1.lg_ref), channel_id=1, source_target_pairs={{0,64},{64,0},{1,65},{65,1},{2,66},{66,2},{3,67},{67,3},{4,68},{68... | collective-permute-start | bytes 786440 | tf_op jit(solution)/shard_map/ppermute | solution.py:460
  79.2 4.9 %copy-start.2 = (bf16[512,128]{1,0:T(8,128)(2,1)S(1)}, bf16[512,128]{1,0:T(8,128)(2,1)}, u32[]{:S(2)}) copy-start(bf16[512,128]{1,0:T(8,128)(2,1)} %copy-done.1) | copy-start | bytes 393220
  85.7 3.8 %collective-permute-start.3 = (f32[32,72,128]{2,1,0:T(8,128)S(1)}, f32[32,72,128]{2,1,0:T(8,128)S(1)}, u32[]{:S(2)}, u32[]{:S(2)}) collective-permute-start(f32[32,72,128]{2,1,0:T(8,128)S(1)} %grads.7), channel_id=1, source_target_pairs={{0,1},{1,0},{2,3},{3,2},{4,5},{5,4},{6,7},{7,6},{8,9},{9,8},{10,11... | collective-permute-start | bytes 3538952 | tf_op jit(solution)/shard_map/ppermute | solution.py:466
  114.8 4.3 %collective-permute-start.4 = (f32[8,72,128]{2,1,0:T(8,128)S(1)}, f32[8,72,128]{2,1,0:T(8,128)S(1)}, u32[]{:S(2)}, u32[]{:S(2)}) collective-permute-start(f32[8,72,128]{2,1,0:T(8,128)S(1)} %all_to_all.27.mine), channel_id=1, source_target_pairs={{0,1},{1,0},{2,3},{3,2},{4,5},{5,4},{6,7},{7,6},{8,9},{9,8},{10,11... | collective-permute-start | bytes 884744 | tf_op jit(solution)/shard_map/ppermute | solution.py:470

commit v6 on v5

--- a/solution.py
+++ b/solution.py
@@ -15,6 +15,7 @@
 log2e = math.log2(math.e)
 per_step = 4
 grads_step = 4
+row_blocks = 4
 
 NT = (((1,), (1,)), ((), ()))
 NN = (((1,), (0,)), ((), ()))
@@ -78,10 +79,11 @@
     def _():
         tot[...] = jnp.zeros(tot.shape, f32)
 
-    rows = keys // 2
-    sums = []
+    rows = keys // row_blocks
     xt = jnp.transpose(cache[...])
-    for block in range(2):
+    e_rows = []
+    total = jnp.zeros((1, queries), f32)
+    for block in range(row_blocks):
         x = xt[block * rows : (block + 1) * rows]
         acc = jnp.zeros((rows, queries), f32)
         for pair in range(heads // 2):
@@ -89,13 +91,13 @@
             for u in range(2):
                 n = nrm[pl.ds(pair * 2 + u, 1), :] * log2e
                 acc += jnp.exp2(s[:, u * queries : (u + 1) * queries] * (att_scale * log2e) - n)
-        sums.append(acc)
-    summed = jnp.concatenate(sums, axis=0)
-    summed = jnp.where(visible_mask(kp[0], qp[...]), summed, 0.0)
-    e = exponent(jnp.max(summed, axis=0, keepdims=True))
-    out[0, pl.ds(0, keys), :] = root_code(summed, e)
-    out[0, pl.ds(keys, 16), :] = to_code(jnp.broadcast_to(e, (16, queries)))
-    tot[...] += jnp.broadcast_to(jnp.sum(summed, axis=0, keepdims=True), tot.shape)
+        acc = jnp.where(visible_mask(kp[0, :, pl.ds(block * rows, rows)], qp[...]), acc, 0.0)
+        e = exponent(jnp.max(acc, axis=0, keepdims=True))
+        out[0, pl.ds(block * rows, rows), :] = root_code(acc, e)
+        e_rows.append(jnp.broadcast_to(e, (16 // row_blocks, queries)))
+        total += jnp.sum(acc, axis=0, keepdims=True)
+    out[0, pl.ds(keys, 16), :] = to_code(jnp.concatenate(e_rows, axis=0))
+    tot[...] += jnp.broadcast_to(total, tot.shape)
 
 
 def probs_call(cache_t, q_t, nrm, kp, qp, parts):
@@ -199,8 +201,13 @@
     n = e.shape[0]
     s = jnp.zeros(e.shape, f32)
     for i in range(rec.shape[0]):
-        ex = from_code(rec[i, pl.ds(n, 16), :])[0:1]
-        s += root_decode(rec[i, pl.ds(0, n), :], ex)
+        ex = from_code(rec[i, pl.ds(n, 16), :])
+        rows, step = n // row_blocks, 16 // row_blocks
+        parts = [
+            root_decode(rec[i, pl.ds(b * rows, rows), :], ex[b * step : b * step + 1])
+            for b in range(row_blocks)
+        ]
+        s += jnp.concatenate(parts, axis=0)
     every, queries = stats[:, 0, :], e.shape[1]
     m_all, z_all, t_all = (every[:, i * queries : (i + 1) * queries] for i in range(3))
     top = jnp.max(m_all, axis=0, keepdims=True)

time: 120 us -> 120 us (level)
  no operation moved by 1% of the time
where the time goes in v6:
time: 120 us
  blocking collectives  40.9 us (34%)
  Pallas kernels  33.7 us (28%)
  starting transfers between devices  22 us (18%)
  waiting for transfers between devices  15.3 us (13%)
  local copies, waits for them, and re-layouts  6.86 us (6%)
    pallas_call x1, Pallas kernels, probs_call(): pl.pallas_call(probs_kernel, grid=(parts,), in_specs=[pl.BlockSpec((width...  18 us
    all_to_all x1, blocking collectives, spread(): lax.all_to_all(jnp.broadcast_to(x[None], (count,) + x.shape), axes, 0, 0,...  16.7 us
    all_to_all x1, blocking collectives, per_device(): lax.all_to_all(code_call(out_mine, got, parts // 2), ('x',) + ZY, 0, 0, t...  14 us
    all_to_all x1, waiting for transfers between devices, per_device(): rec = lax.all_to_all(coded, HEAD, 0, 0, tiled=True)  11.5 us
    all_to_all x1, blocking collectives, per_device(): mine = lax.all_to_all(sum_call(block, zy), ZY, 0, 0, tiled=True)  10.2 us
    pallas_call x4, Pallas kernels, grads_call(): pl.pallas_call(functools.partial(grads_kernel, scale, half_rows, len(qs),...  9.84 us
    all_to_all x1, starting transfers between devices, spread(): lax.all_to_all(jnp.broadcast_to(x[None], (count,) + x.shape), axes, 0, 0,...  8.29 us
    all_to_all x1, starting transfers between devices, per_device(): rec = lax.all_to_all(coded, HEAD, 0, 0, tiled=True)  3.96 us
  transfers between devices with their start and end apart: 7, of which 4 were waited for; matrix products, arithmetic and copies ran while one was open for 1% of the time, Pallas kernels for 25%

profile of v6, /device:TPU:1, one launch (start us, length us, event | category | flops | bytes accessed | tf_op | source)
XLA Modules:
  0.0 119.6 jit_solution(1915047479230959268)
XLA Ops:
  0.6 0.0 copy-start
  0.7 0.7 constant_dynamic-slice_fusion
  1.4 0.2 copy-done
  1.6 1.1 broadcast_in_dim.6
  2.8 0.0 copy-start.6
  2.8 8.3 %all-to-all-start = ((bf16[8,528,128]{2,1,0:T(8,128)(2,1)}), bf16[8,528,128]{2,1,0:T(8,128)(2,1)S(1)}, u32[]{:S(2)}, u32[]{:S(2)}) async-start(bf16[8,528,128]{2,1,0:T(8,128)(2,1)} %broadcast_in_dim.6), calls=%async_computation | async-start | bytes 2162688 | tf_op jit(solution)/shard_map/all_to_all | solution.py:409
  11.1 0.0 copy-done.6
  11.1 3.0 %collective-permute-start = (bf16[512,128]{1,0:T(8,128)(2,1)S(1)}, bf16[512,128]{1,0:T(8,128)(2,1)S(1)}, u32[]{:S(2)}, u32[]{:S(2)}) collective-permute-start(bf16[512,128]{1,0:T(8,128)(2,1)S(1)} %copy-done.6), channel_id=1, source_target_pairs={{0,64},{64,0},{1,65},{65,1},{2,66},{66,2},{3,67},{67,3},{4,68},{68... | collective-permute-start | bytes 393224 | tf_op jit(solution)/shard_map/ppermute | solution.py:452
  14.0 18.0 %probs.1 = (s16[8,528,128]{2,1,0:T(8,128)(2,1)}, f32[8,128]{1,0:T(8,128)}) custom-call(bf16[576,4096]{1,0:T(8,128)(2,1)} %bitcast.23, bf16[16,576,128]{2,1,0:T(8,128)(2,1)} %bitcast.24, f32[16,128]{1,0:T(8,128)} %nrm.1, s32[8,1,512]{2,1,0:T(1,128)} %bitcast.22, s32[1,128]{1,0:T(1,128)} %bitcast.18), custom_call_target="tpu_custom_call" | custom-call | flops 9663676416 | bytes 7077888 | tf_op jit(solution)/shard_map/probs/pallas_call | solution.py:107
  32.0 0.0 collective-permute-done.keys
  32.0 0.0 copy-start.1
  32.0 0.6 copy-done.1
  32.7 0.0 all-to-all-done.refs_1_
  32.7 1.5 %collective-permute-start.1 = (bf16[8,528,128]{2,1,0:T(8,128)(2,1)S(1)}, bf16[8,528,128]{2,1,0:T(8,128)(2,1)S(1)}, u32[]{:S(2)}, u32[]{:S(2)}) collective-permute-start(bf16[8,528,128]{2,1,0:T(8,128)(2,1)S(1)} %all-to-all-done.refs_1_), channel_id=1, source_target_pairs={{0,1},{1,0},{2,3},{3,2},{4,5},{5,4},{6,7},{7,6},{8,9},{9,8},{10,11... | collective-permute-start | bytes 3244040 | tf_op jit(solution)/shard_map/ppermute | solution.py:454
  34.2 4.0 %all-to-all-start.1 = ((s16[8,528,128]{2,1,0:T(8,128)(2,1)}), s16[8,528,128]{2,1,0:T(8,128)(2,1)S(1)}, u32[]{:S(2)}, u32[]{:S(2)}) async-start(s16[8,528,128]{2,1,0:T(8,128)(2,1)} %get-tuple-element.27), calls=%async_computation.1 | async-start | bytes 2162688 | tf_op jit(solution)/shard_map/all_to_all | solution.py:455
  38.2 0.8 dynamic_slice.11
  38.9 0.7 slice.11
  39.6 0.0 copy-start.7
  39.6 0.9 copy-done.7
  40.5 1.5 %logits.2.refs_2_ = f32[512,128]{1,0:T(8,128)S(1)} custom-call(bf16[512,128]{1,0:T(8,128)(2,1)S(1)} %copy-done.7, bf16[8,528,128]{2,1,0:T(8,128)(2,1)S(1)} %all-to-all-done.refs_1_), custom_call_target="tpu_custom_call" | custom-call | flops 1073741824 | bytes 1081344 | tf_op jit(solution)/shard_map/logits/pallas_call | solution.py:183
  42.0 0.0 collective-permute-done.1.refs_1_
  42.0 0.0 copy-done.5
  42.0 1.7 %logits.3 = (f32[512,128]{1,0:T(8,128)S(1)}, f32[8,128]{1,0:T(8,128)S(1)}) custom-call(bf16[512,128]{1,0:T(8,128)(2,1)S(1)} %copy-done.7, bf16[8,528,128]{2,1,0:T(8,128)(2,1)S(1)} %collective-permute-done.1.refs_1_, f32[512,128]{1,0:T(8,128)S(1)} %logits.2.refs_2_, s32[1,512]{1,0:T(1,128)S(1)} %bitcast.16, s32[1,128]{1,0:T(1,128)S(1)} %bitcast.19), custom_call_target="tpu_custom_call" | custom-call | flops 1073741824 | bytes 1081344 | tf_op jit(solution)/shard_map/logits/pallas_call | solution.py:183
  43.7 0.0 copy-start.3
  43.8 0.7 copy-done.3
  44.5 11.5 %all-to-all-done.1.rec = s16[8,528,128]{2,1,0:T(8,128)(2,1)S(1)} async-done(((s16[8,528,128]{2,1,0:T(8,128)(2,1)}), s16[8,528,128]{2,1,0:T(8,128)(2,1)S(1)}, u32[]{:S(2)}, u32[]{:S(2)}) %all-to-all-start.1) | async-done | bytes 1081376 | tf_op jit(solution)/shard_map/all_to_all | solution.py:455
  56.0 0.1 broadcast_in_dim.16
  56.1 16.7 %all_to_all.25.stats = f32[128,1,384]{2,1,0:T(1,128)S(1)} all-to-all(f32[128,1,384]{2,1,0:T(1,128)S(1)} %broadcast_in_dim.16), channel_id=1, replica_groups=mesh['zh'=2,'x'=4,'zl'=2,'y'=4,'core'=2] {'zh','x','zl','y','core'}, dimensions={0} | all-to-all | bytes 393216 | tf_op jit(solution)/shard_map/all_to_all | solution.py:409
  72.8 0.9 copy-done.4
  73.7 0.7 logit_grad.1.lg_ref
  74.4 0.9 collective-permute-start.2
  75.3 0.0 copy-done.8
  75.3 3.4 %grads.4 = (f32[32,72,128]{2,1,0:T(8,128)S(1)}, f32[32,72,128]{2,1,0:T(8,128)S(1)}, f32[512,128]{1,0:T(8,128)S(1)}) custom-call(s32[1]{0:T(128)} %bitcast.7.which, bf16[512,128]{1,0:T(8,128)(2,1)S(1)} %copy-done.8, f32[512,128]{1,0:T(8,128)S(1)} %logit_grad.1.lg_ref, bf16[2,4,528,128]{3,2,1,0:T(8,128)(2,1)S(1)} %bitcast.13, bf16[2,4,528,128]{3,2,1,0:T(8,128)(2,1)S(1)} %bitcast.10), custom_call_target="tpu_custom_call" | custom-call | flops 1610612736 | bytes 3244032 | tf_op jit(solution)/shard_map/grads/pallas_call | solution.py:299
  78.8 0.0 copy-start.2
  78.8 3.2 %grads.5 = f32[512,128]{1,0:T(8,128)} custom-call(s32[1]{0:T(128)S(6)} %sub.3.which, bf16[512,128]{1,0:T(8,128)(2,1)S(1)} %copy-done.8, f32[512,128]{1,0:T(8,128)S(1)} %logit_grad.1.lg_ref, bf16[2,4,528,128]{3,2,1,0:T(8,128)(2,1)S(1)} %bitcast.14, bf16[2,4,528,128]{3,2,1,0:T(8,128)(2,1)S(1)} %bitcast.11, f32[512,128]{1,0:T(8,128)S(1)} %get-tuple-element.36.refs_2_), custom_call_target="tpu_custom_call" | custom-call | flops 1610612736 | bytes 3244032 | tf_op jit(solution)/shard_map/grads/pallas_call | solution.py:299
  81.9 1.7 %collective-permute-done.2.lg_ref = f32[512,128]{1,0:T(8,128)S(1)} collective-permute-done((f32[512,128]{1,0:T(8,128)S(1)}, f32[512,128]{1,0:T(8,128)S(1)}, u32[]{:S(2)}, u32[]{:S(2)}) %collective-permute-start.2) | collective-permute-done | bytes 262176 | tf_op jit(solution)/shard_map/ppermute | solution.py:467
  83.7 0.0 copy-done.2
  83.7 1.6 %grads.7 = f32[32,72,128]{2,1,0:T(8,128)S(1)} custom-call(s32[1]{0:T(128)} %bitcast.7.which, bf16[512,128]{1,0:T(8,128)(2,1)S(1)} %copy-done.2, f32[512,128]{1,0:T(8,128)S(1)} %collective-permute-done.2.lg_ref, bf16[2,4,528,128]{3,2,1,0:T(8,128)(2,1)S(1)} %bitcast.15, f32[32,72,128]{2,1,0:T(8,128)S(1)} %get-tuple-element.39.refs_1_), custom_call_target="tpu_custom_call" | custom-call | flops 805306368 | bytes 1622016 | tf_op jit(solution)/shard_map/grads/pallas_call | solution.py:299
  85.3 1.3 %collective-permute-start.3 = (f32[32,72,128]{2,1,0:T(8,128)S(1)}, f32[32,72,128]{2,1,0:T(8,128)S(1)}, u32[]{:S(2)}, u32[]{:S(2)}) collective-permute-start(f32[32,72,128]{2,1,0:T(8,128)S(1)} %grads.7), channel_id=1, source_target_pairs={{0,1},{1,0},{2,3},{3,2},{4,5},{5,4},{6,7},{7,6},{8,9},{9,8},{10,11... | collective-permute-start | bytes 3538952 | tf_op jit(solution)/shard_map/ppermute | solution.py:473
  86.6 1.6 %grads.6.a = f32[32,72,128]{2,1,0:T(8,128)S(1)} custom-call(s32[1]{0:T(128)} %bitcast.7.which, bf16[512,128]{1,0:T(8,128)(2,1)S(1)} %copy-done.2, f32[512,128]{1,0:T(8,128)S(1)} %collective-permute-done.2.lg_ref, bf16[2,4,528,128]{3,2,1,0:T(8,128)(2,1)S(1)} %bitcast.12, f32[32,72,128]{2,1,0:T(8,128)S(1)} %get-tuple-element.38.refs_1_), custom_call_target="tpu_custom_call" | custom-call | flops 805306368 | bytes 1622016 | tf_op jit(solution)/shard_map/grads/pallas_call | solution.py:299
  88.3 0.8 collective-permute-done.3.b
  89.1 0.7 code_parts.1
  89.8 14.0 %all_to_all.26.rec = s16[32,80,128]{2,1,0:T(8,128)(2,1)S(1)} all-to-all(s16[32,80,128]{2,1,0:T(8,128)(2,1)S(1)} %code_parts.1), channel_id=1, replica_groups=mesh['zh'=2,'x'=4,'zl'=2,'y'=4,'core'=2] {'x','zl','y'}, dimensions={0} | all-to-all | bytes 1310720 | tf_op jit(solution)/shard_map/all_to_all | solution.py:475
  103.9 0.3 sum_parts.1
  104.1 10.2 %all_to_all.27.mine = f32[8,72,128]{2,1,0:T(8,128)S(1)} all-to-all(f32[8,72,128]{2,1,0:T(8,128)S(1)} %sum_parts.1), channel_id=1, replica_groups=mesh['zh'=2,'x'=4,'zl'=2,'y'=4,'core'=2] {'zl','y'}, dimensions={0} | all-to-all | bytes 589824 | tf_op jit(solution)/shard_map/all_to_all | solution.py:476
  114.3 3.1 %collective-permute-start.4 = (f32[8,72,128]{2,1,0:T(8,128)S(1)}, f32[8,72,128]{2,1,0:T(8,128)S(1)}, u32[]{:S(2)}, u32[]{:S(2)}) collective-permute-start(f32[8,72,128]{2,1,0:T(8,128)S(1)} %all_to_all.27.mine), channel_id=1, source_target_pairs={{0,1},{1,0},{2,3},{3,2},{4,5},{5,4},{6,7},{7,6},{8,9},{9,8},{10,11... | collective-permute-start | bytes 884744 | tf_op jit(solution)/shard_map/ppermute | solution.py:477
  117.4 1.2 %collective-permute-done.4.other = f32[8,72,128]{2,1,0:T(8,128)S(1)} collective-permute-done((f32[8,72,128]{2,1,0:T(8,128)S(1)}, f32[8,72,128]{2,1,0:T(8,128)S(1)}, u32[]{:S(2)}, u32[]{:S(2)}) %collective-permute-start.4) | collective-permute-done | bytes 294944 | tf_op jit(solution)/shard_map/ppermute | solution.py:477
  118.6 1.0 place.1
  (8 shorter events, 0.1 us)
Async XLA Ops:
  0.6 1.0 copy-start
  2.8 8.3 %copy-start.6 = (bf16[512,128]{1,0:T(8,128)(2,1)S(1)}, bf16[512,128]{1,0:T(8,128)(2,1)}, u32[]{:S(2)}) copy-start(bf16[512,128]{1,0:T(8,128)(2,1)} %keys.3) | copy-start | bytes 393220
  2.8 29.9 %all-to-all-start = ((bf16[8,528,128]{2,1,0:T(8,128)(2,1)}), bf16[8,528,128]{2,1,0:T(8,128)(2,1)S(1)}, u32[]{:S(2)}, u32[]{:S(2)}) async-start(bf16[8,528,128]{2,1,0:T(8,128)(2,1)} %broadcast_in_dim.6), calls=%async_computation | async-start | bytes 2162688 | tf_op jit(solution)/shard_map/all_to_all | solution.py:409
  11.1 21.0 %collective-permute-start = (bf16[512,128]{1,0:T(8,128)(2,1)S(1)}, bf16[512,128]{1,0:T(8,128)(2,1)S(1)}, u32[]{:S(2)}, u32[]{:S(2)}) collective-permute-start(bf16[512,128]{1,0:T(8,128)(2,1)S(1)} %copy-done.6), channel_id=1, source_target_pairs={{0,64},{64,0},{1,65},{65,1},{2,66},{66,2},{3,67},{67,3},{4,68},{68... | collective-permute-start | bytes 393224 | tf_op jit(solution)/shard_map/ppermute | solution.py:452
  32.0 0.7 copy-start.1
  32.7 9.3 %collective-permute-start.1 = (bf16[8,528,128]{2,1,0:T(8,128)(2,1)S(1)}, bf16[8,528,128]{2,1,0:T(8,128)(2,1)S(1)}, u32[]{:S(2)}, u32[]{:S(2)}) collective-permute-start(bf16[8,528,128]{2,1,0:T(8,128)(2,1)S(1)} %all-to-all-done.refs_1_), channel_id=1, source_target_pairs={{0,1},{1,0},{2,3},{3,2},{4,5},{5,4},{6,7},{7,6},{8,9},{9,8},{10,11... | collective-permute-start | bytes 3244040 | tf_op jit(solution)/shard_map/ppermute | solution.py:454
  34.2 21.7 %all-to-all-start.1 = ((s16[8,528,128]{2,1,0:T(8,128)(2,1)}), s16[8,528,128]{2,1,0:T(8,128)(2,1)S(1)}, u32[]{:S(2)}, u32[]{:S(2)}) async-start(s16[8,528,128]{2,1,0:T(8,128)(2,1)} %get-tuple-element.27), calls=%async_computation.1 | async-start | bytes 2162688 | tf_op jit(solution)/shard_map/all_to_all | solution.py:455
  39.6 0.9 copy-start.7
  40.5 1.5 %copy-start.5 = (s32[128]{0:T(128)S(1)}, s32[128]{0:T(128)}, u32[]{:S(2)}) copy-start(s32[128]{0:T(128)} %param.11) | copy-start | bytes 1540
  43.7 0.7 copy-start.3
  56.0 19.4 %copy-start.8 = (bf16[512,128]{1,0:T(8,128)(2,1)S(1)}, bf16[512,128]{1,0:T(8,128)(2,1)}, u32[]{:S(2)}) copy-start(bf16[512,128]{1,0:T(8,128)(2,1)} %keys.3) | copy-start | bytes 393220
  72.8 1.0 copy-start.4
  74.4 9.3 %collective-permute-start.2 = (f32[512,128]{1,0:T(8,128)S(1)}, f32[512,128]{1,0:T(8,128)S(1)}, u32[]{:S(2)}, u32[]{:S(2)}) collective-permute-start(f32[512,128]{1,0:T(8,128)S(1)} %logit_grad.1.lg_ref), channel_id=1, source_target_pairs={{0,64},{64,0},{1,65},{65,1},{2,66},{66,2},{3,67},{67,3},{4,68},{68... | collective-permute-start | bytes 786440 | tf_op jit(solution)/shard_map/ppermute | solution.py:467
  78.8 4.9 %copy-start.2 = (bf16[512,128]{1,0:T(8,128)(2,1)S(1)}, bf16[512,128]{1,0:T(8,128)(2,1)}, u32[]{:S(2)}) copy-start(bf16[512,128]{1,0:T(8,128)(2,1)} %copy-done.1) | copy-start | bytes 393220
  85.3 3.8 %collective-permute-start.3 = (f32[32,72,128]{2,1,0:T(8,128)S(1)}, f32[32,72,128]{2,1,0:T(8,128)S(1)}, u32[]{:S(2)}, u32[]{:S(2)}) collective-permute-start(f32[32,72,128]{2,1,0:T(8,128)S(1)} %grads.7), channel_id=1, source_target_pairs={{0,1},{1,0},{2,3},{3,2},{4,5},{5,4},{6,7},{7,6},{8,9},{9,8},{10,11... | collective-permute-start | bytes 3538952 | tf_op jit(solution)/shard_map/ppermute | solution.py:473
  114.3 4.3 %collective-permute-start.4 = (f32[8,72,128]{2,1,0:T(8,128)S(1)}, f32[8,72,128]{2,1,0:T(8,128)S(1)}, u32[]{:S(2)}, u32[]{:S(2)}) collective-permute-start(f32[8,72,128]{2,1,0:T(8,128)S(1)} %all_to_all.27.mine), channel_id=1, source_target_pairs={{0,1},{1,0},{2,3},{3,2},{4,5},{5,4},{6,7},{7,6},{8,9},{9,8},{10,11... | collective-permute-start | bytes 884744 | tf_op jit(solution)/shard_map/ppermute | solution.py:477

commit v7 on v6

--- a/solution.py
+++ b/solution.py
@@ -80,11 +80,10 @@
         tot[...] = jnp.zeros(tot.shape, f32)
 
     rows = keys // row_blocks
-    xt = jnp.transpose(cache[...])
     e_rows = []
     total = jnp.zeros((1, queries), f32)
     for block in range(row_blocks):
-        x = xt[block * rows : (block + 1) * rows]
+        x = jnp.transpose(cache[:, pl.ds(block * rows, rows)])
         acc = jnp.zeros((rows, queries), f32)
         for pair in range(heads // 2):
             s = dot(x, jnp.concatenate([q[pair * 2], q[pair * 2 + 1]], axis=1))

time: 120 us -> 120 us (level)
  no operation moved by 1% of the time
where the time goes in v7:
time: 120 us
  blocking collectives  40.9 us (34%)
  Pallas kernels  33.6 us (28%)
  starting transfers between devices  22 us (18%)
  waiting for transfers between devices  15.3 us (13%)
  local copies, waits for them, and re-layouts  6.86 us (6%)
    pallas_call x1, Pallas kernels, probs_call(): pl.pallas_call(probs_kernel, grid=(parts,), in_specs=[pl.BlockSpec((width...  18 us
    all_to_all x1, blocking collectives, spread(): lax.all_to_all(jnp.broadcast_to(x[None], (count,) + x.shape), axes, 0, 0,...  16.7 us
    all_to_all x1, blocking collectives, per_device(): lax.all_to_all(code_call(out_mine, got, parts // 2), ('x',) + ZY, 0, 0, t...  14.1 us
    all_to_all x1, waiting for transfers between devices, per_device(): rec = lax.all_to_all(coded, HEAD, 0, 0, tiled=True)  11.5 us
    all_to_all x1, blocking collectives, per_device(): mine = lax.all_to_all(sum_call(block, zy), ZY, 0, 0, tiled=True)  10.2 us
    pallas_call x4, Pallas kernels, grads_call(): pl.pallas_call(functools.partial(grads_kernel, scale, half_rows, len(qs),...  9.84 us
    all_to_all x1, starting transfers between devices, spread(): lax.all_to_all(jnp.broadcast_to(x[None], (count,) + x.shape), axes, 0, 0,...  8.29 us
    all_to_all x1, starting transfers between devices, per_device(): rec = lax.all_to_all(coded, HEAD, 0, 0, tiled=True)  3.96 us
  transfers between devices with their start and end apart: 7, of which 4 were waited for; matrix products, arithmetic and copies ran while one was open for 1% of the time, Pallas kernels for 25%

profile of v7, /device:TPU:1, one launch (start us, length us, event | category | flops | bytes accessed | tf_op | source)
XLA Modules:
  0.0 119.5 jit_solution(14119827450489699592)
XLA Ops:
  0.6 0.0 copy-start
  0.7 0.7 constant_dynamic-slice_fusion
  1.4 0.2 copy-done
  1.6 1.1 broadcast_in_dim.6
  2.8 0.0 copy-start.6
  2.8 8.3 %all-to-all-start = ((bf16[8,528,128]{2,1,0:T(8,128)(2,1)}), bf16[8,528,128]{2,1,0:T(8,128)(2,1)S(1)}, u32[]{:S(2)}, u32[]{:S(2)}) async-start(bf16[8,528,128]{2,1,0:T(8,128)(2,1)} %broadcast_in_dim.6), calls=%async_computation | async-start | bytes 2162688 | tf_op jit(solution)/shard_map/all_to_all | solution.py:408
  11.1 0.0 copy-done.6
  11.1 3.0 %collective-permute-start = (bf16[512,128]{1,0:T(8,128)(2,1)S(1)}, bf16[512,128]{1,0:T(8,128)(2,1)S(1)}, u32[]{:S(2)}, u32[]{:S(2)}) collective-permute-start(bf16[512,128]{1,0:T(8,128)(2,1)S(1)} %copy-done.6), channel_id=1, source_target_pairs={{0,64},{64,0},{1,65},{65,1},{2,66},{66,2},{3,67},{67,3},{4,68},{68... | collective-permute-start | bytes 393224 | tf_op jit(solution)/shard_map/ppermute | solution.py:451
  14.0 18.0 %probs.1 = (s16[8,528,128]{2,1,0:T(8,128)(2,1)}, f32[8,128]{1,0:T(8,128)}) custom-call(bf16[576,4096]{1,0:T(8,128)(2,1)} %bitcast.23, bf16[16,576,128]{2,1,0:T(8,128)(2,1)} %bitcast.24, f32[16,128]{1,0:T(8,128)} %nrm.1, s32[8,1,512]{2,1,0:T(1,128)} %bitcast.22, s32[1,128]{1,0:T(1,128)} %bitcast.18), custom_call_target="tpu_custom_call" | custom-call | flops 9663676416 | bytes 7077888 | tf_op jit(solution)/shard_map/probs/pallas_call | solution.py:106
  32.0 0.0 collective-permute-done.keys
  32.0 0.0 copy-start.1
  32.0 0.6 copy-done.1
  32.6 0.0 all-to-all-done.refs_1_
  32.6 1.5 %collective-permute-start.1 = (bf16[8,528,128]{2,1,0:T(8,128)(2,1)S(1)}, bf16[8,528,128]{2,1,0:T(8,128)(2,1)S(1)}, u32[]{:S(2)}, u32[]{:S(2)}) collective-permute-start(bf16[8,528,128]{2,1,0:T(8,128)(2,1)S(1)} %all-to-all-done.refs_1_), channel_id=1, source_target_pairs={{0,1},{1,0},{2,3},{3,2},{4,5},{5,4},{6,7},{7,6},{8,9},{9,8},{10,11... | collective-permute-start | bytes 3244040 | tf_op jit(solution)/shard_map/ppermute | solution.py:453
  34.2 4.0 %all-to-all-start.1 = ((s16[8,528,128]{2,1,0:T(8,128)(2,1)}), s16[8,528,128]{2,1,0:T(8,128)(2,1)S(1)}, u32[]{:S(2)}, u32[]{:S(2)}) async-start(s16[8,528,128]{2,1,0:T(8,128)(2,1)} %get-tuple-element.27), calls=%async_computation.1 | async-start | bytes 2162688 | tf_op jit(solution)/shard_map/all_to_all | solution.py:454
  38.1 0.8 dynamic_slice.11
  38.9 0.7 slice.11
  39.6 0.0 copy-start.7
  39.6 0.9 copy-done.7
  40.5 1.5 %logits.2.refs_2_ = f32[512,128]{1,0:T(8,128)S(1)} custom-call(bf16[512,128]{1,0:T(8,128)(2,1)S(1)} %copy-done.7, bf16[8,528,128]{2,1,0:T(8,128)(2,1)S(1)} %all-to-all-done.refs_1_), custom_call_target="tpu_custom_call" | custom-call | flops 1073741824 | bytes 1081344 | tf_op jit(solution)/shard_map/logits/pallas_call | solution.py:182
  42.0 0.0 collective-permute-done.1.refs_1_
  42.0 0.0 copy-done.5
  42.0 1.7 %logits.3 = (f32[512,128]{1,0:T(8,128)S(1)}, f32[8,128]{1,0:T(8,128)S(1)}) custom-call(bf16[512,128]{1,0:T(8,128)(2,1)S(1)} %copy-done.7, bf16[8,528,128]{2,1,0:T(8,128)(2,1)S(1)} %collective-permute-done.1.refs_1_, f32[512,128]{1,0:T(8,128)S(1)} %logits.2.refs_2_, s32[1,512]{1,0:T(1,128)S(1)} %bitcast.16, s32[1,128]{1,0:T(1,128)S(1)} %bitcast.19), custom_call_target="tpu_custom_call" | custom-call | flops 1073741824 | bytes 1081344 | tf_op jit(solution)/shard_map/logits/pallas_call | solution.py:182
  43.7 0.0 copy-start.3
  43.7 0.7 copy-done.3
  44.4 11.5 %all-to-all-done.1.rec = s16[8,528,128]{2,1,0:T(8,128)(2,1)S(1)} async-done(((s16[8,528,128]{2,1,0:T(8,128)(2,1)}), s16[8,528,128]{2,1,0:T(8,128)(2,1)S(1)}, u32[]{:S(2)}, u32[]{:S(2)}) %all-to-all-start.1) | async-done | bytes 1081376 | tf_op jit(solution)/shard_map/all_to_all | solution.py:454
  55.9 0.1 broadcast_in_dim.16
  56.0 16.7 %all_to_all.25.stats = f32[128,1,384]{2,1,0:T(1,128)S(1)} all-to-all(f32[128,1,384]{2,1,0:T(1,128)S(1)} %broadcast_in_dim.16), channel_id=1, replica_groups=mesh['zh'=2,'x'=4,'zl'=2,'y'=4,'core'=2] {'zh','x','zl','y','core'}, dimensions={0} | all-to-all | bytes 393216 | tf_op jit(solution)/shard_map/all_to_all | solution.py:408
  72.7 0.9 copy-done.4
  73.7 0.7 logit_grad.1.lg_ref
  74.4 0.9 collective-permute-start.2
  75.3 0.0 copy-done.8
  75.3 3.4 %grads.4 = (f32[32,72,128]{2,1,0:T(8,128)S(1)}, f32[32,72,128]{2,1,0:T(8,128)S(1)}, f32[512,128]{1,0:T(8,128)S(1)}) custom-call(s32[1]{0:T(128)} %bitcast.7.which, bf16[512,128]{1,0:T(8,128)(2,1)S(1)} %copy-done.8, f32[512,128]{1,0:T(8,128)S(1)} %logit_grad.1.lg_ref, bf16[2,4,528,128]{3,2,1,0:T(8,128)(2,1)S(1)} %bitcast.13, bf16[2,4,528,128]{3,2,1,0:T(8,128)(2,1)S(1)} %bitcast.10), custom_call_target="tpu_custom_call" | custom-call | flops 1610612736 | bytes 3244032 | tf_op jit(solution)/shard_map/grads/pallas_call | solution.py:298
  78.7 0.0 copy-start.2
  78.7 3.2 %grads.5 = f32[512,128]{1,0:T(8,128)} custom-call(s32[1]{0:T(128)S(6)} %sub.3.which, bf16[512,128]{1,0:T(8,128)(2,1)S(1)} %copy-done.8, f32[512,128]{1,0:T(8,128)S(1)} %logit_grad.1.lg_ref, bf16[2,4,528,128]{3,2,1,0:T(8,128)(2,1)S(1)} %bitcast.14, bf16[2,4,528,128]{3,2,1,0:T(8,128)(2,1)S(1)} %bitcast.11, f32[512,128]{1,0:T(8,128)S(1)} %get-tuple-element.36.refs_2_), custom_call_target="tpu_custom_call" | custom-call | flops 1610612736 | bytes 3244032 | tf_op jit(solution)/shard_map/grads/pallas_call | solution.py:298
  81.9 1.8 %collective-permute-done.2.lg_ref = f32[512,128]{1,0:T(8,128)S(1)} collective-permute-done((f32[512,128]{1,0:T(8,128)S(1)}, f32[512,128]{1,0:T(8,128)S(1)}, u32[]{:S(2)}, u32[]{:S(2)}) %collective-permute-start.2) | collective-permute-done | bytes 262176 | tf_op jit(solution)/shard_map/ppermute | solution.py:466
  83.6 0.0 copy-done.2
  83.6 1.6 %grads.7 = f32[32,72,128]{2,1,0:T(8,128)S(1)} custom-call(s32[1]{0:T(128)} %bitcast.7.which, bf16[512,128]{1,0:T(8,128)(2,1)S(1)} %copy-done.2, f32[512,128]{1,0:T(8,128)S(1)} %collective-permute-done.2.lg_ref, bf16[2,4,528,128]{3,2,1,0:T(8,128)(2,1)S(1)} %bitcast.15, f32[32,72,128]{2,1,0:T(8,128)S(1)} %get-tuple-element.39.refs_1_), custom_call_target="tpu_custom_call" | custom-call | flops 805306368 | bytes 1622016 | tf_op jit(solution)/shard_map/grads/pallas_call | solution.py:298
  85.3 1.3 %collective-permute-start.3 = (f32[32,72,128]{2,1,0:T(8,128)S(1)}, f32[32,72,128]{2,1,0:T(8,128)S(1)}, u32[]{:S(2)}, u32[]{:S(2)}) collective-permute-start(f32[32,72,128]{2,1,0:T(8,128)S(1)} %grads.7), channel_id=1, source_target_pairs={{0,1},{1,0},{2,3},{3,2},{4,5},{5,4},{6,7},{7,6},{8,9},{9,8},{10,11... | collective-permute-start | bytes 3538952 | tf_op jit(solution)/shard_map/ppermute | solution.py:472
  86.6 1.6 %grads.6.a = f32[32,72,128]{2,1,0:T(8,128)S(1)} custom-call(s32[1]{0:T(128)} %bitcast.7.which, bf16[512,128]{1,0:T(8,128)(2,1)S(1)} %copy-done.2, f32[512,128]{1,0:T(8,128)S(1)} %collective-permute-done.2.lg_ref, bf16[2,4,528,128]{3,2,1,0:T(8,128)(2,1)S(1)} %bitcast.12, f32[32,72,128]{2,1,0:T(8,128)S(1)} %get-tuple-element.38.refs_1_), custom_call_target="tpu_custom_call" | custom-call | flops 805306368 | bytes 1622016 | tf_op jit(solution)/shard_map/grads/pallas_call | solution.py:298
  88.2 0.8 collective-permute-done.3.b
  89.1 0.7 code_parts.1
  89.8 14.1 %all_to_all.26.rec = s16[32,80,128]{2,1,0:T(8,128)(2,1)S(1)} all-to-all(s16[32,80,128]{2,1,0:T(8,128)(2,1)S(1)} %code_parts.1), channel_id=1, replica_groups=mesh['zh'=2,'x'=4,'zl'=2,'y'=4,'core'=2] {'x','zl','y'}, dimensions={0} | all-to-all | bytes 1310720 | tf_op jit(solution)/shard_map/all_to_all | solution.py:474
  103.8 0.3 sum_parts.1
  104.1 10.2 %all_to_all.27.mine = f32[8,72,128]{2,1,0:T(8,128)S(1)} all-to-all(f32[8,72,128]{2,1,0:T(8,128)S(1)} %sum_parts.1), channel_id=1, replica_groups=mesh['zh'=2,'x'=4,'zl'=2,'y'=4,'core'=2] {'zl','y'}, dimensions={0} | all-to-all | bytes 589824 | tf_op jit(solution)/shard_map/all_to_all | solution.py:475
  114.3 3.1 %collective-permute-start.4 = (f32[8,72,128]{2,1,0:T(8,128)S(1)}, f32[8,72,128]{2,1,0:T(8,128)S(1)}, u32[]{:S(2)}, u32[]{:S(2)}) collective-permute-start(f32[8,72,128]{2,1,0:T(8,128)S(1)} %all_to_all.27.mine), channel_id=1, source_target_pairs={{0,1},{1,0},{2,3},{3,2},{4,5},{5,4},{6,7},{7,6},{8,9},{9,8},{10,11... | collective-permute-start | bytes 884744 | tf_op jit(solution)/shard_map/ppermute | solution.py:476
  117.3 1.2 %collective-permute-done.4.other = f32[8,72,128]{2,1,0:T(8,128)S(1)} collective-permute-done((f32[8,72,128]{2,1,0:T(8,128)S(1)}, f32[8,72,128]{2,1,0:T(8,128)S(1)}, u32[]{:S(2)}, u32[]{:S(2)}) %collective-permute-start.4) | collective-permute-done | bytes 294944 | tf_op jit(solution)/shard_map/ppermute | solution.py:476
  118.5 1.0 place.1
  (8 shorter events, 0.1 us)
Async XLA Ops:
  0.6 1.0 copy-start
  2.8 8.3 %copy-start.6 = (bf16[512,128]{1,0:T(8,128)(2,1)S(1)}, bf16[512,128]{1,0:T(8,128)(2,1)}, u32[]{:S(2)}) copy-start(bf16[512,128]{1,0:T(8,128)(2,1)} %keys.3) | copy-start | bytes 393220
  2.8 29.9 %all-to-all-start = ((bf16[8,528,128]{2,1,0:T(8,128)(2,1)}), bf16[8,528,128]{2,1,0:T(8,128)(2,1)S(1)}, u32[]{:S(2)}, u32[]{:S(2)}) async-start(bf16[8,528,128]{2,1,0:T(8,128)(2,1)} %broadcast_in_dim.6), calls=%async_computation | async-start | bytes 2162688 | tf_op jit(solution)/shard_map/all_to_all | solution.py:408
  11.1 20.9 %collective-permute-start = (bf16[512,128]{1,0:T(8,128)(2,1)S(1)}, bf16[512,128]{1,0:T(8,128)(2,1)S(1)}, u32[]{:S(2)}, u32[]{:S(2)}) collective-permute-start(bf16[512,128]{1,0:T(8,128)(2,1)S(1)} %copy-done.6), channel_id=1, source_target_pairs={{0,64},{64,0},{1,65},{65,1},{2,66},{66,2},{3,67},{67,3},{4,68},{68... | collective-permute-start | bytes 393224 | tf_op jit(solution)/shard_map/ppermute | solution.py:451
  32.0 0.7 copy-start.1
  32.6 9.3 %collective-permute-start.1 = (bf16[8,528,128]{2,1,0:T(8,128)(2,1)S(1)}, bf16[8,528,128]{2,1,0:T(8,128)(2,1)S(1)}, u32[]{:S(2)}, u32[]{:S(2)}) collective-permute-start(bf16[8,528,128]{2,1,0:T(8,128)(2,1)S(1)} %all-to-all-done.refs_1_), channel_id=1, source_target_pairs={{0,1},{1,0},{2,3},{3,2},{4,5},{5,4},{6,7},{7,6},{8,9},{9,8},{10,11... | collective-permute-start | bytes 3244040 | tf_op jit(solution)/shard_map/ppermute | solution.py:453
  34.2 21.7 %all-to-all-start.1 = ((s16[8,528,128]{2,1,0:T(8,128)(2,1)}), s16[8,528,128]{2,1,0:T(8,128)(2,1)S(1)}, u32[]{:S(2)}, u32[]{:S(2)}) async-start(s16[8,528,128]{2,1,0:T(8,128)(2,1)} %get-tuple-element.27), calls=%async_computation.1 | async-start | bytes 2162688 | tf_op jit(solution)/shard_map/all_to_all | solution.py:454
  39.6 0.9 copy-start.7
  40.5 1.5 %copy-start.5 = (s32[128]{0:T(128)S(1)}, s32[128]{0:T(128)}, u32[]{:S(2)}) copy-start(s32[128]{0:T(128)} %param.11) | copy-start | bytes 1540
  43.7 0.7 copy-start.3
  55.9 19.4 %copy-start.8 = (bf16[512,128]{1,0:T(8,128)(2,1)S(1)}, bf16[512,128]{1,0:T(8,128)(2,1)}, u32[]{:S(2)}) copy-start(bf16[512,128]{1,0:T(8,128)(2,1)} %keys.3) | copy-start | bytes 393220
  72.7 1.0 copy-start.4
  74.4 9.3 %collective-permute-start.2 = (f32[512,128]{1,0:T(8,128)S(1)}, f32[512,128]{1,0:T(8,128)S(1)}, u32[]{:S(2)}, u32[]{:S(2)}) collective-permute-start(f32[512,128]{1,0:T(8,128)S(1)} %logit_grad.1.lg_ref), channel_id=1, source_target_pairs={{0,64},{64,0},{1,65},{65,1},{2,66},{66,2},{3,67},{67,3},{4,68},{68... | collective-permute-start | bytes 786440 | tf_op jit(solution)/shard_map/ppermute | solution.py:466
  78.7 4.9 %copy-start.2 = (bf16[512,128]{1,0:T(8,128)(2,1)S(1)}, bf16[512,128]{1,0:T(8,128)(2,1)}, u32[]{:S(2)}) copy-start(bf16[512,128]{1,0:T(8,128)(2,1)} %copy-done.1) | copy-start | bytes 393220
  85.3 3.8 %collective-permute-start.3 = (f32[32,72,128]{2,1,0:T(8,128)S(1)}, f32[32,72,128]{2,1,0:T(8,128)S(1)}, u32[]{:S(2)}, u32[]{:S(2)}) collective-permute-start(f32[32,72,128]{2,1,0:T(8,128)S(1)} %grads.7), channel_id=1, source_target_pairs={{0,1},{1,0},{2,3},{3,2},{4,5},{5,4},{6,7},{7,6},{8,9},{9,8},{10,11... | collective-permute-start | bytes 3538952 | tf_op jit(solution)/shard_map/ppermute | solution.py:472
  114.3 4.3 %collective-permute-start.4 = (f32[8,72,128]{2,1,0:T(8,128)S(1)}, f32[8,72,128]{2,1,0:T(8,128)S(1)}, u32[]{:S(2)}, u32[]{:S(2)}) collective-permute-start(f32[8,72,128]{2,1,0:T(8,128)S(1)} %all_to_all.27.mine), channel_id=1, source_target_pairs={{0,1},{1,0},{2,3},{3,2},{4,5},{5,4},{6,7},{7,6},{8,9},{9,8},{10,11... | collective-permute-start | bytes 884744 | tf_op jit(solution)/shard_map/ppermute | solution.py:476
